TPU v7x, 32 devices: a whole 2x2x4 slice. The times are simulated.
32 devices in a mesh: rows: 8 (over z, y), tp: 4 (over x, core).
Axes of the slice: x: 2, y: 2, z: 4, core: 2. Of those that a mesh axis runs over, the one named last changes fastest.
Arguments:
- datapoints: bfloat16 [16384, 1024], P('rows', 'tp'), may hold values from -6 to 6
- lengths: int32 [8, 3], P('rows'), may hold values from 1 to 1024, 2048 in all within a row
- qkv_weight: bfloat16 [3, 1024, 1024], P(None, None, 'tp'), may hold values from -0.1875 to 0.1875
- out_weight: bfloat16 [1024, 1024], P('tp'), may hold values from -3 to 3
- up_weight: bfloat16 [1024, 4096], P(None, 'tp'), may hold values from -0.1875 to 0.1875
- up_bias: float32 [4096], P('tp'), may hold values from -3 to 3
- down_weight: bfloat16 [4096, 1024], P('tp'), may hold values from -0.09375 to 0.09375
- down_bias: float32 [1024], P('tp'), may hold values from -3 to 3
- gain_one: float32 [1024], P('tp'), may hold values from 0.5 to 1.5
- shift_one: float32 [1024], P('tp'), may hold values from -2 to 2
- gain_two: float32 [1024], P('tp'), may hold values from 0.5 to 1.5
- shift_two: float32 [1024], P('tp'), may hold values from -2 to 2
- grad_out: bfloat16 [16384, 1024], P('rows', 'tp'), may hold values from -6 to 6
Outputs:
- output: bfloat16 [16384, 1024], P('rows', 'tp')
- d_input: float32 [16384, 1024], P('rows', 'tp')
- d_qkv: float32 [3, 1024, 1024], P(None, None, 'tp')
- d_out: float32 [1024, 1024], P('tp')
- d_up: float32 [1024, 4096], P(None, 'tp')
- d_up_bias: float32 [4096], P('tp')
- d_down: float32 [4096, 1024], P('tp')
- d_down_bias: float32 [1024], P('tp')
- d_gain_one: float32 [1024], P('tp')
- d_shift_one: float32 [1024], P('tp')
- d_gain_two: float32 [1024], P('tp')
- d_shift_two: float32 [1024], P('tp')
Inputs may be any that keep to these rules, and one draw needn't show every extreme that they name: Each row lists 3 dataset lengths that sum to 2048; the largest in each row is 1024.
All inputs are finite; a program needn't handle non-finite values.
Results may differ from a plain program's by a relative error of at most 0.029.
Values may be sent and summed in bfloat16 or wider, within the bound.
No kernel may reach another device: no remote copies, remote signals or barrier semaphores. Data moves between devices by JAX's collectives and lax.ppermute only.
A program may use at most 192 MiB of HBM per device.

v0:
```python
import jax
import jax.numpy as jnp
from jax import lax
from jax.sharding import PartitionSpec as P

D = 1024
DH = 128
BLK = 512


EPS_NORM = 1e-05
NEG_FILL = -1e30


def dataset_ids(lengths, count):
    ends = jnp.cumsum(lengths.reshape(-1))
    place = lax.broadcasted_iota(jnp.int32, (count, 1), 0)
    return jnp.sum((place >= ends[None, :]).astype(jnp.int32), axis=1)


def column_total(partial_value):
    return lax.psum_scatter(
        partial_value.astype(jnp.bfloat16), "tp", scatter_dimension=1, tiled=True
    ).astype(jnp.float32)


def row_totals(first, second):
    return lax.psum((first, second), "tp")


def masked_scores(q_block, key_rows, s_block, dataset_of):
    scores = jnp.einsum("qhd,khd->hqk", q_block, key_rows, preferred_element_type=jnp.float32)
    allowed = (s_block[:, None] == dataset_of[None, :])[None]
    return jnp.where(allowed, scores, NEG_FILL)


def attend(queries, key_rows, value_rows, dataset_of):
    tok_rows, n_heads, head_size = queries.shape
    n_blocks = tok_rows // BLK

    def attend_one(block_item):
        q_block, s_block = block_item
        scores = masked_scores(q_block, key_rows, s_block, dataset_of)
        row_max = jnp.max(scores, axis=-1, keepdims=True)
        weights = jnp.exp(scores - row_max)
        row_total = jnp.sum(weights, axis=-1, keepdims=True)
        softmaxed = weights / row_total
        block_mix = jnp.einsum(
            "hqk,khd->qhd",
            softmaxed.astype(jnp.bfloat16),
            value_rows,
            preferred_element_type=jnp.float32,
        )
        outputs = (block_mix.astype(jnp.bfloat16), row_max, row_total)
        return outputs

    return lax.map(
        attend_one,
        (queries.reshape(n_blocks, BLK, n_heads, head_size), dataset_of.reshape(n_blocks, BLK)),
    )


def attend_back(queries, key_rows, value_rows, dataset_of, d_mixed, kept_stats):
    tok_rows, n_heads, head_size = queries.shape
    n_blocks = tok_rows // BLK

    def back_step(acc_pair, block_item):
        d_keys, d_values = acc_pair
        q_block, s_block, g_block, stats_blk = block_item
        scores = masked_scores(q_block, key_rows, s_block, dataset_of)
        softmaxed = jnp.exp(scores - stats_blk[0]) / stats_blk[1]
        d_values = d_values + jnp.einsum(
            "hqk,qhd->khd",
            softmaxed.astype(jnp.bfloat16),
            g_block,
            preferred_element_type=jnp.float32,
        )
        d_probs = jnp.einsum(
            "qhd,khd->hqk", g_block, value_rows, preferred_element_type=jnp.float32
        )
        d_scores = (
            softmaxed * (d_probs - jnp.sum(softmaxed * d_probs, axis=-1, keepdims=True))
        ).astype(jnp.bfloat16)
        d_query = jnp.einsum(
            "hqk,khd->qhd", d_scores, key_rows, preferred_element_type=jnp.float32
        ).astype(jnp.bfloat16)
        d_keys = d_keys + jnp.einsum(
            "hqk,qhd->khd", d_scores, q_block, preferred_element_type=jnp.float32
        )
        return ((d_keys, d_values), d_query)

    zeros_f = jnp.zeros(key_rows.shape, jnp.float32)
    items = (
        queries.reshape(n_blocks, BLK, n_heads, head_size),
        dataset_of.reshape(n_blocks, BLK),
        d_mixed.reshape(n_blocks, BLK, n_heads, head_size),
        kept_stats,
    )
    (d_keys, d_values), d_query = lax.scan(back_step, (zeros_f, zeros_f), items)
    col_width = n_heads * head_size
    return (
        d_query.reshape(tok_rows, col_width),
        d_keys.astype(jnp.bfloat16).reshape(tok_rows, col_width),
        d_values.astype(jnp.bfloat16).reshape(tok_rows, col_width),
    )


def local(
    datapoints,
    lengths,
    qkv_weight,
    out_weight,
    up_weight,
    up_bias,
    down_weight,
    down_bias,
    gain_one,
    shift_one,
    gain_two,
    shift_two,
    grad_out,
):
    tok_rows, col_width = datapoints.shape
    n_heads = col_width // DH
    col_start = lax.axis_index("tp") * col_width
    q_scale = DH ** (-0.5)
    dataset_of = dataset_ids(lengths, tok_rows)
    full_rows, gain_full, shift_full = (
        lax.all_gather(datapoints, "tp", axis=1, tiled=True),
        lax.all_gather(gain_one.astype(jnp.bfloat16), "tp", axis=0, tiled=True).astype(
            gain_one.dtype
        ),
        lax.all_gather(shift_one.astype(jnp.bfloat16), "tp", axis=0, tiled=True).astype(
            shift_one.dtype
        ),
    )
    full_rows = full_rows.astype(jnp.float32)
    mean_one = jnp.mean(full_rows, axis=-1, keepdims=True)
    centered = full_rows - mean_one
    rstd_one = lax.rsqrt(jnp.mean(centered * centered, axis=-1, keepdims=True) + EPS_NORM)
    normed_one = centered * rstd_one
    normed_acts = (normed_one * gain_full + shift_full).astype(jnp.bfloat16)
    projected = jnp.einsum(
        "td,sdc->stc", normed_acts, qkv_weight, preferred_element_type=jnp.float32
    )
    queries = (projected[0] * q_scale).astype(jnp.bfloat16).reshape(tok_rows, n_heads, DH)
    key_rows = projected[1].astype(jnp.bfloat16).reshape(tok_rows, n_heads, DH)
    value_rows = projected[2].astype(jnp.bfloat16).reshape(tok_rows, n_heads, DH)
    kept_state = attend(queries, key_rows, value_rows, dataset_of)
    attn_mixed = kept_state[0].reshape(tok_rows, col_width)
    attn_part = jnp.dot(attn_mixed, out_weight, preferred_element_type=jnp.float32)
    residual = datapoints.astype(jnp.float32) + column_total(attn_part)
    row_sum, squares = row_totals(jnp.sum(residual, axis=-1), jnp.sum(residual * residual, axis=-1))
    mean_two = (row_sum / D)[:, None]
    rstd_two = lax.rsqrt(squares[:, None] / D - mean_two * mean_two + EPS_NORM)
    normed_two = (residual - mean_two) * rstd_two
    mlp_input = (normed_two * gain_two + shift_two).astype(jnp.bfloat16)
    mlp_full = lax.all_gather(mlp_input, "tp", axis=1, tiled=True)
    pre_act = jnp.dot(mlp_full, up_weight, preferred_element_type=jnp.float32) + up_bias
    active, gelu_back = jax.vjp(jax.nn.gelu, pre_act)
    hidden = active.astype(jnp.bfloat16)
    out_part = jnp.dot(hidden, down_weight, preferred_element_type=jnp.float32)
    output = (residual + column_total(out_part) + down_bias).astype(jnp.bfloat16)
    grad_local = grad_out.astype(jnp.float32)
    grad_full = lax.all_gather(grad_out, "tp", axis=1, tiled=True)
    d_down_bias = jnp.sum(grad_local, axis=0)
    d_down = jnp.einsum("tf,td->fd", hidden, grad_full, preferred_element_type=jnp.float32)
    d_hidden = jnp.einsum("td,fd->tf", grad_full, down_weight, preferred_element_type=jnp.float32)
    d_pre = gelu_back(d_hidden)[0].astype(jnp.bfloat16)
    d_up_bias = jnp.sum(d_pre.astype(jnp.float32), axis=0)
    d_up = jnp.einsum("td,tf->df", mlp_full, d_pre, preferred_element_type=jnp.float32)
    d_inner = column_total(
        jnp.einsum("tf,df->td", d_pre, up_weight, preferred_element_type=jnp.float32)
    )
    d_gain_two = jnp.sum(d_inner * normed_two, axis=0)
    d_shift_two = jnp.sum(d_inner, axis=0)
    scaled_two = d_inner * gain_two
    moment_a, moment_b = row_totals(
        jnp.sum(scaled_two, axis=-1), jnp.sum(scaled_two * normed_two, axis=-1)
    )
    d_resid = grad_local + rstd_two * (
        scaled_two - moment_a[:, None] / D - normed_two * moment_b[:, None] / D
    )
    d_branch = d_resid.astype(jnp.bfloat16)
    d_branch_full = lax.all_gather(d_branch, "tp", axis=1, tiled=True)
    d_out = jnp.einsum("tc,td->cd", attn_mixed, d_branch_full, preferred_element_type=jnp.float32)
    d_mixed = jnp.einsum(
        "td,cd->tc", d_branch_full, out_weight, preferred_element_type=jnp.float32
    ).astype(jnp.bfloat16)
    d_query, d_keys, d_values = attend_back(
        queries,
        key_rows,
        value_rows,
        dataset_of,
        d_mixed.reshape(tok_rows, n_heads, DH),
        kept_state[1:],
    )
    stacked = jnp.stack([d_query, d_keys, d_values])
    factors = jnp.array([q_scale, 1.0, 1.0], jnp.float32)
    d_qkv = (
        jnp.einsum("td,stc->sdc", normed_acts, stacked, preferred_element_type=jnp.float32)
        * factors[:, None, None]
    )
    d_acts = q_scale * jnp.einsum(
        "tc,dc->td", d_query, qkv_weight[0], preferred_element_type=jnp.float32
    )
    d_acts = d_acts + jnp.einsum(
        "tc,dc->td", d_keys, qkv_weight[1], preferred_element_type=jnp.float32
    )
    d_acts = d_acts + jnp.einsum(
        "tc,dc->td", d_values, qkv_weight[2], preferred_element_type=jnp.float32
    )
    d_norm = column_total(d_acts)
    normed_mine = lax.dynamic_slice_in_dim(normed_one, col_start, col_width, 1)
    d_gain_one = jnp.sum(d_norm * normed_mine, axis=0)
    d_shift_one = jnp.sum(d_norm, axis=0)
    scaled_one = d_norm * gain_one
    moment_c, moment_d = row_totals(
        jnp.sum(scaled_one, axis=-1), jnp.sum(scaled_one * normed_mine, axis=-1)
    )
    d_input = d_resid + rstd_one * (
        scaled_one - moment_c[:, None] / D - normed_mine * moment_d[:, None] / D
    )
    (
        d_qkv,
        d_out,
        d_gain_one,
        d_shift_one,
        d_up,
        d_up_bias,
        d_down,
        d_down_bias,
        d_gain_two,
        d_shift_two,
    ) = lax.psum(
        (
            d_qkv,
            d_out,
            d_gain_one,
            d_shift_one,
            d_up,
            d_up_bias,
            d_down,
            d_down_bias,
            d_gain_two,
            d_shift_two,
        ),
        "rows",
    )
    return (
        output,
        d_input,
        d_qkv,
        d_out,
        d_up,
        d_up_bias,
        d_down,
        d_down_bias,
        d_gain_one,
        d_shift_one,
        d_gain_two,
        d_shift_two,
    )


def solution(mesh):
    placed = (
        P("rows", "tp"),
        P("rows", None),
        P(None, None, "tp"),
        P("tp", None),
        P(None, "tp"),
        P("tp"),
        P("tp", None),
        P("tp"),
        P("tp"),
        P("tp"),
        P("tp"),
        P("tp"),
        P("rows", "tp"),
    )
    return jax.shard_map(
        local,
        mesh=mesh,
        in_specs=placed,
        out_specs=(
            P("rows", "tp"),
            P("rows", "tp"),
            P(None, None, "tp"),
            P("tp", None),
            P(None, "tp"),
            P("tp"),
            P("tp", None),
            P("tp"),
            P("tp"),
            P("tp"),
            P("tp"),
            P("tp"),
        ),
        check_vma=False,
    )
```

profile of v0, /device:TPU:0, one launch (start us, length us, event | category | flops | bytes accessed | tf_op | source)
XLA Modules:
  0.0 1025.4 jit_solution(16918290814643451072)
XLA Ops:
  21.7 25.7 %all-gather.7.cloned.1.call-done = bf16[2048,1024]{1,0:T(8,128)(2,1)} async-done(((bf16[2048,256]{1,0:T(8,128)(2,1)}), bf16[2048,1024]{1,0:T(8,128)(2,1)}) %all-gather.7.cloned.1.call-update) | async-done | bytes 4194320 | tf_op jit(solution)/shard_map/all_gather | solution.py:129
  70.6 41.9 %while.29 = (s32[]{:T(128)}, bf16[4,512,2,128]{3,2,1,0:T(2,128)(2,1)}, f32[4,2,512,1]{2,1,3,0:T(2,128)S(1)}, f32[4,2,512,1]{2,1,3,0:T(2,128)S(1)}, s32[4,512]{1,...) while((s32[]{:T(128)}, ...), condition=%wide.region_7.8_spmd, body=%wide.region_4.7_spmd.sunk | while | flops 1093793792 | bytes 32557180 | solution.py:57
  118.4 44.4 %reduce-scatter.5.cloned.1.call-done = bf16[2048,256]{1,0:T(8,128)(2,1)} async-done(((bf16[2048,1024]{1,0:T(8,128)(2,1)}), bf16[2048,256]{1,0:T(8,128)(2,1)}) %reduce-scatter.5.cloned.1.call-update) | async-done | bytes 1048592 | tf_op jit(solution)/shard_map/reduce_scatter | solution.py:22
  164.7 10.1 all-reduce.4
  178.1 35.6 %all-gather.9.cloned.1.call-done = bf16[2048,1024]{1,0:T(8,128)(2,1)} async-done(((bf16[2048,256]{1,0:T(8,128)(2,1)}), bf16[2048,1024]{1,0:T(8,128)(2,1)}) %all-gather.9.cloned.1.call-update) | async-done | bytes 4194320 | tf_op jit(solution)/shard_map/all_gather | solution.py:158
  213.6 11.1 %fusion.88 = f32[2048,1024]{1,0:T(8,128)} fusion(bf16[2048,1024]{1,0:T(8,128)(2,1)} %all-gather.9.cloned.1.call-done, bf16[1024,1024]{1,0:T(8,128)(2,1)} %param.22), kind=kOutput, calls=%fused_computation.132 | convolution fusion | flops 4294967296 | bytes 14680064 | tf_op jit(solution)/shard_map/dot_general | solution.py:159
  224.7 25.4 %all-gather.11.cloned.1.call-done = bf16[2048,1024]{1,0:T(8,128)(2,1)} async-done(((bf16[2048,256]{1,0:T(8,128)(2,1)}), bf16[2048,1024]{1,0:T(8,128)(2,1)}) %all-gather.11.cloned.1.call-update) | async-done | bytes 4194320 | tf_op jit(solution)/shard_map/all_gather | solution.py:165
  250.2 13.4 %convert_reduce_fusion.1 = (f32[1024]{0:T(1024)}, bf16[2048,1024]{1,0:T(8,128)(2,1)S(1)}) fusion(f32[2048,1024]{1,0:T(8,128)} %fusion.88, f32[1024]{0:T(1024)S(1)} %copy-done.49, bf16[2048,1024]{1,0:T(8,128)(2,1)} %all-gather.11.cloned.1.call-done, bf16[1024,1024]{1,0:T(8,128)(2,1)S(1)} %copy-done), kind=kOutput, calls=%fused_computation.56 | convolution fusion | flops 4343200768 | bytes 18882560 | tf_op jit(solution)/shard_map/td,fd->tf/dot_general | solution.py:168
  271.8 44.6 %reduce-scatter.9.cloned.1.call-done = bf16[2048,256]{1,0:T(8,128)(2,1)} async-done(((bf16[2048,1024]{1,0:T(8,128)(2,1)}), bf16[2048,256]{1,0:T(8,128)(2,1)}) %reduce-scatter.9.cloned.1.call-update) | async-done | bytes 1048592 | tf_op jit(solution)/shard_map/reduce_scatter | solution.py:22
  319.7 10.6 %all-reduce.3 = (f32[2048]{0:T(1024)S(1)}, f32[2048]{0:T(1024)S(1)}) all-reduce(f32[2048]{0:T(1024)S(1)} %get-tuple-element.305, f32[2048]{0:T(1024)S(1)} %get-tuple-element.308), channel_id=1, replica_groups=mesh['rows'=8,'tp'=4] {'tp'}, use_global_device_ids=true, to_apply=%region_18.19 | all-reduce | flops 4096 | bytes 32768 | tf_op jit(solution)/shard_map/psum | solution.py:28
  335.3 36.2 %all-gather.13.cloned.1.call-done = bf16[2048,1024]{1,0:T(8,128)(2,1)} async-done(((bf16[2048,256]{1,0:T(8,128)(2,1)}), bf16[2048,1024]{1,0:T(8,128)(2,1)}) %all-gather.13.cloned.1.call-update) | async-done | bytes 4194320 | tf_op jit(solution)/shard_map/all_gather | solution.py:185
  376.2 121.9 %while.30 = (s32[]{:T(128)}, f32[2048,2,128]{0,2,1:T(8,128)}, f32[2048,2,128]{0,2,1:T(8,128)}, bf16[4,512,2,128]{3,1,2,0:T(8,128)(2,1)}, bf16[4,512,2,128]{3,1,2...) while((s32[]{:T(128)}, f32[2048,2,128]{0,2,1:T(8,128)}, ...), condition=%wide.region_21.22_spmd.clone, body=%wide.region_19.21_spmd.clone.sunk | while | flops 2706504704 | bytes 170703264 | solution.py:99
  387.2 8.7 multiply_convert_fusion.5
  411.1 6.6 multiply_reduce_fusion.3
  417.7 8.7 multiply_convert_fusion.5
  448.1 8.7 multiply_convert_fusion.5
  478.5 8.7 multiply_convert_fusion.5
  508.4 11.2 %convolution_convert_fusion.3 = bf16[2048,1024]{1,0:T(8,128)(2,1)} fusion(bf16[1024,1024]{1,0:T(8,128)(2,1)S(1)} %copy-done, f32[2048,1024]{1,0:T(8,128)} %fusion.88, f32[1024]{0:T(1024)S(1)} %copy-done.50), kind=kOutput, calls=%fused_computation.64 | convolution fusion | flops 4318035968 | bytes 14684160 | tf_op jit(solution)/shard_map/dot_general | solution.py:162
  519.9 10.1 fusion.89
  530.1 11.4 %fusion.82 = f32[1024,1024]{1,0:T(8,128)} fusion(bf16[2048,1024]{1,0:T(8,128)(2,1)S(1)} %copy-done.47, f32[2048,1024]{1,0:T(8,128)} %fusion.88, f32[1024]{0:T(1024)S(1)} %copy-done.50), kind=kOutput, calls=%fused_computation.129 | convolution fusion | flops 4315938816 | bytes 16781312 | tf_op jit(solution)/shard_map/tf,td->fd/dot_general | solution.py:167
  566.8 10.2 all-reduce.2
  577.0 23.2 %reduce-scatter.7.cloned.1.call-done = bf16[2048,256]{1,0:T(8,128)(2,1)} async-done(((bf16[2048,1024]{1,0:T(8,128)(2,1)}), bf16[2048,256]{1,0:T(8,128)(2,1)}) %reduce-scatter.7.cloned.1.call-update) | async-done | bytes 1048592 | tf_op jit(solution)/shard_map/reduce_scatter | solution.py:22
  606.6 23.7 %all-reduce = (f32[1024]{0:T(1024)}, f32[256]{0:T(256)}, f32[256]{0:T(256)}, f32[256]{0:T(256)}, f32[256]{0:T(256)}, /*index=5*/f32[256]{0:T(256)}) all-reduce(f32[1024]{0:T(1024)S(1)} %copy-done.44, f32[256]{0:T(256)S(1)} %get-tuple-element.384, f32[256]{0:T(256)S(1)} %get-tuple-element.302, ...), channel_id=1, replica_groups=mesh['rows'=8,'tp'=4] {'rows'}, use_global_device_ids=true, to_apply=%region_31.32 | all-reduce | flops 2304 | bytes 18432 | tf_op jit(solution)/shard_map/psum | solution.py:235
  630.3 376.5 %all-reduce.7.cloned.1.call-done = (f32[3,1024,256]{1,2,0:T(8,128)}, f32[256,1024]{1,0:T(8,128)}, f32[1024,1024]{1,0:T(8,128)}, f32[1024,1024]{1,0:T(8,128)}) async-done(((f32[3,1024,256]{1,2,0:T(8,128)}, f32[256,1024]{1,0:T(8,128)}, f32[1024,1024]{1,0:T(8,128)}, f32[1024,1024]{1,0:T(8,128)}), (f32[3,1024,256]{1,2,0:T(8,128)}, f32[256,1024]{1,0:T(8,128)}, f32[1024,1024]{1,0:T(8,128)}, ...) | async-done | bytes 12582928 | tf_op jit(solution)/shard_map/psum | solution.py:235
  (292 shorter events, 244.9 us)
Async XLA Ops:
  7.2 243.0 %copy-start = (bf16[1024,1024]{1,0:T(8,128)(2,1)S(1)}, bf16[1024,1024]{1,0:T(8,128)(2,1)}, u32[]{:S(2)}) copy-start(bf16[1024,1024]{1,0:T(8,128)(2,1)} %param.24) | copy-start | bytes 6291460
  7.2 40.1 %all-gather.7.cloned.1.call-start = ((), (), s32[]{:S(2)}) async-start(), calls=%async_computation.4 | async-start | bytes 5242880 | tf_op jit(solution)/shard_map/all_gather | solution.py:129
  7.9 154.9 %reduce-scatter.5.cloned.1.call-start = ((), (), s32[]{:S(2)}) async-start(), calls=%async_computation.5 | async-start | bytes 5242880 | tf_op jit(solution)/shard_map/reduce_scatter | solution.py:22
  118.1 44.7 %copy-start.8 = (bf16[2048,256]{1,0:T(8,128)(2,1)S(1)}, bf16[2048,256]{1,0:T(8,128)(2,1)}, u32[]{:S(2)}) copy-start(bf16[2048,256]{1,0:T(8,128)(2,1)} %param.18) | copy-start | bytes 3145732
  118.1 56.7 %copy-start.35 = (f32[256]{0:T(256)S(1)}, f32[256]{0:T(256)}, u32[]{:S(2)}) copy-start(f32[256]{0:T(256)} %param.28) | copy-start | bytes 3076
  118.1 56.7 %copy-start.45 = (f32[256]{0:T(256)S(1)}, f32[256]{0:T(256)}, u32[]{:S(2)}) copy-start(f32[256]{0:T(256)} %param.29) | copy-start | bytes 3076
  118.1 95.5 %all-gather.9.cloned.1.call-start = ((), (), s32[]{:S(2)}) async-start(), calls=%async_computation.6 | async-start | bytes 5242880 | tf_op jit(solution)/shard_map/all_gather | solution.py:158
  174.8 155.5 %copy-start.23 = (f32[2048]{0:T(1024)}, f32[2048]{0:T(1024)S(1)}, u32[]{:S(2)}) copy-start(f32[2048]{0:T(1024)S(1)} %get-tuple-element.385) | copy-start | bytes 24580
  174.8 155.5 %copy-start.25 = (f32[2048]{0:T(1024)}, f32[2048]{0:T(1024)S(1)}, u32[]{:S(2)}) copy-start(f32[2048]{0:T(1024)S(1)} %get-tuple-element.386) | copy-start | bytes 24580
  177.4 72.8 %all-gather.11.cloned.1.call-start = ((), (), s32[]{:S(2)}) async-start(), calls=%async_computation.8 | async-start | bytes 5242880 | tf_op jit(solution)/shard_map/all_gather | solution.py:165
  178.0 72.2 %copy-start.49 = (f32[1024]{0:T(1024)S(1)}, f32[1024]{0:T(1024)}, u32[]{:S(2)}) copy-start(f32[1024]{0:T(1024)} %param.23) | copy-start | bytes 12292
  178.0 138.4 %reduce-scatter.9.cloned.1.call-start = ((), (), s32[]{:S(2)}) async-start(), calls=%async_computation.9 | async-start | bytes 5242880 | tf_op jit(solution)/shard_map/reduce_scatter | solution.py:22
  271.8 99.7 %all-gather.13.cloned.1.call-start = ((), (), s32[]{:S(2)}) async-start(), calls=%async_computation.10 | async-start | bytes 5242880 | tf_op jit(solution)/shard_map/all_gather | solution.py:185
  330.3 44.8 %copy-start.33 = (f32[2048]{0:T(1024)}, f32[2048]{0:T(1024)S(1)}, u32[]{:S(2)}) copy-start(f32[2048]{0:T(1024)S(1)} %get-tuple-element.366) | copy-start | bytes 24580
  335.2 228.0 %reduce-scatter.11.cloned.1.call-start = ((), (), s32[]{:S(2)}) async-start(), calls=%async_computation.11 | async-start | bytes 5242880 | tf_op jit(solution)/shard_map/reduce_scatter | solution.py:22
  507.8 92.5 %reduce-scatter.7.cloned.1.call-start = ((), (), s32[]{:S(2)}) async-start(), calls=%async_computation.7 | async-start | bytes 5242880 | tf_op jit(solution)/shard_map/reduce_scatter | solution.py:22
  519.6 487.2 %all-reduce.7.cloned.1.call-start = ((), (), s32[]{:S(2)}) async-start(), calls=%async_computation.12 | async-start | bytes 25165824 | tf_op jit(solution)/shard_map/psum | solution.py:235
  557.3 43.0 %copy-start.9 = (bf16[2048,256]{1,0:T(8,128)(2,1)S(1)}, bf16[2048,256]{1,0:T(8,128)(2,1)}, u32[]{:S(2)}) copy-start(bf16[2048,256]{1,0:T(8,128)(2,1)} %param.18) | copy-start | bytes 3145732
  557.3 42.9 %copy-start.24 = (f32[2048]{0:T(1024)S(1)}, f32[2048]{0:T(1024)}, u32[]{:S(2)}) copy-start(f32[2048]{0:T(1024)} %copy-done.23) | copy-start | bytes 24580
  557.4 42.9 %copy-start.26 = (f32[2048]{0:T(1024)S(1)}, f32[2048]{0:T(1024)}, u32[]{:S(2)}) copy-start(f32[2048]{0:T(1024)} %copy-done.25) | copy-start | bytes 24580
  557.4 42.9 %copy-start.32 = (f32[2048]{0:T(1024)S(1)}, f32[2048]{0:T(1024)}, u32[]{:S(2)}) copy-start(f32[2048]{0:T(1024)} %copy-done.31) | copy-start | bytes 24580
  557.4 42.9 %copy-start.34 = (f32[2048]{0:T(1024)S(1)}, f32[2048]{0:T(1024)}, u32[]{:S(2)}) copy-start(f32[2048]{0:T(1024)} %copy-done.33) | copy-start | bytes 24580
  557.4 42.9 %copy-start.36 = (f32[256]{0:T(256)S(1)}, f32[256]{0:T(256)}, u32[]{:S(2)}) copy-start(f32[256]{0:T(256)} %param.28) | copy-start | bytes 3076
  557.4 42.9 %copy-start.46 = (f32[256]{0:T(256)S(1)}, f32[256]{0:T(256)}, u32[]{:S(2)}) copy-start(f32[256]{0:T(256)} %param.25) | copy-start | bytes 3076
  (62 other events, 347.2 us)
Sparse Core Ops, SparseCore 0:
  9.6 37.7 all-gather.6
  118.3 44.4 reduce-scatter.4
  177.6 36.0 all-gather.8
  215.1 35.0 all-gather.10
  271.9 44.5 reduce-scatter.8
  335.3 36.1 all-gather.12
  507.9 44.4 reduce-scatter.10
  555.7 44.5 reduce-scatter.6
  605.6 401.1 all-reduce.6
where the time goes:
time: 1040 us; the launch traced here: 1030 us
  waiting for transfers between devices  613 us (59%)
  matrix products  192 us (18%)
  other arithmetic  88.1 us (8%)
  blocking collectives  66 us (6%)
  local copies, waits for them, and re-layouts  50.1 us (5%)
  between operations  14.9 us (1%)
    psum x1, waiting for transfers between devices, local(): lax.psum((d_qkv, d_out, d_gain_one, d_shift_one, d_up, d_up_bias, d_down,...  377 us
    reduce_scatter x4, waiting for transfers between devices, column_total(): lax.psum_scatter(partial_value.astype(jnp.bfloat16), 'tp', scatter_dimens...  112 us
    dot_general x8, matrix products, masked_scores(): jnp.einsum('qhd,khd->hqk', q_block, key_rows, preferred_element_type=jnp....  36.4 us
    all_gather x1, waiting for transfers between devices, local(): d_branch_full = lax.all_gather(d_branch, 'tp', axis=1, tiled=True)  36.2 us
    all_gather x1, waiting for transfers between devices, local(): mlp_full = lax.all_gather(mlp_input, 'tp', axis=1, tiled=True)  35.6 us
    convert_element_type x4, other arithmetic, back_step(): d_scores = (softmaxed * (d_probs - jnp.sum(softmaxed * d_probs, axis=-1,...  34.9 us
    psum x3, blocking collectives, row_totals(): return lax.psum((first, second), 'tp')  31 us
    all_gather x1, waiting for transfers between devices, local(): lax.all_gather(datapoints, 'tp', axis=1, tiled=True)  25.7 us
  transfers between devices with their start and end apart: 9, of which 8 were waited for; matrix products, arithmetic and copies ran while one was open for 8% of the time, Pallas kernels for 0%

commit v1 on v0

v1 whole, which is shorter than its diff:
```python
import functools

import jax
import jax.numpy as jnp
from jax import lax
from jax.experimental import pallas as pl
from jax.experimental.pallas import tpu as pltpu
from jax.sharding import PartitionSpec as P

DH = 128
TILE = 256
EPS_NORM = 1e-05
NEG_FILL = -1e30
F32 = jnp.float32
BF16 = jnp.bfloat16
VMEM_LIMIT = 48 * 1024 * 1024
GELU_C = 0.7978845608028654


def dot_nn(a, b):
    return jnp.dot(a, b, preferred_element_type=F32)


def dot_nt(a, b):
    return lax.dot_general(a, b, (((1,), (1,)), ((), ())), preferred_element_type=F32)


def dot_tn(a, b):
    return lax.dot_general(a, b, (((0,), (0,)), ((), ())), preferred_element_type=F32)


def call(body, grid, in_specs, out_specs, out_shape, scalars, operands, scratch=(), flops=0):
    bytes_moved = sum(o.size * o.dtype.itemsize for o in operands)
    bytes_moved += sum(
        o.size * jnp.dtype(o.dtype).itemsize for o in jax.tree_util.tree_leaves(out_shape)
    )
    return pl.pallas_call(
        body,
        grid_spec=pltpu.PrefetchScalarGridSpec(
            num_scalar_prefetch=1,
            grid=grid,
            in_specs=in_specs,
            out_specs=out_specs,
            scratch_shapes=list(scratch),
        ),
        out_shape=out_shape,
        compiler_params=pltpu.CompilerParams(
            vmem_limit_bytes=VMEM_LIMIT,
            dimension_semantics=("arbitrary",) * len(grid),
        ),
        cost_estimate=pl.CostEstimate(
            flops=int(flops), bytes_accessed=int(bytes_moved), transcendentals=0
        ),
    )(scalars, *operands)


def full(shape):
    zeros = (0,) * len(shape)
    return pl.BlockSpec(shape, lambda *_: zeros, pipeline_mode=pl.Buffered(1))


def shape_of(shape, dtype):
    return jax.ShapeDtypeStruct(shape, dtype)


def ln_qkv_body(sc, x0, x1, x2, x3, gains, weight, qkv, acts, stats):
    t = sc[0]
    pieces = [x[...].astype(F32) for x in (x0, x1, x2, x3)]
    width = pieces[0].shape[1]
    count = width * len(pieces)
    mean = sum(jnp.sum(x, axis=1, keepdims=True) for x in pieces) / count
    centered = [x - mean for x in pieces]
    var = sum(jnp.sum(c * c, axis=1, keepdims=True) for c in centered) / count
    rstd = lax.rsqrt(var + EPS_NORM)
    total = [0.0, 0.0, 0.0]
    for k, c in enumerate(centered):
        j = jnp.bitwise_xor(t, k)
        part = (c * rstd * gains[k, 0:1, :] + gains[k, 1:2, :]).astype(BF16)
        acts[:, pl.ds(pl.multiple_of(j * width, width), width)] = part
        for s in range(3):
            total[s] = total[s] + dot_nn(part, weight[s, j])
    qkv[0] = (total[0] * (DH ** (-0.5))).astype(BF16)
    qkv[1] = total[1].astype(BF16)
    qkv[2] = total[2].astype(BF16)
    stats[:, 0:1] = mean
    stats[:, 1:2] = rstd


def ln_qkv(scalars, pieces, gains, weight4):
    rows, width = pieces[0].shape
    n = len(pieces)
    tiles = rows // TILE
    return call(
        ln_qkv_body,
        (tiles,),
        [pl.BlockSpec((TILE, width), lambda i, sc: (i, 0))] * n
        + [full(gains.shape), full(weight4.shape)],
        [
            pl.BlockSpec((3, TILE, width), lambda i, sc: (0, i, 0)),
            pl.BlockSpec((TILE, n * width), lambda i, sc: (i, 0)),
            pl.BlockSpec((TILE, 2), lambda i, sc: (i, 0)),
        ],
        [
            shape_of((3, rows, width), BF16),
            shape_of((rows, n * width), BF16),
            shape_of((rows, 2), F32),
        ],
        scalars,
        [*pieces, gains, weight4],
        flops=2 * rows * n * width * 3 * width,
    )


def attend_body(masked, sc, q, k, v, o, lse):
    i = pl.program_id(1)
    scores = dot_nt(q[0], k[0])
    rows, cols = scores.shape
    if masked:
        q_side = (i * rows + lax.broadcasted_iota(jnp.int32, (rows, 1), 0)) < sc[1]
        k_side = lax.broadcasted_iota(jnp.int32, (1, cols), 1) < sc[1]
        scores = jnp.where(jnp.logical_xor(q_side, k_side), NEG_FILL, scores)
    top = jnp.max(scores, axis=1, keepdims=True)
    weights = jnp.exp(scores - top)
    total = jnp.sum(weights, axis=1, keepdims=True)
    mixed = dot_nn(weights.astype(BF16), v[0])
    o[...] = (mixed / total).astype(BF16)
    stat = jnp.broadcast_to(top + jnp.log(total), (rows, DH))
    lse[0] = jnp.transpose(stat)[0:1, :]


def attend(scalars, qkv, masked):
    _, rows, width = qkv.shape
    heads = width // DH
    tiles = rows // TILE
    return call(
        functools.partial(attend_body, masked),
        (heads, tiles),
        [
            pl.BlockSpec((1, TILE, DH), lambda h, i, sc: (0, i, h)),
            pl.BlockSpec((1, rows, DH), lambda h, i, sc: (1, 0, h)),
            pl.BlockSpec((1, rows, DH), lambda h, i, sc: (2, 0, h)),
        ],
        [
            pl.BlockSpec((TILE, DH), lambda h, i, sc: (i, h)),
            pl.BlockSpec((1, 1, TILE), lambda h, i, sc: (h, 0, i)),
        ],
        [shape_of((rows, width), BF16), shape_of((heads, 1, rows), F32)],
        scalars,
        [qkv, qkv, qkv],
        flops=4 * rows * rows * width * 2,
    )


def feed_body(
    sc, x0, x1, x2, x3, o0, o1, o2, o3, d0, d1, d2, d3, w0, w1, w2, w3,
    gains, up, up_t, down_t, bias,
    y_out, b_out, g_out, du_out, dy_out, send, keep, bias_grad, y_acc,
):
    t = sc[0]
    i = pl.program_id(0)
    xs, os, ds, ws = (x0, x1, x2, x3), (o0, o1, o2, o3), (d0, d1, d2, d3), (w0, w1, w2, w3)
    width = x0.shape[1]
    n = len(xs)
    count = n * width

    def block(k):
        j = jnp.bitwise_xor(t, k)
        return pl.ds(pl.multiple_of(j * width, width), width)

    y_acc[...] = sum(dot_nn(o[...], w[...]) for o, w in zip(os, ws))
    for k in range(n):
        y_acc[:, block(k)] += xs[k][...].astype(F32)
        dy_out[:, block(k)] = ds[k][...]
    y = y_acc[...]
    y_out[...] = y
    mean = jnp.sum(y, axis=1, keepdims=True) / count
    centered = y - mean
    rstd = lax.rsqrt(jnp.sum(centered * centered, axis=1, keepdims=True) / count + EPS_NORM)
    b = (centered * rstd * gains[2:3, :] + gains[3:4, :]).astype(BF16)
    b_out[...] = b
    dy = dy_out[...]
    hidden = up.shape[1]
    step = 256
    total = None
    for f in range(0, hidden, step):
        cols = slice(f, f + step)
        u = dot_nn(b, up[:, cols]) + bias[:, cols]
        dh = dot_nn(dy, down_t[:, cols])
        cubic = u * u
        th = jnp.tanh(GELU_C * u * (1.0 + 0.044715 * cubic))
        half = 0.5 * (1.0 + th)
        g_out[:, cols] = (u * half).astype(BF16)
        slope = half + (0.5 * GELU_C) * u * (1.0 - th * th) * (1.0 + 0.134145 * cubic)
        du = (dh * slope).astype(BF16)
        du_out[:, cols] = du
        sums = jnp.sum(du.astype(F32), axis=0, keepdims=True)

        @pl.when(i == 0)
        def _():
            bias_grad[:, cols] = sums

        @pl.when(i > 0)
        def _():
            bias_grad[:, cols] += sums

        part = dot_nn(du, up_t[cols, :])
        total = part if total is None else total + part
    low = total.astype(BF16)

    @pl.when(i < 2)
    def _():
        send[0] = low

    @pl.when(i >= 2)
    def _():
        keep[0] = low


def relative(i):
    return jnp.where(i < 2, 2 * i + 1, 2 * i - 4)


def feed(scalars, xs, os, dys, ows, gains, up, up_t, down_t, bias):
    rows, width = xs[0].shape
    n = len(xs)
    count = n * width
    hidden = up.shape[1]
    tiles = rows // TILE

    def tile(i, sc):
        return (jnp.bitwise_xor(sc[0], relative(i)), 0)

    return call(
        feed_body,
        (tiles,),
        [pl.BlockSpec((TILE, width), tile)] * (3 * n)
        + [full(w.shape) for w in ows]
        + [full(gains.shape), full(up.shape), full(up_t.shape), full(down_t.shape), full(bias.shape)],
        [
            pl.BlockSpec((TILE, count), tile),
            pl.BlockSpec((TILE, count), tile),
            pl.BlockSpec((TILE, hidden), tile),
            pl.BlockSpec((TILE, hidden), tile),
            pl.BlockSpec((TILE, count), tile),
            pl.BlockSpec((1, TILE, count), lambda i, sc: (jnp.minimum(i, 1), 0, 0)),
            pl.BlockSpec((1, TILE, count), lambda i, sc: (jnp.maximum(i - 2, 0), 0, 0)),
            pl.BlockSpec((1, hidden), lambda i, sc: (0, 0)),
        ],
        [
            shape_of((rows, count), F32),
            shape_of((rows, count), BF16),
            shape_of((rows, hidden), BF16),
            shape_of((rows, hidden), BF16),
            shape_of((rows, count), BF16),
            shape_of((2, TILE, count), BF16),
            shape_of((2, TILE, count), BF16),
            shape_of((1, hidden), F32),
        ],
        scalars,
        [*xs, *os, *dys, *ows, gains, up, up_t, down_t, bias],
        scratch=[pltpu.VMEM((TILE, count), F32)],
        flops=2 * rows * count * (count + 3 * hidden),
    )


def norm_back_body(sc, p0, p1, p2, y, dy, gains, dz, sums):
    db = p0[0].astype(F32) + p1[0].astype(F32) + p2[...].astype(F32)
    yv = y[...]
    count = yv.shape[1]
    mean = jnp.sum(yv, axis=1, keepdims=True) / count
    centered = yv - mean
    rstd = lax.rsqrt(jnp.sum(centered * centered, axis=1, keepdims=True) / count + EPS_NORM)
    nhat = centered * rstd
    n = db * gains[2:3, :]
    first = jnp.sum(n, axis=1, keepdims=True) / count
    second = jnp.sum(n * nhat, axis=1, keepdims=True) / count
    dz[...] = (dy[...].astype(F32) + rstd * (n - first - nhat * second)).astype(BF16)
    sums[0:1, :] = jnp.sum(db * nhat, axis=0, keepdims=True)
    sums[1:2, :] = jnp.sum(db, axis=0, keepdims=True)


def norm_back(scalars, keep, got_core, got_x, y, dy, gains):
    rows, count = got_x.shape
    return call(
        norm_back_body,
        (1,),
        [
            pl.BlockSpec((1, rows, count), lambda i, sc: (0, 0, 0)),
            pl.BlockSpec((1, rows, count), lambda i, sc: (0, 0, 0)),
            pl.BlockSpec((rows, count), lambda i, sc: (0, 0)),
            pl.BlockSpec((rows, count), lambda i, sc: (sc[0], 0)),
            pl.BlockSpec((rows, count), lambda i, sc: (sc[0], 0)),
            full(gains.shape),
        ],
        [
            pl.BlockSpec((rows, count), lambda i, sc: (0, 0)),
            pl.BlockSpec((2, count), lambda i, sc: (0, 0)),
        ],
        [shape_of((rows, count), BF16), shape_of((2, count), F32)],
        scalars,
        [keep, got_core, got_x, y, dy, gains],
    )


def attend_back_body(masked, sc, z0, z1, z2, z3, out_t, q, k, v, lse, dq, dk, dv, dz_out, dk_acc, dv_acc):
    i = pl.program_id(0)
    t = sc[0]
    for j, z in enumerate((z0, z1, z2, z3)):

        @pl.when(i == j)
        def _(z=z):
            dz_out[...] = z[...]

    d_mixed = dot_nn(dz_out[...], out_t[...]).astype(BF16)
    rows = d_mixed.shape[0]
    keys = k.shape[1]
    for h in range(d_mixed.shape[1] // DH):
        cols = slice(h * DH, (h + 1) * DH)
        q_h, k_h, v_h, do_h = q[0, :, cols], k[0, :, cols], v[0, :, cols], d_mixed[:, cols]
        scores = dot_nt(k_h, q_h)
        if masked:
            base = jnp.bitwise_xor(t, i) * rows
            q_side = (base + lax.broadcasted_iota(jnp.int32, (1, rows), 1)) < sc[1]
            k_side = lax.broadcasted_iota(jnp.int32, (keys, 1), 0) < sc[1]
            scores = jnp.where(jnp.logical_xor(q_side, k_side), NEG_FILL, scores)
        p = jnp.exp(scores - lse[h])
        d_p = dot_nt(v_h, do_h)
        prod = p * d_p
        delta = jnp.sum(prod, axis=0, keepdims=True)
        d_s = (prod - p * delta).astype(BF16)
        d_v = dot_nn(p.astype(BF16), do_h)
        d_k = dot_nn(d_s, q_h)

        @pl.when(i == 0)
        def _():
            dv_acc[:, cols] = d_v
            dk_acc[:, cols] = d_k

        @pl.when(i > 0)
        def _():
            dv_acc[:, cols] += d_v
            dk_acc[:, cols] += d_k

        dq[:, cols] = dot_tn(d_s, k_h).astype(BF16)

    @pl.when(i == pl.num_programs(0) - 1)
    def _():
        dk[...] = dk_acc[...].astype(BF16)
        dv[...] = dv_acc[...].astype(BF16)


def attend_back(scalars, dzs, out_t, qkv, lse, masked):
    _, rows, width = qkv.shape
    heads = width // DH
    count = out_t.shape[0]
    tiles = rows // TILE

    def tile(i, sc):
        return (jnp.bitwise_xor(sc[0], i), 0)

    return call(
        functools.partial(attend_back_body, masked),
        (tiles,),
        [full(dz.shape) for dz in dzs]
        + [
            full(out_t.shape),
            pl.BlockSpec((1, TILE, width), lambda i, sc: (0, jnp.bitwise_xor(sc[0], i), 0)),
            pl.BlockSpec((1, rows, width), lambda i, sc: (1, 0, 0)),
            pl.BlockSpec((1, rows, width), lambda i, sc: (2, 0, 0)),
            pl.BlockSpec((heads, 1, TILE), lambda i, sc: (0, 0, jnp.bitwise_xor(sc[0], i))),
        ],
        [
            pl.BlockSpec((TILE, width), tile),
            pl.BlockSpec((rows, width), lambda i, sc: (0, 0)),
            pl.BlockSpec((rows, width), lambda i, sc: (0, 0)),
            pl.BlockSpec((TILE, count), tile),
        ],
        [
            shape_of((rows, width), BF16),
            shape_of((rows, width), BF16),
            shape_of((rows, width), BF16),
            shape_of((rows, count), BF16),
        ],
        scalars,
        [*dzs, out_t, qkv, qkv, qkv, lse],
        scratch=[pltpu.VMEM((rows, width), F32), pltpu.VMEM((rows, width), F32)],
        flops=2 * rows * count * width + 20 * rows * rows * width,
    )


def spread_body(scale, n_in, sc, *refs):
    lefts, rights, send, keep = refs[:n_in], refs[n_in : 2 * n_in], refs[-2], refs[-1]
    total = None
    for left, right in zip(lefts, rights):
        part = dot_nn(left[...], right[...])
        if total is None:
            total = part * scale if scale != 1.0 else part
        else:
            total = total + part
    low = total.astype(BF16)
    i = pl.program_id(0)

    @pl.when(i < 2)
    def _():
        send[0] = low

    @pl.when(i >= 2)
    def _():
        keep[0] = low


def spread(scalars, lefts, rights, scale=1.0):
    rows = lefts[0].shape[0]
    count = rights[0].shape[1]
    width = count // 4

    def cols(i, sc):
        return (0, jnp.bitwise_xor(sc[0], relative(i)))

    return call(
        functools.partial(spread_body, scale, len(lefts)),
        (4,),
        [full(a.shape) for a in lefts]
        + [pl.BlockSpec((b.shape[0], width), cols) for b in rights],
        [
            pl.BlockSpec((1, rows, width), lambda i, sc: (jnp.minimum(i, 1), 0, 0)),
            pl.BlockSpec((1, rows, width), lambda i, sc: (jnp.maximum(i - 2, 0), 0, 0)),
        ],
        [shape_of((2, rows, width), BF16), shape_of((2, rows, width), BF16)],
        scalars,
        [*lefts, *rights],
        flops=sum(2 * a.shape[0] * a.shape[1] * b.shape[1] for a, b in zip(lefts, rights)),
    )


def weight_grad_body(bit, n_cols, sc, a0, a1, *refs):
    rights0, rights1 = refs[:n_cols], refs[n_cols : 2 * n_cols]
    send, keep = refs[-2], refs[-1]
    i = pl.program_id(0)
    at = 0
    for r0, r1 in zip(rights0, rights1):
        width = r0.shape[1]
        low = (dot_tn(a0[...], r0[...]) + dot_tn(a1[...], r1[...])).astype(BF16)

        @pl.when(i == 0)
        def _():
            send[:, at : at + width] = low

        @pl.when(i == 1)
        def _():
            keep[:, at : at + width] = low

        at += width


def weight_grad(scalars, lefts, rights0, rights1, bit):
    rows, m = lefts[0].shape
    count = sum(b.shape[1] for b in rights0)

    def half(i, sc):
        mine = jnp.bitwise_and(jnp.right_shift(sc[2], bit), 1)
        return (0, jnp.where(i == 0, 1 - mine, mine))

    return call(
        functools.partial(weight_grad_body, bit, len(rights0)),
        (2,),
        [pl.BlockSpec((rows, m // 2), half)] * 2 + [full(b.shape) for b in (*rights0, *rights1)],
        [full((m // 2, count))] * 2,
        [shape_of((m // 2, count), BF16)] * 2,
        scalars,
        [*lefts, *rights0, *rights1],
        flops=4 * rows * m * count,
    )


def place_body(sc, first, second, out):
    i = pl.program_id(0)
    half = pl.num_programs(0) // 2

    @pl.when(i < half)
    def _():
        out[...] = first[...].astype(F32)

    @pl.when(i >= half)
    def _():
        out[...] = second[...].astype(F32)


def place(index, first, second, blocks):
    m, count = first.shape[0] * 2, first.shape[1]
    rows = m // blocks
    half = blocks // 2
    return call(
        place_body,
        (blocks,),
        [
            pl.BlockSpec((rows, count), lambda i, sc: (jnp.minimum(i, half - 1), 0)),
            pl.BlockSpec((rows, count), lambda i, sc: (jnp.maximum(i - half, 0), 0)),
        ],
        pl.BlockSpec((rows, count), lambda i, sc: (jnp.bitwise_xor(sc[0], i), 0)),
        shape_of((m, count), F32),
        index,
        [first, second],
    )


class RowSum:
    def __init__(self, r, n_rows, send, keep, bits):
        self.r, self.n_rows = r, n_rows
        self.bits = bits
        self.rest = [b for b in range(n_rows.bit_length() - 1) if b not in bits]
        self.send, self.keep = send, keep

    def flip(self, value, bit):
        return lax.ppermute(
            value, "rows", [(i, i ^ (1 << bit)) for i in range(self.n_rows)]
        )

    def bit(self, b):
        return jnp.bitwise_and(jnp.right_shift(self.r, b), 1)

    def scatter(self):
        send, keep = self.send, self.keep
        for at, b in enumerate(self.bits):
            got = self.flip(send, b)
            if at + 1 < len(self.bits):
                nxt = self.bit(self.bits[at + 1])
                half = keep.shape[0] // 2
                other, mine = (1 - nxt) * half, nxt * half

                def part(start):
                    a = lax.dynamic_slice_in_dim(keep, start, half, 0).astype(F32)
                    c = lax.dynamic_slice_in_dim(got, start, half, 0).astype(F32)
                    return a + c

                send, keep = part(other).astype(BF16), part(mine)
            else:
                total = keep.astype(F32) + got.astype(F32)
        for b in self.rest:
            low = total.astype(BF16)
            total = low.astype(F32) + self.flip(low, b).astype(F32)
        self.own = total.astype(BF16)
        return self

    def gather(self):
        buf = self.own
        index = 0
        for b in reversed(self.bits):
            got = self.flip(buf, b)
            last, buf = buf, jnp.concatenate([buf, got], 0) if b != self.bits[0] else None
        for b in self.bits:
            index = index * 2 + self.bit(b)
        blocks = 1 << len(self.bits)
        return place(jnp.stack([index, index]).astype(jnp.int32), last, got, blocks)


def local(
    n_tp, n_rows,
    datapoints, lengths, qkv_weight, out_weight, up_weight, up_bias, down_weight, down_bias,
    gain_one, shift_one, gain_two, shift_two, grad_out,
):
    tok, width = datapoints.shape
    count = n_tp * width
    half = tok // 2
    q_scale = DH ** (-0.5)
    t, r = lax.axis_index("tp"), lax.axis_index("rows")

    def core_flip(v):
        return lax.ppermute(v, "tp", [(i, i ^ 1) for i in range(n_tp)])

    def x_flip(v):
        return lax.ppermute(v, "tp", [(i, i ^ 2) for i in range(n_tp)])

    def gather(own):
        across = x_flip(own)
        return [own, core_flip(own), across, core_flip(across)]

    def row_flip(v, b):
        return lax.ppermute(v, "rows", [(i, i ^ (1 << b)) for i in range(n_rows)])

    lens = lengths.reshape(-1)
    sets = lens.shape[0]
    big = jnp.argmax(lens)
    start = jnp.sum(jnp.where(jnp.arange(sets) < big, lens, 0))
    border = lens[lax.rem(big + 1, sets)]
    scalars = jnp.stack([t, border, r]).astype(jnp.int32)

    def halves(v):
        twice = jnp.concatenate([v, v[:half]], 0)
        return [
            lax.dynamic_slice_in_dim(v, start, half, 0),
            lax.dynamic_slice_in_dim(twice, start + half, half, 0),
        ]

    def unroll(first, second):
        thrice = jnp.concatenate([second, first, second], 0)
        return lax.dynamic_slice_in_dim(thrice, half - start, tok, 0)

    x_own, dy_own = halves(datapoints), halves(grad_out)
    vectors = jnp.stack([gain_one, shift_one, gain_two, shift_two])
    gains_rel = jnp.stack(gather(vectors))
    order = jnp.bitwise_xor(t, jnp.arange(n_tp))
    gains = jnp.transpose(gains_rel[order], (1, 0, 2)).reshape(4, count)
    xs = [gather(x) for x in x_own]
    ows = gather(out_weight)
    dys = [gather(d) for d in dy_own]

    weight4 = qkv_weight.reshape(3, n_tp, width, width)
    qkv_t = jnp.transpose(qkv_weight, (0, 2, 1))
    out_t = out_weight.T
    up_t = up_weight.T
    down_t = down_weight.T
    bias = up_bias.reshape(1, -1)

    qkv, acts, stats, mixed, lse = [], [], [], [], []
    for h in range(2):
        p, a, s = ln_qkv(scalars, xs[h], gains_rel, weight4)
        o, l = attend(scalars, p, h == 1)
        qkv.append(p)
        acts.append(a)
        stats.append(s)
        mixed.append(o)
        lse.append(l)
    mixed_all = [gather(o) for o in mixed]

    y, b, g, du, dy, d_up_bias, dz_own, two_sums = [], [], [], [], [], 0.0, [], 0.0
    for h in range(2):
        yh, bh, gh, duh, dyh, send, keep, bias_grad = feed(
            scalars, xs[h], mixed_all[h], dys[h], ows, gains, up_weight, up_t, down_t, bias
        )
        got = core_flip(send)
        got_x = x_flip((keep[1].astype(F32) + got[1].astype(F32)).astype(BF16))
        dz, sums = norm_back(scalars, keep, got, got_x, yh, dyh, gains)
        y.append(yh)
        b.append(bh)
        g.append(gh)
        du.append(duh)
        dy.append(dyh)
        dz_own.append(dz)
        d_up_bias = d_up_bias + bias_grad
        two_sums = two_sums + sums
    dzs = [gather(dz) for dz in dz_own]

    d_down = RowSum(r, n_rows, *weight_grad(scalars, g, [dy[0]], [dy[1]], 0), [0, 1, 2])
    d_up = RowSum(r, n_rows, *weight_grad(scalars, b, [du[0]], [du[1]], 1), [1, 0, 2])
    d_down.scatter()
    d_up.scatter()

    outs = []
    for h in range(2):
        send, keep = spread(scalars, [g[h]], [down_weight])
        got = core_flip(send)
        got_x = x_flip((keep[1].astype(F32) + got[1].astype(F32)).astype(BF16))
        y_mine = lax.dynamic_slice_in_dim(y[h], t * width, width, 1)
        total = keep[0].astype(F32) + got[0].astype(F32) + got_x.astype(F32)
        outs.append((y_mine + total + down_bias).astype(BF16))
    output = unroll(*outs)

    d_parts, dz_nat = [], []
    d_inputs, one_gain, one_shift = [], 0.0, 0.0
    for h in range(2):
        dq, dk, dv, dzn = attend_back(scalars, dzs[h], out_t, qkv[h], lse[h], h == 1)
        d_parts.append([dq, dk, dv])
        dz_nat.append(dzn)

    d_out = RowSum(
        r, n_rows, *weight_grad(scalars, mixed, [dz_nat[0]], [dz_nat[1]], 1), [1, 0, 2]
    )
    d_qkv = RowSum(r, n_rows, *weight_grad(scalars, acts, d_parts[0], d_parts[1], 0), [0, 1, 2])
    d_out.scatter()
    d_qkv.scatter()

    for h in range(2):
        send, keep = spread(scalars, d_parts[h], [qkv_t[0], qkv_t[1], qkv_t[2]], q_scale)
        got = core_flip(send)
        got_x = x_flip((keep[1].astype(F32) + got[1].astype(F32)).astype(BF16))
        da = keep[0].astype(F32) + got[0].astype(F32) + got_x.astype(F32)
        mean, rstd = stats[h][:, 0:1], stats[h][:, 1:2]
        nhat = (x_own[h].astype(F32) - mean) * rstd
        one_gain = one_gain + jnp.sum(da * nhat, axis=0)
        one_shift = one_shift + jnp.sum(da, axis=0)
        n = da * gain_one
        moments = jnp.stack([jnp.sum(n, axis=1), jnp.sum(n * nhat, axis=1)])
        moments = moments + core_flip(moments)
        moments = moments + x_flip(moments)
        first, second = moments[0][:, None] / count, moments[1][:, None] / count
        dz_mine = lax.dynamic_slice_in_dim(dz_nat[h], t * width, width, 1).astype(F32)
        d_inputs.append(dz_mine + rstd * (n - first - nhat * second))
    d_input = unroll(*d_inputs)

    d_down_bias = jnp.sum(grad_out.astype(F32), axis=0)
    two_sums = two_sums + core_flip(two_sums)
    two_sums = two_sums + x_flip(two_sums)
    two_mine = lax.dynamic_slice_in_dim(two_sums, t * width, width, 1)
    small = jnp.concatenate(
        [d_up_bias.reshape(-1), d_down_bias, one_gain, one_shift, two_mine[0], two_mine[1]]
    ).reshape(-1, 128)
    for bit in range(n_rows.bit_length() - 1):
        small = small + row_flip(small, bit)
    small = small.reshape(-1)
    hidden = up_bias.shape[0]
    d_up_bias = small[:hidden]
    d_down_bias, d_gain_one, d_shift_one, d_gain_two, d_shift_two = small[hidden:].reshape(5, width)

    d_qkv = jnp.transpose(d_qkv.gather().reshape(count, 3, width), (1, 0, 2))
    d_qkv = d_qkv * jnp.array([q_scale, 1.0, 1.0], F32)[:, None, None]
    return (
        output, d_input, d_qkv, d_out.gather(), d_up.gather(), d_up_bias, d_down.gather(),
        d_down_bias, d_gain_one, d_shift_one, d_gain_two, d_shift_two,
    )


def solution(mesh):
    grid = P("rows", "tp")
    placed = (
        grid, P("rows", None), P(None, None, "tp"), P("tp", None), P(None, "tp"), P("tp"),
        P("tp", None), P("tp"), P("tp"), P("tp"), P("tp"), P("tp"), grid,
    )
    return jax.shard_map(
        functools.partial(local, mesh.shape["tp"], mesh.shape["rows"]),
        mesh=mesh,
        in_specs=placed,
        out_specs=(
            grid, grid, P(None, None, "tp"), P("tp", None), P(None, "tp"), P("tp"),
            P("tp", None), P("tp"), P("tp"), P("tp"), P("tp"), P("tp"),
        ),
        check_vma=False,
    )
```

time: 1040 us -> 482 us (0.46)
  waiting for transfers between devices: 613 us -> 151 us
  matrix products: 192 us -> 0 us
  Pallas kernels: 0 us -> 171 us
  blocking collectives: 66 us -> 0 us
  starting transfers between devices: 0.79 us -> 64.1 us
  other arithmetic: 88.1 us -> 42.2 us
  local copies, waits for them, and re-layouts: 50.1 us -> 36.8 us
    psum x1 -> x0, waiting for transfers between devices: 377 us -> none  [local(): lax.psum((d_qkv, d_out, d_gain_one, d_shift_one, d_up, d_up_bias, d_down,...]
    dot_general x42 -> x0, matrix products: 192 us -> none  [the longest x8 36.4 us: masked_scores(): jnp.einsum('qhd,khd->hqk', q_block, key_rows, preferred_element_type=jnp....]
    pallas_call x0 -> x22, Pallas kernels: none -> 171 us  [call(): pl.pallas_call(body, grid_spec=pltpu.PrefetchScalarGridSpec(num_scalar_pr...]
    ppermute x0 -> x75, waiting for transfers between devices: none -> 151 us  [the longest x24 87.2 us: flip(): lax.ppermute(value, 'rows', [(i, i ^ 1 << bit) for i in range(self.n_rows)])]
    all_gather x4 -> x0, waiting for transfers between devices: 123 us -> none  [the longest x1 36.2 us: local(): d_branch_full = lax.all_gather(d_branch, 'tp', axis=1, tiled=True)]
    reduce_scatter x4 -> x0, waiting for transfers between devices: 112 us -> none  [column_total(): lax.psum_scatter(partial_value.astype(jnp.bfloat16), 'tp', scatter_dimens...]
    ppermute x0 -> x75, starting transfers between devices: none -> 64.1 us  [the longest x24 30.3 us: flip(): lax.ppermute(value, 'rows', [(i, i ^ 1 << bit) for i in range(self.n_rows)])]
    psum x4 -> x0, blocking collectives: 54.7 us -> none  [the longest x3 31 us: row_totals(): return lax.psum((first, second), 'tp')]
  transfers between devices with their start and end apart: 9 -> 75, of which waited for: 8 -> 22; matrix products, arithmetic and copies ran while one was open for 8% -> 11% of each run, Pallas kernels for 0% -> 29%
where the time goes in v1:
time: 482 us; the launch traced here: 473 us
  Pallas kernels  171 us (35%)
  waiting for transfers between devices  151 us (31%)
  starting transfers between devices  64.1 us (13%)
  other arithmetic  42.2 us (9%)
  local copies, waits for them, and re-layouts  36.8 us (8%)
  between operations  7.37 us (2%)
    pallas_call x22, Pallas kernels, call(): pl.pallas_call(body, grid_spec=pltpu.PrefetchScalarGridSpec(num_scalar_pr...  171 us
    ppermute x24, waiting for transfers between devices, flip(): lax.ppermute(value, 'rows', [(i, i ^ 1 << bit) for i in range(self.n_rows)])  87.2 us
    ppermute x19, waiting for transfers between devices, x_flip(): return lax.ppermute(v, 'tp', [(i, i ^ 2) for i in range(n_tp)])  62.9 us
    ppermute x24, starting transfers between devices, flip(): lax.ppermute(value, 'rows', [(i, i ^ 1 << bit) for i in range(self.n_rows)])  30.3 us
    unnamed x136, local copies, waits for them, and re-layouts  28.8 us
    ppermute x19, starting transfers between devices, x_flip(): return lax.ppermute(v, 'tp', [(i, i ^ 2) for i in range(n_tp)])  24.8 us
  transfers between devices with their start and end apart: 75, of which 22 were waited for; matrix products, arithmetic and copies ran while one was open for 11% of the time, Pallas kernels for 29%

profile of v1, /device:TPU:0, one launch (start us, length us, event | category | flops | bytes accessed | tf_op | source)
XLA Modules:
  0.0 472.6 jit_solution(11780761382908637396)
XLA Ops:
  13.3 12.7 %collective-permute-done.1.x2 = bf16[1024,256]{1,0:T(8,128)(2,1)S(1)} collective-permute-done((bf16[1024,256]{1,0:T(8,128)(2,1)S(1)}, bf16[1024,256]{1,0:T(8,128)(2,1)S(1)}, u32[]{:S(2)}, u32[]{:S(2)}) %collective-permute-start.1) | collective-permute-done | bytes 524320 | tf_op jit(solution)/shard_map/ppermute | solution.py:572
  55.2 6.4 %shard_map.229 = (bf16[3,1024,256]{2,1,0:T(8,128)(2,1)S(1)}, bf16[1024,1024]{1,0:T(8,128)(2,1)}, f32[1024,2]{1,0:T(8,128)S(1)}) custom-call(s32[3]{0:T(128)S(1)} %pad_add_fusion.sc, bf16[1024,256]{1,0:T(8,128)(2,1)S(1)} %fusion.17.x0, bf16[1024,256]{1,0:T(8,128)(2,1)} %collective-permute-done.x1, bf16[1024,256]{1,0:T(8,128)(2,1)S(1)} %copy-done.13, ...), custom_call_target="tpu_custom_call" | custom-call | flops 1610612736 | bytes 7364608 | tf_op jit(solution)/shard_map/pallas_call | solution.py:37
  61.6 7.4 %shard_map.230 = (bf16[1024,256]{1,0:T(8,128)(2,1)}, f32[2,1,1024]{2,1,0:T(1,128)S(1)}) custom-call(s32[3]{0:T(128)S(1)} %pad_add_fusion.sc, bf16[3,1024,256]{2,1,0:T(8,128)(2,1)S(1)} %get-tuple-element.68.q.k.v, bf16[3,1024,256]{2,1,0:T(8,128)(2,1)S(1)} %get-tuple-element.68.q.k.v, bf16[3,1024,256]{2,1,0:T(8,128)(2,1)S(1)} %get-tuple-element.68.q.k.v), custom_call_target="tpu_custom_call" | custom-call | flops 2147483648 | bytes 5251072 | tf_op jit(solution)/shard_map/pallas_call | solution.py:37
  71.2 6.3 %shard_map.233 = (bf16[3,1024,256]{2,1,0:T(8,128)(2,1)S(1)}, bf16[1024,1024]{1,0:T(8,128)(2,1)}, f32[1024,2]{1,0:T(8,128)S(1)}) custom-call(s32[3]{0:T(128)S(1)} %pad_add_fusion.sc, bf16[1024,256]{1,0:T(8,128)(2,1)S(1)} %get-tuple-element.157.x0, bf16[1024,256]{1,0:T(8,128)(2,1)S(1)} %collective-permute-done.17.x1, ...), custom_call_target="tpu_custom_call" | custom-call | flops 1610612736 | bytes 7364608 | tf_op jit(solution)/shard_map/pallas_call | solution.py:37
  77.5 6.9 %shard_map.234 = (bf16[1024,256]{1,0:T(8,128)(2,1)}, f32[2,1,1024]{2,1,0:T(1,128)S(1)}) custom-call(s32[3]{0:T(128)S(1)} %pad_add_fusion.sc, bf16[3,1024,256]{2,1,0:T(8,128)(2,1)S(1)} %get-tuple-element.74.q.k.v, bf16[3,1024,256]{2,1,0:T(8,128)(2,1)S(1)} %get-tuple-element.74.q.k.v, bf16[3,1024,256]{2,1,0:T(8,128)(2,1)S(1)} %get-tuple-element.74.q.k.v), custom_call_target="tpu_custom_call" | custom-call | flops 2147483648 | bytes 5251072 | tf_op jit(solution)/shard_map/pallas_call | solution.py:37
  90.0 9.6 %collective-permute-done.7.o2 = bf16[1024,256]{1,0:T(8,128)(2,1)} collective-permute-done((bf16[1024,256]{1,0:T(8,128)(2,1)}, bf16[1024,256]{1,0:T(8,128)(2,1)}, u32[]{:S(2)}, u32[]{:S(2)}) %collective-permute-start.7) | collective-permute-done | bytes 524320 | tf_op jit(solution)/shard_map/ppermute | solution.py:572
  102.6 7.3 %collective-permute-done.21.o2 = bf16[1024,256]{1,0:T(8,128)(2,1)} collective-permute-done((bf16[1024,256]{1,0:T(8,128)(2,1)}, bf16[1024,256]{1,0:T(8,128)(2,1)}, u32[]{:S(2)}, u32[]{:S(2)}) %collective-permute-start.21) | collective-permute-done | bytes 524320 | tf_op jit(solution)/shard_map/ppermute | solution.py:572
  112.0 25.4 %shard_map.231 = (f32[1024,1024]{1,0:T(8,128)}, bf16[1024,1024]{1,0:T(8,128)(2,1)}, bf16[1024,1024]{1,0:T(8,128)(2,1)}, bf16[1024,1024]{1,0:T(8,128)(2,1)}, bf16...) custom-call(s32[3]{0:T(128)S(1)} %pad_add_fusion.sc, ...), custom_call_target="tpu_custom_call" | custom-call | flops 8589934592 | bytes 29384704 | tf_op jit(solution)/shard_map/pallas_call | solution.py:37
  138.3 24.3 %shard_map.235 = (f32[1024,1024]{1,0:T(8,128)}, bf16[1024,1024]{1,0:T(8,128)(2,1)}, bf16[1024,1024]{1,0:T(8,128)(2,1)}, bf16[1024,1024]{1,0:T(8,128)(2,1)}, bf16...) custom-call(s32[3]{0:T(128)S(1)} %pad_add_fusion.sc, ...), custom_call_target="tpu_custom_call" | custom-call | flops 8589934592 | bytes 29384704 | tf_op jit(solution)/shard_map/pallas_call | solution.py:37
  164.2 8.1 %shard_map.249 = (bf16[512,1024]{1,0:T(8,128)(2,1)S(1)}, bf16[512,1024]{1,0:T(8,128)(2,1)S(1)}) custom-call(s32[3]{0:T(128)S(1)} %pad_add_fusion.sc, bf16[1024,1024]{1,0:T(8,128)(2,1)S(1)} %copy-done.29, bf16[1024,1024]{1,0:T(8,128)(2,1)} %get-tuple-element.71.refs_0_.a1, bf16[1024,1024]{1,0:T(8,128)(2,1)} %get-tuple-element.94.dy.refs_0_, ...), custom_call_target="tpu_custom_call" | custom-call | flops 4294967296 | bytes 10485760 | tf_op jit(solution)/shard_map/pallas_call | solution.py:37
  174.8 9.1 %shard_map.247 = (bf16[512,1024]{1,0:T(8,128)(2,1)}, bf16[512,1024]{1,0:T(8,128)(2,1)S(1)}) custom-call(s32[3]{0:T(128)S(1)} %pad_add_fusion.sc, bf16[1024,1024]{1,0:T(8,128)(2,1)S(1)} %copy-done.39, bf16[1024,1024]{1,0:T(8,128)(2,1)} %get-tuple-element.111.a1, bf16[1024,1024]{1,0:T(8,128)(2,1)} %get-tuple-element.112.refs_0_, ...), custom_call_target="tpu_custom_call" | custom-call | flops 4294967296 | bytes 10485760 | tf_op jit(solution)/shard_map/pallas_call | solution.py:37
  187.0 5.2 %shard_map.232 = (bf16[2,1024,256]{2,1,0:T(8,128)(2,1)S(1)}, bf16[2,1024,256]{2,1,0:T(8,128)(2,1)S(1)}) custom-call(s32[3]{0:T(128)S(1)} %pad_add_fusion.sc, bf16[1024,1024]{1,0:T(8,128)(2,1)S(1)} %copy-done.28, bf16[1024,1024]{1,0:T(8,128)(2,1)} %refs_1_.3), custom_call_target="tpu_custom_call" | custom-call | flops 2147483648 | bytes 6291456 | tf_op jit(solution)/shard_map/pallas_call | solution.py:37
  194.4 5.9 %shard_map.236 = (bf16[2,1024,256]{2,1,0:T(8,128)(2,1)}, bf16[2,1024,256]{2,1,0:T(8,128)(2,1)S(1)}) custom-call(s32[3]{0:T(128)S(1)} %pad_add_fusion.sc, bf16[1024,1024]{1,0:T(8,128)(2,1)S(1)} %copy-done.30, bf16[1024,1024]{1,0:T(8,128)(2,1)} %refs_1_.3), custom_call_target="tpu_custom_call" | custom-call | flops 2147483648 | bytes 6291456 | tf_op jit(solution)/shard_map/pallas_call | solution.py:37
  224.1 6.3 %collective-permute-done.29.p2 = bf16[256,1024]{1,0:T(8,128)(2,1)S(1)} collective-permute-done((bf16[256,1024]{1,0:T(8,128)(2,1)}, bf16[256,1024]{1,0:T(8,128)(2,1)S(1)}, u32[]{:S(2)}, u32[]{:S(2)}) %collective-permute-start.29) | collective-permute-done | bytes 524320 | tf_op jit(solution)/shard_map/ppermute | solution.py:572
  241.8 11.2 %collective-permute-done.27 = bf16[1024,256]{1,0:T(8,128)(2,1)} collective-permute-done((bf16[1024,256]{1,0:T(8,128)(2,1)S(1)}, bf16[1024,256]{1,0:T(8,128)(2,1)}, u32[]{:S(2)}, u32[]{:S(2)}) %collective-permute-start.27) | collective-permute-done | bytes 524320 | tf_op jit(solution)/shard_map/ppermute | solution.py:572
  269.0 7.2 %collective-permute-done.60 = bf16[128,1024]{1,0:T(8,128)(2,1)S(1)} collective-permute-done((bf16[128,1024]{1,0:T(8,128)(2,1)S(1)}, bf16[128,1024]{1,0:T(8,128)(2,1)S(1)}, u32[]{:S(2)}, u32[]{:S(2)}) %collective-permute-start.60) | collective-permute-done | bytes 262176 | tf_op jit(solution)/shard_map/ppermute | solution.py:515
  286.2 13.8 %shard_map.241 = (bf16[1024,256]{1,0:T(8,128)(2,1)S(1)}, bf16[1024,256]{1,0:T(8,128)(2,1)S(1)}, bf16[1024,256]{1,0:T(8,128)(2,1)S(1)}, bf16[1024,1024]{1,0:T(8,128)(2,1)}) custom-call(s32[3]{0:T(128)S(1)} %pad_add_fusion.sc, bf16[256,1024]{1,0:T(8,128)(2,1)S(1)} %get-tuple-element.95.z0, bf16[256,1024]{1,0:T(8,128)(2,1)S(1)} %collective-permute-done.39.z1, ...), custom_call_target="tpu_custom_call" | custom-call | flops 5905580032 | bytes 11018240 | tf_op jit(solution)/shard_map/pallas_call | solution.py:37
  300.8 13.9 %shard_map.238 = (bf16[1024,256]{1,0:T(8,128)(2,1)S(1)}, bf16[1024,256]{1,0:T(8,128)(2,1)S(1)}, bf16[1024,256]{1,0:T(8,128)(2,1)S(1)}, bf16[1024,1024]{1,0:T(8,128)(2,1)}) custom-call(s32[3]{0:T(128)S(1)} %pad_add_fusion.sc, bf16[256,1024]{1,0:T(8,128)(2,1)S(1)} %get-tuple-element.83.z0, bf16[256,1024]{1,0:T(8,128)(2,1)S(1)} %collective-permute-done.30.z1, ...), custom_call_target="tpu_custom_call" | custom-call | flops 5905580032 | bytes 11018240 | tf_op jit(solution)/shard_map/pallas_call | solution.py:37
  331.0 9.6 %shard_map.243 = (bf16[512,768]{1,0:T(8,128)(2,1)}, bf16[512,768]{1,0:T(8,128)(2,1)S(1)}) custom-call(s32[3]{0:T(128)S(1)} %pad_add_fusion.sc, bf16[1024,1024]{1,0:T(8,128)(2,1)} %get-tuple-element.104.a0, bf16[1024,1024]{1,0:T(8,128)(2,1)} %get-tuple-element.105.a1, bf16[1024,256]{1,0:T(8,128)(2,1)S(1)} %copy-done.34, bf16[1024,256]{1,0:T(8,128)(2,1)S(1)} %copy-done.36, ...), custom_call_target="tpu_custom_call" | custom-call | flops 3221225472 | bytes 8912896 | tf_op jit(solution)/shard_map/pallas_call | solution.py:37
  356.1 13.8 %collective-permute-done.56 = bf16[64,1024]{1,0:T(8,128)(2,1)S(1)} collective-permute-done((bf16[64,1024]{1,0:T(8,128)(2,1)S(1)}, bf16[64,1024]{1,0:T(8,128)(2,1)S(1)}, u32[]{:S(2)}, u32[]{:S(2)}) %collective-permute-start.56) | collective-permute-done | bytes 131104 | tf_op jit(solution)/shard_map/ppermute | solution.py:515
  374.5 26.4 %collective-permute-done.57.second = bf16[128,1024]{1,0:T(8,128)(2,1)S(1)} collective-permute-done((bf16[128,1024]{1,0:T(8,128)(2,1)S(1)}, bf16[128,1024]{1,0:T(8,128)(2,1)S(1)}, u32[]{:S(2)}, u32[]{:S(2)}) %collective-permute-start.57) | collective-permute-done | bytes 262176 | tf_op jit(solution)/shard_map/ppermute | solution.py:515
  418.0 8.5 %collective-permute-done.48 = bf16[128,768]{1,0:T(8,128)(2,1)S(1)} collective-permute-done((bf16[128,768]{1,0:T(8,128)(2,1)S(1)}, bf16[128,768]{1,0:T(8,128)(2,1)S(1)}, u32[]{:S(2)}, u32[]{:S(2)}) %collective-permute-start.48) | collective-permute-done | bytes 196640 | tf_op jit(solution)/shard_map/ppermute | solution.py:515
  428.2 6.9 %collective-permute-done.49 = bf16[128,768]{1,0:T(8,128)(2,1)S(1)} collective-permute-done((bf16[128,768]{1,0:T(8,128)(2,1)S(1)}, bf16[128,768]{1,0:T(8,128)(2,1)S(1)}, u32[]{:S(2)}, u32[]{:S(2)}) %collective-permute-start.49) | collective-permute-done | bytes 196640 | tf_op jit(solution)/shard_map/ppermute | solution.py:515
  452.2 11.9 %collective-permute-done.51.second = bf16[512,768]{1,0:T(8,128)(2,1)S(1)} collective-permute-done((bf16[512,768]{1,0:T(8,128)(2,1)S(1)}, bf16[512,768]{1,0:T(8,128)(2,1)S(1)}, u32[]{:S(2)}, u32[]{:S(2)}) %collective-permute-start.51) | collective-permute-done | bytes 786464 | tf_op jit(solution)/shard_map/ppermute | solution.py:515
  (359 shorter events, 201.0 us)
Async XLA Ops:
  13.2 39.3 %collective-permute-start.18 = (bf16[1024,256]{1,0:T(8,128)(2,1)S(1)}, bf16[1024,256]{1,0:T(8,128)(2,1)}, u32[]{:S(2)}, u32[]{:S(2)}) collective-permute-start(bf16[1024,256]{1,0:T(8,128)(2,1)S(1)} %get-tuple-element.157.x0), channel_id=1, source_target_pairs={{0,2},{1,3},{2,0},{3,1},{4,6},{5,7},{6,4},{7,5},{8,10},{9,11},{10,... | collective-permute-start | bytes 1572872 | tf_op jit(solution)/shard_map/ppermute | solution.py:572
  13.3 39.9 %collective-permute-start = (bf16[1024,256]{1,0:T(8,128)(2,1)S(1)}, bf16[1024,256]{1,0:T(8,128)(2,1)}, u32[]{:S(2)}, u32[]{:S(2)}) collective-permute-start(bf16[1024,256]{1,0:T(8,128)(2,1)S(1)} %fusion.17.x0), channel_id=1, source_target_pairs={{0,1},{1,0},{2,3},{3,2},{4,5},{5,4},{6,7},{7,6},{8,9},{9,8},{10,11... | collective-permute-start | bytes 1572872 | tf_op jit(solution)/shard_map/ppermute | solution.py:569
  53.3 31.1 %collective-permute-start.9 = (bf16[1024,256]{1,0:T(8,128)(2,1)}, bf16[1024,256]{1,0:T(8,128)(2,1)S(1)}, u32[]{:S(2)}, u32[]{:S(2)}) collective-permute-start(bf16[1024,256]{1,0:T(8,128)(2,1)} %get-tuple-element.156.d0), channel_id=1, source_target_pairs={{0,1},{1,0},{2,3},{3,2},{4,5},{5,4},{6,7},{7,6},{8,9},{9,8},{10,11... | collective-permute-start | bytes 1572872 | tf_op jit(solution)/shard_map/ppermute | solution.py:569
  53.8 30.6 %collective-permute-start.13 = (bf16[256,1024]{1,0:T(8,128)(2,1)}, bf16[256,1024]{1,0:T(8,128)(2,1)}, u32[]{:S(2)}, u32[]{:S(2)}) collective-permute-start(bf16[256,1024]{1,0:T(8,128)(2,1)} %w0.3), channel_id=1, source_target_pairs={{0,2},{1,3},{2,0},{3,1},{4,6},{5,7},{6,4},{7,5},{8,10},{9,11},{10,... | collective-permute-start | bytes 1572872 | tf_op jit(solution)/shard_map/ppermute | solution.py:572
  101.5 35.9 %collective-permute-start.23 = (bf16[1024,256]{1,0:T(8,128)(2,1)}, bf16[1024,256]{1,0:T(8,128)(2,1)S(1)}, u32[]{:S(2)}, u32[]{:S(2)}) collective-permute-start(bf16[1024,256]{1,0:T(8,128)(2,1)} %get-tuple-element.155.d0), channel_id=1, source_target_pairs={{0,1},{1,0},{2,3},{3,2},{4,5},{5,4},{6,7},{7,6},{8,9},{9,8},{10,11... | collective-permute-start | bytes 1572872 | tf_op jit(solution)/shard_map/ppermute | solution.py:569
  102.1 35.4 %collective-permute-start.25 = (bf16[1024,256]{1,0:T(8,128)(2,1)}, bf16[1024,256]{1,0:T(8,128)(2,1)S(1)}, u32[]{:S(2)}, u32[]{:S(2)}) collective-permute-start(bf16[1024,256]{1,0:T(8,128)(2,1)} %copy-done.19), channel_id=1, source_target_pairs={{0,1},{1,0},{2,3},{3,2},{4,5},{5,4},{6,7},{7,6},{8,9},{9,8},{10,11... | collective-permute-start | bytes 1572872 | tf_op jit(solution)/shard_map/ppermute | solution.py:569
  102.2 35.3 %collective-permute-start.20 = (bf16[1024,256]{1,0:T(8,128)(2,1)}, bf16[1024,256]{1,0:T(8,128)(2,1)S(1)}, u32[]{:S(2)}, u32[]{:S(2)}) collective-permute-start(bf16[1024,256]{1,0:T(8,128)(2,1)} %get-tuple-element.75.o0.a0), channel_id=1, source_target_pairs={{0,1},{1,0},{2,3},{3,2},{4,5},{5,4},{6,7},{7,6},{8,9},{9,8},{10,11... | collective-permute-start | bytes 1572872 | tf_op jit(solution)/shard_map/ppermute | solution.py:569
  174.3 29.4 %collective-permute-start.37 = (bf16[2,256,1024]{2,1,0:T(8,128)(2,1)}, bf16[2,256,1024]{2,1,0:T(8,128)(2,1)S(1)}, u32[]{:S(2)}, u32[]{:S(2)}) collective-permute-start(bf16[2,256,1024]{2,1,0:T(8,128)(2,1)} %get-tuple-element.93), channel_id=1, source_target_pairs={{0,1},{1,0},{2,3},{3,2},{4,5},{5,4},{6,7},{7,6},{8,9},{9,8},{10,11... | collective-permute-start | bytes 3145736 | tf_op jit(solution)/shard_map/ppermute | solution.py:569
  174.5 29.8 %collective-permute-start.28 = (bf16[2,256,1024]{2,1,0:T(8,128)(2,1)}, bf16[2,256,1024]{2,1,0:T(8,128)(2,1)S(1)}, u32[]{:S(2)}, u32[]{:S(2)}) collective-permute-start(bf16[2,256,1024]{2,1,0:T(8,128)(2,1)} %get-tuple-element.81), channel_id=1, source_target_pairs={{0,1},{1,0},{2,3},{3,2},{4,5},{5,4},{6,7},{7,6},{8,9},{9,8},{10,11... | collective-permute-start | bytes 3145736 | tf_op jit(solution)/shard_map/ppermute | solution.py:569
  203.7 31.2 %collective-permute-start.70 = (bf16[256,1024]{1,0:T(8,128)(2,1)}, bf16[256,1024]{1,0:T(8,128)(2,1)}, u32[]{:S(2)}, u32[]{:S(2)}) collective-permute-start(bf16[256,1024]{1,0:T(8,128)(2,1)} %get-tuple-element.146), channel_id=1, source_target_pairs={{0,8},{4,12},{8,0},{12,4},{16,24},{20,28},{24,16},{28,20},{1,9},{5... | collective-permute-start | bytes 1572872 | tf_op jit(solution)/shard_map/ppermute | solution.py:515
  219.2 33.8 %collective-permute-start.27 = (bf16[1024,256]{1,0:T(8,128)(2,1)S(1)}, bf16[1024,256]{1,0:T(8,128)(2,1)}, u32[]{:S(2)}, u32[]{:S(2)}) collective-permute-start(bf16[1024,256]{1,0:T(8,128)(2,1)S(1)} %fusion.11), channel_id=1, source_target_pairs={{0,2},{1,3},{2,0},{3,1},{4,6},{5,7},{6,4},{7,5},{8,10},{9,11},{10,... | collective-permute-start | bytes 1572872 | tf_op jit(solution)/shard_map/ppermute | solution.py:572
  230.5 33.7 %collective-permute-start.40 = (bf16[256,1024]{1,0:T(8,128)(2,1)S(1)}, bf16[256,1024]{1,0:T(8,128)(2,1)S(1)}, u32[]{:S(2)}, u32[]{:S(2)}) collective-permute-start(bf16[256,1024]{1,0:T(8,128)(2,1)S(1)} %get-tuple-element.95.z0), channel_id=1, source_target_pairs={{0,2},{1,3},{2,0},{3,1},{4,6},{5,7},{6,4},{7,5},{8,10},{9,11},{10,... | collective-permute-start | bytes 1572872 | tf_op jit(solution)/shard_map/ppermute | solution.py:572
  234.9 47.1 %collective-permute-start.39 = (bf16[256,1024]{1,0:T(8,128)(2,1)S(1)}, bf16[256,1024]{1,0:T(8,128)(2,1)S(1)}, u32[]{:S(2)}, u32[]{:S(2)}) collective-permute-start(bf16[256,1024]{1,0:T(8,128)(2,1)S(1)} %get-tuple-element.95.z0), channel_id=1, source_target_pairs={{0,1},{1,0},{2,3},{3,2},{4,5},{5,4},{6,7},{7,6},{8,9},{9,8},{10,11... | collective-permute-start | bytes 1572872 | tf_op jit(solution)/shard_map/ppermute | solution.py:569
  280.7 73.3 %collective-permute-start.65 = (f32[2,1024]{1,0:T(2,128)S(1)}, f32[2,1024]{1,0:T(2,128)S(1)}, u32[]{:S(2)}, u32[]{:S(2)}) collective-permute-start(f32[2,1024]{1,0:T(2,128)S(1)} %add.365), channel_id=1, source_target_pairs={{0,2},{1,3},{2,0},{3,1},{4,6},{5,7},{6,4},{7,5},{8,10},{9,11},{10,... | collective-permute-start | bytes 24584 | tf_op jit(solution)/shard_map/ppermute | solution.py:572
  282.0 37.8 %collective-permute-start.61 = (bf16[128,1024]{1,0:T(8,128)(2,1)S(1)}, bf16[128,1024]{1,0:T(8,128)(2,1)S(1)}, u32[]{:S(2)}, u32[]{:S(2)}) collective-permute-start(bf16[128,1024]{1,0:T(8,128)(2,1)S(1)} %add_convert_fusion.11), channel_id=1, source_target_pairs={{0,16},{4,20},{8,24},{12,28},{16,0},{20,4},{24,8},{28,12},{1,17},{... | collective-permute-start | bytes 786440 | tf_op jit(solution)/shard_map/ppermute | solution.py:515
  282.1 65.8 %collective-permute-start.73 = (bf16[256,1024]{1,0:T(8,128)(2,1)}, bf16[256,1024]{1,0:T(8,128)(2,1)}, u32[]{:S(2)}, u32[]{:S(2)}) collective-permute-start(bf16[256,1024]{1,0:T(8,128)(2,1)} %pad_maximum_fusion.4), channel_id=1, source_target_pairs={{0,8},{4,12},{8,0},{12,4},{16,24},{20,28},{24,16},{28,20},{1,9},{5... | collective-permute-start | bytes 1572872 | tf_op jit(solution)/shard_map/ppermute | solution.py:515
  319.9 34.0 %collective-permute-start.62 = (bf16[256,1024]{1,0:T(8,128)(2,1)S(1)}, bf16[256,1024]{1,0:T(8,128)(2,1)S(1)}, u32[]{:S(2)}, u32[]{:S(2)}) collective-permute-start(bf16[256,1024]{1,0:T(8,128)(2,1)S(1)} %pad_maximum_fusion.3), channel_id=1, source_target_pairs={{0,4},{4,0},{8,12},{12,8},{16,20},{20,16},{24,28},{28,24},{1,5},{5... | collective-permute-start | bytes 1572872 | tf_op jit(solution)/shard_map/ppermute | solution.py:515
  324.0 49.0 %collective-permute-start.42 = (bf16[2,1024,256]{2,1,0:T(8,128)(2,1)S(1)}, bf16[2,1024,256]{2,1,0:T(8,128)(2,1)S(1)}, u32[]{:S(2)}, u32[]{:S(2)}) collective-permute-start(bf16[2,1024,256]{2,1,0:T(8,128)(2,1)S(1)} %get-tuple-element.103), channel_id=1, source_target_pairs={{0,1},{1,0},{2,3},{3,2},{4,5},{5,4},{6,7},{7,6},{8,9},{9,8},{10,11... | collective-permute-start | bytes 3145736 | tf_op jit(solution)/shard_map/ppermute | solution.py:569
  353.8 51.8 %collective-permute-start.33 = (bf16[2,1024,256]{2,1,0:T(8,128)(2,1)}, bf16[2,1024,256]{2,1,0:T(8,128)(2,1)S(1)}, u32[]{:S(2)}, u32[]{:S(2)}) collective-permute-start(bf16[2,1024,256]{2,1,0:T(8,128)(2,1)} %get-tuple-element.91), channel_id=1, source_target_pairs={{0,1},{1,0},{2,3},{3,2},{4,5},{5,4},{6,7},{7,6},{8,9},{9,8},{10,11... | collective-permute-start | bytes 3145736 | tf_op jit(solution)/shard_map/ppermute | solution.py:569
  354.0 56.4 %collective-permute-start.74 = (bf16[512,1024]{1,0:T(8,128)(2,1)S(1)}, bf16[512,1024]{1,0:T(8,128)(2,1)S(1)}, u32[]{:S(2)}, u32[]{:S(2)}) collective-permute-start(bf16[512,1024]{1,0:T(8,128)(2,1)S(1)} %pad_maximum_fusion.1.first), channel_id=1, source_target_pairs={{0,4},{4,0},{8,12},{12,8},{16,20},{20,16},{24,28},{28,24},{1,5},{5... | collective-permute-start | bytes 3145736 | tf_op jit(solution)/shard_map/ppermute | solution.py:515
  369.9 36.5 %collective-permute-start.63 = (bf16[512,1024]{1,0:T(8,128)(2,1)S(1)}, bf16[512,1024]{1,0:T(8,128)(2,1)S(1)}, u32[]{:S(2)}, u32[]{:S(2)}) collective-permute-start(bf16[512,1024]{1,0:T(8,128)(2,1)S(1)} %pad_maximum_fusion.first), channel_id=1, source_target_pairs={{0,8},{4,12},{8,0},{12,4},{16,24},{20,28},{24,16},{28,20},{1,9},{5... | collective-permute-start | bytes 3145736 | tf_op jit(solution)/shard_map/ppermute | solution.py:515
  371.2 29.6 %collective-permute-start.57 = (bf16[128,1024]{1,0:T(8,128)(2,1)S(1)}, bf16[128,1024]{1,0:T(8,128)(2,1)S(1)}, u32[]{:S(2)}, u32[]{:S(2)}) collective-permute-start(bf16[128,1024]{1,0:T(8,128)(2,1)S(1)} %pad_maximum_fusion.6.first), channel_id=1, source_target_pairs={{0,8},{4,12},{8,0},{12,4},{16,24},{20,28},{24,16},{28,20},{1,9},{5... | collective-permute-start | bytes 786440 | tf_op jit(solution)/shard_map/ppermute | solution.py:515
  373.0 41.5 %collective-permute-start.47 = (bf16[256,768]{1,0:T(8,128)(2,1)}, bf16[256,768]{1,0:T(8,128)(2,1)S(1)}, u32[]{:S(2)}, u32[]{:S(2)}) collective-permute-start(bf16[256,768]{1,0:T(8,128)(2,1)} %get-tuple-element.150), channel_id=1, source_target_pairs={{0,8},{4,12},{8,0},{12,4},{16,24},{20,28},{24,16},{28,20},{1,9},{5... | collective-permute-start | bytes 1179656 | tf_op jit(solution)/shard_map/ppermute | solution.py:515
  405.8 30.4 %collective-permute-start.34 = (bf16[1024,256]{1,0:T(8,128)(2,1)S(1)}, bf16[1024,256]{1,0:T(8,128)(2,1)S(1)}, u32[]{:S(2)}, u32[]{:S(2)}) collective-permute-start(bf16[1024,256]{1,0:T(8,128)(2,1)S(1)} %fusion.13), channel_id=1, source_target_pairs={{0,2},{1,3},{2,0},{3,1},{4,6},{5,7},{6,4},{7,5},{8,10},{9,11},{10,... | collective-permute-start | bytes 1572872 | tf_op jit(solution)/shard_map/ppermute | solution.py:572
  (116 other events, 1553.0 us)

commit v2 on v1

v2 whole, which is shorter than its diff:
```python
import functools

import jax
import jax.numpy as jnp
from jax import lax
from jax.experimental import pallas as pl
from jax.experimental.pallas import tpu as pltpu
from jax.sharding import PartitionSpec as P

DH = 128
TILE = 256
EPS_NORM = 1e-05
NEG_FILL = -1e30
F32 = jnp.float32
BF16 = jnp.bfloat16
MIB = 1024 * 1024
COST = 1.0
GELU_C = 0.7978845608028654


def dot_nn(a, b):
    return jnp.dot(a, b, preferred_element_type=F32)


def dot_nt(a, b):
    return lax.dot_general(a, b, (((1,), (1,)), ((), ())), preferred_element_type=F32)


def dot_tn(a, b):
    return lax.dot_general(a, b, (((0,), (0,)), ((), ())), preferred_element_type=F32)


def call(body, grid, in_specs, out_specs, out_shape, scalars, operands, scratch=(), flops=0, vmem=24, hbm=()):
    bytes_moved = sum(o.size * o.dtype.itemsize for o in operands)
    bytes_moved += sum(
        o.size * jnp.dtype(o.dtype).itemsize for o in jax.tree_util.tree_leaves(out_shape)
    )
    operands = [
        pltpu.with_memory_space_constraint(o, pltpu.HBM) if i in hbm else o
        for i, o in enumerate(operands)
    ]
    return pl.pallas_call(
        body,
        grid_spec=pltpu.PrefetchScalarGridSpec(
            num_scalar_prefetch=1,
            grid=grid,
            in_specs=in_specs,
            out_specs=out_specs,
            scratch_shapes=list(scratch),
        ),
        out_shape=out_shape,
        compiler_params=pltpu.CompilerParams(
            vmem_limit_bytes=vmem * MIB,
            dimension_semantics=("arbitrary",) * len(grid),
        ),
        cost_estimate=pl.CostEstimate(
            flops=int(flops * COST), bytes_accessed=int(bytes_moved * COST), transcendentals=0
        ),
    )(scalars, *operands)


def full(shape):
    zeros = (0,) * len(shape)
    return pl.BlockSpec(shape, lambda *_: zeros, pipeline_mode=pl.Buffered(1))


def shape_of(shape, dtype):
    return jax.ShapeDtypeStruct(shape, dtype)


def far_first(i, n, sc):
    c = jnp.bitwise_and(sc[0], 1)
    return jnp.where(i < n // 2, (1 - c) * (n // 2) + i, c * (n // 2) + i - n // 2)


def first_body(
    masked, tile, sc, x0, x1, x2, x3, dy_other, dy_mine, gains, weight,
    qkv, acts, stats, o, lse, other, mine, q_all, k_all, v_all,
):
    t = sc[0]
    i = pl.program_id(0)
    n = pl.num_programs(0) // 2

    @pl.when(i == 0)
    def _():
        rows = dy_mine.shape[0]
        other[rows:, :] = dy_other[...]
        mine[rows:, :] = dy_mine[...]

    @pl.when(i < n)
    def _():
        pieces = [x[...].astype(F32) for x in (x0, x1, x2, x3)]
        width = pieces[0].shape[1]
        count = width * len(pieces)
        mean = sum(jnp.sum(x, axis=1, keepdims=True) for x in pieces) / count
        centered = [x - mean for x in pieces]
        var = sum(jnp.sum(c * c, axis=1, keepdims=True) for c in centered) / count
        rstd = lax.rsqrt(var + EPS_NORM)
        total = [0.0, 0.0, 0.0]
        for k, c in enumerate(centered):
            j = jnp.bitwise_xor(t, k)
            part = (c * rstd * gains[k, 0:1, :] + gains[k, 1:2, :]).astype(BF16)
            acts[:, pl.ds(pl.multiple_of(j * width, width), width)] = part
            for s in range(3):
                total[s] = total[s] + dot_nn(part, weight[s, j])
        rows = pl.ds(pl.multiple_of(i * tile, tile), tile)
        for s, (value, kept) in enumerate(zip(total, (q_all, k_all, v_all))):
            low = (value * (DH ** (-0.5)) if s == 0 else value).astype(BF16)
            qkv[s] = low
            kept[rows, :] = low
        stats[:, 0:1] = mean
        stats[:, 1:2] = rstd

    @pl.when(i >= n)
    def _():
        cols = k_all.shape[0]
        first = far_first(i - n, n, sc) * tile
        rows = pl.ds(pl.multiple_of(first, tile), tile)
        if masked:
            q_side = (first + lax.broadcasted_iota(jnp.int32, (tile, 1), 0)) < sc[1]
            k_side = lax.broadcasted_iota(jnp.int32, (1, cols), 1) < sc[1]
            apart = jnp.logical_xor(q_side, k_side)
        for h in range(q_all.shape[1] // DH):
            part = slice(h * DH, (h + 1) * DH)
            scores = dot_nt(q_all[rows, part], k_all[:, part])
            if masked:
                scores = jnp.where(apart, NEG_FILL, scores)
            top = jnp.max(scores, axis=1, keepdims=True)
            weights = jnp.exp(scores - top)
            total = jnp.sum(weights, axis=1, keepdims=True)
            mixed = dot_nn(weights.astype(BF16), v_all[:, part])
            low = (mixed / total).astype(BF16)
            o[:, part] = low
            to = lax.rem(i, n // 2) * tile
            to = pl.ds(pl.multiple_of(to, tile), tile)

            @pl.when(i < n + n // 2)
            def _():
                other[to, part] = low

            @pl.when(i >= n + n // 2)
            def _():
                mine[to, part] = low

            stat = jnp.broadcast_to(top + jnp.log(total), (tile, DH))
            lse[h] = jnp.transpose(stat)[0:1, :]


def first_layer(scalars, pieces, dy, gains, weight4, h):
    rows, width = pieces[0].shape
    n = len(pieces)
    heads = width // DH
    tile = 256
    steps = rows // tile

    def early(i, sc):
        return (jnp.minimum(i, steps - 1), 0)

    def late(i, sc):
        return far_first(jnp.maximum(i - steps, 0), steps, sc)

    def rows_of(mine):
        def index(i, sc):
            c = jnp.bitwise_and(sc[0], 1)
            return (2 * h + (c if mine else 1 - c), 0)

        return pl.BlockSpec((rows // 2, width), index, pipeline_mode=pl.Buffered(1))

    whole = pl.BlockSpec((rows, width), lambda i, sc: (0, 0))

    return call(
        functools.partial(first_body, h == 1, tile),
        (2 * steps,),
        [pl.BlockSpec((tile, width), early)] * n
        + [rows_of(False), rows_of(True), full(gains.shape), full(weight4.shape)],
        [
            pl.BlockSpec((3, tile, width), lambda i, sc: (0, jnp.minimum(i, steps - 1), 0)),
            pl.BlockSpec((tile, n * width), early),
            pl.BlockSpec((tile, 2), early),
            pl.BlockSpec((tile, width), lambda i, sc: (late(i, sc), 0)),
            pl.BlockSpec((heads, 1, tile), lambda i, sc: (0, 0, late(i, sc))),
            whole,
            whole,
        ],
        [
            shape_of((3, rows, width), BF16),
            shape_of((rows, n * width), BF16),
            shape_of((rows, 2), F32),
            shape_of((rows, width), BF16),
            shape_of((heads, 1, rows), F32),
            shape_of((rows, width), BF16),
            shape_of((rows, width), BF16),
        ],
        scalars,
        [*pieces, dy, dy, gains, weight4],
        scratch=[pltpu.VMEM((rows, width), BF16)] * 3,
        flops=2 * rows * n * width * 3 * width + 4 * rows * rows * width,
    )


def quarter(u):
    return 2 * jnp.bitwise_and(u, 1) + jnp.right_shift(u, 1)


def feed_body(
    sc, x0, x1, x2, x3, p0, p1, p2, p3, ow, gains, up, down, bias,
    y_cols, y_rows, dy_rows, b_out, dy_out, g_out, du_out, send, keep, bias_grad, y_acc, total,
):
    t = sc[0]
    i = pl.program_id(0)
    side = jnp.right_shift(t, 1)
    xs, ps = (x0, x1, x2, x3), (p0, p1, p2, p3)
    rows, width = x0.shape
    n = len(xs)
    count = n * width

    @pl.when(i == 0)
    def _():
        def block(k):
            j = jnp.bitwise_xor(t, k)
            return pl.ds(pl.multiple_of(j * width, width), width)

        for k in range(n):
            y_acc[:, block(k)] = xs[k][...].astype(F32)
            dy_out[:, block(k)] = ps[k][rows:, :]
        y = y_acc[...]
        for k in range(n):
            y = y + dot_nn(ps[k][:rows, :], ow[block(k), :])
        y_acc[...] = y
        mean = jnp.sum(y, axis=1, keepdims=True) / count
        centered = y - mean
        rstd = lax.rsqrt(jnp.sum(centered * centered, axis=1, keepdims=True) / count + EPS_NORM)
        b_out[...] = (centered * rstd * gains[2:3, :] + gains[3:4, :]).astype(BF16)
        total[...] = jnp.zeros_like(total)
        wide = y_cols.shape[1]
        y_cols[...] = y_acc[:, pl.ds(pl.multiple_of(side * wide, wide), wide)]
        part = y_rows.shape[0]
        mine = pl.ds(pl.multiple_of(side * part, part), part)
        y_rows[...] = y_acc[mine, :]
        dy_rows[...] = dy_out[mine, :]

    u = dot_nn(b_out[...], up[...]) + bias[...]
    dh = dot_nt(dy_out[...], down[...])
    square = u * u
    half = 0.5 + 0.5 * jnp.tanh(u * (GELU_C + (GELU_C * 0.044715) * square))
    g_out[...] = (u * half).astype(BF16)
    inner = u * (2 * GELU_C + (6 * 0.044715 * GELU_C) * square)
    du = (dh * (half + (half - half * half) * inner)).astype(BF16)
    du_out[...] = du
    bias_grad[...] = jnp.sum(du.astype(F32), axis=0, keepdims=True)
    total[...] += dot_nt(du, up[...])

    @pl.when(i == pl.num_programs(0) - 1)
    def _():
        part = send.shape[0]
        for out, at in ((send, 1 - side), (keep, side)):
            out[...] = total[pl.ds(pl.multiple_of(at * part, part), part), :].astype(BF16)


def feed(scalars, xs, pieces, ow, gains, up, down, bias):
    rows, width = xs[0].shape
    n = len(xs)
    count = n * width
    hidden = up.shape[1]
    half = rows // 2
    part = half // 2
    step = 512

    def mine(i, sc):
        return (jnp.bitwise_and(sc[0], 1), 0)

    def fixed(i, sc):
        return (0, 0)

    def along(i, sc):
        return (0, i)

    return call(
        feed_body,
        (hidden // step,),
        [pl.BlockSpec((half, width), mine, pipeline_mode=pl.Buffered(1))] * n
        + [full(p.shape) for p in pieces]
        + [full(ow.shape), full(gains.shape)]
        + [
            pl.BlockSpec((count, step), along),
            pl.BlockSpec((step, count), lambda i, sc: (i, 0)),
            pl.BlockSpec((1, step), along),
        ],
        [
            pl.BlockSpec((half, count // 2), fixed),
            pl.BlockSpec((part, count), fixed),
            pl.BlockSpec((part, count), fixed),
            pl.BlockSpec((half, count), fixed),
            pl.BlockSpec((half, count), fixed),
            pl.BlockSpec((half, step), along),
            pl.BlockSpec((half, step), along),
            pl.BlockSpec((part, count), fixed),
            pl.BlockSpec((part, count), fixed),
            pl.BlockSpec((1, step), along),
        ],
        [
            shape_of((half, count // 2), F32),
            shape_of((part, count), F32),
            shape_of((part, count), BF16),
            shape_of((half, count), BF16),
            shape_of((half, count), BF16),
            shape_of((half, hidden), BF16),
            shape_of((half, hidden), BF16),
            shape_of((part, count), BF16),
            shape_of((part, count), BF16),
            shape_of((1, hidden), F32),
        ],
        scalars,
        [*xs, *pieces, ow, gains, up, down, bias],
        scratch=[pltpu.VMEM((half, count), F32), pltpu.VMEM((half, count), F32)],
        flops=2 * half * count * (count + 3 * hidden),
        vmem=32,
    )


def norm_back_body(sc, p0, p1, y, dy, gains, dz, sums):
    db = p0[...].astype(F32) + p1[...].astype(F32)
    yv = y[...]
    count = yv.shape[1]
    mean = jnp.sum(yv, axis=1, keepdims=True) / count
    centered = yv - mean
    rstd = lax.rsqrt(jnp.sum(centered * centered, axis=1, keepdims=True) / count + EPS_NORM)
    nhat = centered * rstd
    n = db * gains[2:3, :]
    first = jnp.sum(n, axis=1, keepdims=True) / count
    second = jnp.sum(n * nhat, axis=1, keepdims=True) / count
    dz[...] = (dy[...].astype(F32) + rstd * (n - first - nhat * second)).astype(BF16)
    sums[0:1, :] = jnp.sum(db * nhat, axis=0, keepdims=True)
    sums[1:2, :] = jnp.sum(db, axis=0, keepdims=True)


def norm_back(scalars, keep, got_x, y, dy, gains):
    rows, count = got_x.shape
    return call(
        norm_back_body,
        (1,),
        [full(v.shape) for v in (keep, got_x, y, dy, gains)],
        [
            pl.BlockSpec((rows, count), lambda i, sc: (0, 0)),
            pl.BlockSpec((2, count), lambda i, sc: (0, 0)),
        ],
        [shape_of((rows, count), BF16), shape_of((2, count), F32)],
        scalars,
        [keep, got_x, y, dy, gains],
    )


def attend_back_body(masked, sc, z0, z1, z2, z3, out_w, q, k, v, lse, grads, dz_out, dk_acc, dv_acc):
    i = pl.program_id(0)
    place = quarter(jnp.bitwise_xor(sc[0], i))

    @pl.when(i == 0)
    def _():
        dk_acc[...] = jnp.zeros_like(dk_acc)
        dv_acc[...] = jnp.zeros_like(dv_acc)

    for j, z in enumerate((z0, z1, z2, z3)):

        @pl.when(i == j)
        def _(z=z):
            dz_out[...] = z[...]

    d_mixed = dot_nt(dz_out[...], out_w[...]).astype(BF16)
    rows = d_mixed.shape[0]
    keys = k.shape[1]
    for h in range(d_mixed.shape[1] // DH):
        cols = slice(h * DH, (h + 1) * DH)
        q_h, k_h, v_h, do_h = q[0, :, cols], k[0, :, cols], v[0, :, cols], d_mixed[:, cols]
        scores = dot_nt(k_h, q_h)
        if masked:
            base = place * rows
            q_side = (base + lax.broadcasted_iota(jnp.int32, (1, rows), 1)) < sc[1]
            k_side = lax.broadcasted_iota(jnp.int32, (keys, 1), 0) < sc[1]
            scores = jnp.where(jnp.logical_xor(q_side, k_side), NEG_FILL, scores)
        p = jnp.exp(scores - lse[h])
        d_p = dot_nt(v_h, do_h)
        prod = p * d_p
        delta = jnp.sum(prod, axis=0, keepdims=True)
        d_s = (prod - p * delta).astype(BF16)
        dv_acc[:, cols] += dot_nn(p.astype(BF16), do_h)
        dk_acc[:, cols] += dot_nn(d_s, q_h)
        here = pl.ds(pl.multiple_of(place * rows, rows), rows)
        grads[here, cols] = dot_tn(d_s, k_h).astype(BF16)

    @pl.when(i == pl.num_programs(0) - 1)
    def _():
        width = dk_acc.shape[1]
        grads[:, width : 2 * width] = dk_acc[...].astype(BF16)
        grads[:, 2 * width :] = dv_acc[...].astype(BF16)


def attend_back(scalars, dzs, out_w, qkv, lse, masked):
    _, rows, width = qkv.shape
    heads = width // DH
    count = out_w.shape[1]
    tiles = rows // TILE

    def tile(i, sc):
        return (quarter(jnp.bitwise_xor(sc[0], i)), 0)

    return call(
        functools.partial(attend_back_body, masked),
        (tiles,),
        [full(dz.shape) for dz in dzs]
        + [
            full(out_w.shape),
            pl.BlockSpec((1, TILE, width), lambda i, sc: (0, tile(i, sc)[0], 0)),
            pl.BlockSpec((1, rows, width), lambda i, sc: (1, 0, 0)),
            pl.BlockSpec((1, rows, width), lambda i, sc: (2, 0, 0)),
            pl.BlockSpec((heads, 1, TILE), lambda i, sc: (0, 0, tile(i, sc)[0])),
        ],
        [
            pl.BlockSpec((rows, 3 * width), lambda i, sc: (0, 0)),
            pl.BlockSpec((TILE, count), tile),
        ],
        [shape_of((rows, 3 * width), BF16), shape_of((rows, count), BF16)],
        scalars,
        [*dzs, out_w, qkv, qkv, qkv, lse],
        scratch=[pltpu.VMEM((rows, width), F32), pltpu.VMEM((rows, width), F32)],
        flops=2 * rows * count * width + 10 * rows * rows * width,
    )


def relative(i):
    return jnp.where(i < 2, 2 * i + 1, 2 * i - 4)


def spread_body(scales, flipped, n_left, sc, *refs):
    lefts, right, send, keep = refs[:n_left], refs[n_left], refs[-2], refs[-1]
    i = pl.program_id(0)
    rows = lefts[0].shape[0]
    parts = []
    for left in lefts:
        if flipped:
            width = right.shape[2]
            total = None
            for s, scale in enumerate(scales):
                part = dot_nt(left[:, s * width : (s + 1) * width], right[s])
                part = part * scale if scale != 1.0 else part
                total = part if total is None else total + part
        else:
            total = dot_nn(left[...], right[...])
        parts.append(total.astype(BF16))

    def put(out):
        for at, part in enumerate(parts):
            out[0, at * rows : (at + 1) * rows, :] = part

    @pl.when(i < 2)
    def _():
        put(send)

    @pl.when(i >= 2)
    def _():
        put(keep)


def spread(scalars, lefts, right, n_tp, scales=None):
    flipped = scales is not None
    rows = sum(a.shape[0] for a in lefts)
    count = right.shape[1]
    width = count // n_tp

    def cols(i, sc):
        j = jnp.bitwise_xor(sc[0], relative(i))
        return (0, j, 0) if flipped else (0, j)

    block = (right.shape[0], width, right.shape[2]) if flipped else (right.shape[0], width)
    return call(
        functools.partial(spread_body, scales, flipped, len(lefts)),
        (n_tp,),
        [full(a.shape) for a in lefts] + [pl.BlockSpec(block, cols)],
        [
            pl.BlockSpec((1, rows, width), lambda i, sc: (jnp.minimum(i, 1), 0, 0)),
            pl.BlockSpec((1, rows, width), lambda i, sc: (jnp.maximum(i - 2, 0), 0, 0)),
        ],
        [shape_of((2, rows, width), BF16), shape_of((2, rows, width), BF16)],
        scalars,
        [*lefts, right],
        flops=2 * rows * lefts[0].shape[1] * count,
    )


def out_body(n_left, sc, *refs):
    lefts, right, send, keep = refs[:n_left], refs[n_left], refs[-2], refs[-1]
    i = pl.program_id(0)
    rows = lefts[0].shape[0]
    parts = [dot_nn(left[...], right[...]).astype(BF16) for left in lefts]
    for step, out in enumerate((send, keep)):

        @pl.when(i == step)
        def _(out=out):
            for at, part in enumerate(parts):
                out[at * rows : (at + 1) * rows, :] = part


def out_product(scalars, lefts, right):
    rows = sum(a.shape[0] for a in lefts)
    hidden, count = right.shape

    def cols(i, sc):
        side = jnp.right_shift(sc[0], 1)
        return (0, jnp.where(i == 0, 1 - side, side))

    return call(
        functools.partial(out_body, len(lefts)),
        (2,),
        [full(a.shape) for a in lefts] + [pl.BlockSpec((hidden, count // 2), cols)],
        [pl.BlockSpec((rows, count // 2), lambda i, sc: (0, 0))] * 2,
        [shape_of((rows, count // 2), BF16)] * 2,
        scalars,
        [*lefts, right],
        flops=2 * rows * hidden * count,
    )


def pair_grad_body(sc, a0, a1, b0, b1, send, keep):
    i = pl.program_id(0)
    low = (dot_tn(a0[...], b0[...]) + dot_tn(a1[...], b1[...])).astype(BF16)
    for step, out in enumerate((send, keep)):

        @pl.when(i == step)
        def _(out=out):
            out[...] = low


def pair_grad(scalars, lefts, rights, split_left):
    rows = lefts[0].shape[0]
    halved = lambda i, sc: (0, 1 - i)
    m = lefts[0].shape[1] // (2 if split_left else 1)
    count = rights[0].shape[1] // (1 if split_left else 2)
    left = pl.BlockSpec((rows, m), halved) if split_left else full((rows, m))
    right = full((rows, count)) if split_left else pl.BlockSpec((rows, count), halved)
    return call(
        pair_grad_body,
        (2,),
        [left, left, right, right],
        [pl.BlockSpec((m, count), lambda i, sc: (0, 0))] * 2,
        [shape_of((m, count), BF16)] * 2,
        scalars,
        [*lefts, *rights],
        flops=8 * rows * m * count,
        vmem=32,
    )


def norm_sums_body(sc, da, x, stats, gain, moments, sums):
    d = da[...].astype(F32)
    nhat = (x[...].astype(F32) - stats[:, 0:1]) * stats[:, 1:2]
    n = d * gain[...]
    prod = d * nhat
    rows = d.shape[0]
    for at, v in enumerate((n, n * nhat)):
        total = jnp.broadcast_to(jnp.sum(v, axis=1, keepdims=True), (rows, 128))
        moments[at : at + 1, :] = jnp.transpose(total)[0:1, :]
    sums[0:1, :] = jnp.sum(prod, axis=0, keepdims=True)
    sums[1:2, :] = jnp.sum(d, axis=0, keepdims=True)


def norm_sums(scalars, da, x, stats, gain):
    rows, width = da.shape
    return call(
        norm_sums_body,
        (1,),
        [full(v.shape) for v in (da, x, stats, gain)],
        [pl.BlockSpec((2, rows), lambda i, sc: (0, 0)), pl.BlockSpec((2, width), lambda i, sc: (0, 0))],
        [shape_of((2, rows), F32), shape_of((2, width), F32)],
        scalars,
        [da, x, stats, gain],
    )


def attn_grad_body(sc, a0, a1, c0, c1, z0, z1, d0, d1, o0, o1, send1, keep1, send2, keep2):
    i = pl.program_id(0)
    width = o0.shape[1]
    low1 = dot_tn(a0[...], d0[:, : 2 * width]) + dot_tn(a1[...], d1[:, : 2 * width])
    low2 = dot_tn(c0[...], d0[:, 2 * width :]) + dot_tn(c1[...], d1[:, 2 * width :])
    low3 = dot_tn(z0[...], o0[...]) + dot_tn(z1[...], o1[...])
    low1, low2, low3 = low1.astype(BF16), low2.astype(BF16), low3.astype(BF16)
    for step, (out1, out2) in enumerate(((send1, send2), (keep1, keep2))):

        @pl.when(i == step)
        def _(out1=out1, out2=out2):
            out1[...] = low1
            out2[:, :width] = low2
            out2[:, width:] = low3


def attn_grad(scalars, acts, dzs, grads, mixed, bits):
    rows, m = acts[0].shape
    width = mixed[0].shape[1]

    def half(bit):
        def index(i, sc):
            mine = jnp.bitwise_and(jnp.right_shift(sc[2], bit), 1)
            return (0, jnp.where(i == 0, 1 - mine, mine))

        return pl.BlockSpec((rows, m // 2), index)

    shape = (m // 2, 2 * width)
    return call(
        attn_grad_body,
        (2,),
        [half(bits[0])] * 2 + [half(bits[1])] * 4 + [full(v.shape) for v in (*grads, *mixed)],
        [pl.BlockSpec(shape, lambda i, sc: (0, 0))] * 4,
        [shape_of(shape, BF16)] * 4,
        scalars,
        [*acts, *acts, *dzs, *grads, *mixed],
        flops=16 * rows * m * width,
        vmem=32,
    )


def place_body(blocks, sc, first, second, out):
    rows = first.shape[0] * 2 // blocks
    half = blocks // 2
    for k in range(blocks):
        src = first if k < half else second
        at = (k if k < half else k - half) * rows
        to = pl.ds(pl.multiple_of(jnp.bitwise_xor(sc[0], k) * rows, rows), rows)
        out[to, :] = src[at : at + rows, :].astype(F32)


def place(index, first, second, blocks, width):
    m, count = first.shape[0] * 2, first.shape[1]
    half = pl.BlockSpec((m // 2, width), lambda i, sc: (0, i))
    return call(
        functools.partial(place_body, blocks),
        (count // width,),
        [half, half],
        pl.BlockSpec((m, width), lambda i, sc: (0, i)),
        shape_of((m, count), F32),
        index,
        [first, second],
    )


def unpack_body(scale, blocks, sc, f1, s1, f2, s2, d_qkv, d_out):
    i = pl.program_id(0)
    rows = f1.shape[0] * 2 // blocks
    half = blocks // 2

    def each(first, second, index, put):
        for k in range(blocks):
            src = first if k < half else second
            at = (k if k < half else k - half) * rows
            to = pl.ds(pl.multiple_of(jnp.bitwise_xor(index, k) * rows, rows), rows)
            put(to, src[at : at + rows, :].astype(F32))

    def plain(to, value):
        d_qkv[0, to, :] = value

    def scaled(to, value):
        d_qkv[0, to, :] = value * jnp.where(i == 0, jnp.float32(scale), jnp.float32(1.0))

    def turned(to, value):
        d_out[:, to] = jnp.transpose(value)

    @pl.when(i < 2)
    def _():
        each(f1, s1, sc[0], scaled)

    @pl.when(i == 2)
    def _():
        each(f2, s2, sc[1], plain)

    @pl.when(i == 3)
    def _():
        each(f2, s2, sc[1], turned)


def unpack(index, first1, second1, first2, second2, blocks, scale):
    m, count = first1.shape[0] * 2, first1.shape[1]
    width = count // 2
    one = pl.BlockSpec((m // 2, width), lambda i, sc: (0, jnp.minimum(i, 1)))
    two = pl.BlockSpec((m // 2, width), lambda i, sc: (0, jnp.maximum(i - 2, 0)))
    return call(
        functools.partial(unpack_body, scale, blocks),
        (4,),
        [one, one, two, two],
        [
            pl.BlockSpec((1, m, width), lambda i, sc: (jnp.minimum(i, 2), 0, 0)),
            pl.BlockSpec((width, m), lambda i, sc: (0, 0)),
        ],
        [shape_of((3, m, width), F32), shape_of((width, m), F32)],
        index,
        [first1, second1, first2, second2],
    )


def halve_body(bits, sc, *refs):
    n = len(bits)
    keeps, gots, sends, nexts = refs[:n], refs[n : 2 * n], refs[2 * n : 3 * n], refs[3 * n :]
    for bit, keep, got, send, nxt in zip(bits, keeps, gots, sends, nexts):
        half = send.shape[0]
        mine = jnp.bitwise_and(jnp.right_shift(sc[2], bit), 1)
        for out, side in ((send, 1 - mine), (nxt, mine)):
            rows = pl.ds(pl.multiple_of(side * half, half), half)
            out[...] = (keep[rows, :].astype(F32) + got[rows, :].astype(F32)).astype(BF16)


def halve(scalars, keeps, gots, bits):
    shapes = [shape_of((k.shape[0] // 2, k.shape[1]), BF16) for k in keeps] * 2
    return call(
        functools.partial(halve_body, bits),
        (1,),
        [full(v.shape) for v in (*keeps, *gots)],
        [pl.BlockSpec(v.shape, lambda i, sc: (0, 0)) for v in shapes],
        shapes,
        scalars,
        [*keeps, *gots],
    )


def join_body(added, sc, *refs):
    n = len(refs) // 3
    for a, c, out in zip(refs[:n], refs[n : 2 * n], refs[2 * n :]):
        rows = a.shape[0]
        if added:
            out[...] = (a[...].astype(F32) + c[...].astype(F32)).astype(BF16)
        else:
            out[:rows, :] = a[...]
            out[rows:, :] = c[...]


def join(scalars, firsts, seconds, added):
    times = 1 if added else 2
    shapes = [shape_of((a.shape[0] * times, a.shape[1]), BF16) for a in firsts]
    return call(
        functools.partial(join_body, added),
        (1,),
        [full(v.shape) for v in (*firsts, *seconds)],
        [pl.BlockSpec(v.shape, lambda i, sc: (0, 0)) for v in shapes],
        shapes,
        scalars,
        [*firsts, *seconds],
    )


def prepare_body(half, lens, here, out):
    count = lens.shape[1]
    start, border, before = jnp.int32(0), jnp.int32(0), jnp.int32(0)
    for i in range(count):
        big = lens[0, i] == half
        start = jnp.where(big, before, start)
        border = jnp.where(big, lens[0, (i + 1) % count], border)
        before = before + lens[0, i]
    out[0] = here[0]
    out[1] = border
    out[2] = here[1]
    out[3] = start


def prepare(lengths, here, half):
    smem = pl.BlockSpec(memory_space=pltpu.SMEM)
    return pl.pallas_call(
        functools.partial(prepare_body, half),
        in_specs=[smem, smem],
        out_specs=smem,
        out_shape=shape_of((4,), jnp.int32),
    )(lengths, here)


class Chain:
    def __init__(self):
        self.last = ()

    def tie(self, value, *need):
        return lax.optimization_barrier((value, need, self.last))[0]

    def do(self, fn, *args, **keywords):
        leaves, tree = jax.tree_util.tree_flatten(args)
        arrays = iter(self.tie([v for v in leaves if isinstance(v, jax.Array)]))
        leaves = [next(arrays) if isinstance(v, jax.Array) else v for v in leaves]
        out = fn(*jax.tree_util.tree_unflatten(tree, leaves), **keywords)
        self.last = jax.tree_util.tree_leaves(out)[0]
        return out


class RowSums:
    def __init__(self, chain, scalars, r, n_rows, orders, pairs, core_flip=None):
        self.chain, self.scalars, self.r, self.n_rows = chain, scalars, r, n_rows
        self.orders = orders
        self.depth = len(orders[0])
        self.rest = [b for b in range(n_rows.bit_length() - 1) if b not in orders[0]]
        self.keeps = [keep for _, keep in pairs]
        sends = [send for send, _ in pairs]
        self.at = 0 if core_flip is None else -1
        self.gots = self.flips(sends) if core_flip is None else [core_flip(v) for v in sends]

    def flip(self, value, bit):
        return lax.ppermute(value, "rows", [(i, i ^ (1 << bit)) for i in range(self.n_rows)])

    def flips(self, values):
        return [self.flip(v, order[self.at]) for v, order in zip(values, self.orders)]

    def scatter(self):
        self.at += 1
        if self.at < self.depth:
            bits = [order[self.at] for order in self.orders]
            out = self.chain.do(halve, self.scalars, self.keeps, self.gots, bits)
            n = len(self.orders)
            self.keeps = out[n:]
            self.gots = self.flips(out[:n])
            return
        total = self.chain.do(join, self.scalars, self.keeps, self.gots, True)
        for b in self.rest:
            total = self.chain.do(join, self.scalars, total, [self.flip(v, b) for v in total], True)
        self.bufs = total
        self.at = self.depth - 1
        self.gots = self.flips(self.bufs)

    def gather(self):
        self.at -= 1
        self.bufs = self.chain.do(join, self.scalars, self.bufs, self.gots, False)
        self.gots = self.flips(self.bufs)

    def index(self, which):
        index = 0
        for b in self.orders[which]:
            index = index * 2 + jnp.bitwise_and(jnp.right_shift(self.r, b), 1)
        return index

    def finish(self, which, width):
        index = jnp.stack([self.index(which)] * 2).astype(jnp.int32)
        return self.chain.do(
            place, index, self.bufs[which], self.gots[which], 1 << self.depth, width
        )

    def finish_attn(self, scale):
        index = jnp.stack([self.index(0), self.index(1)]).astype(jnp.int32)
        return self.chain.do(
            unpack, index, self.bufs[0], self.gots[0], self.bufs[1], self.gots[1],
            1 << self.depth, scale,
        )


def local(
    n_tp, n_rows,
    datapoints, lengths, qkv_weight, out_weight, up_weight, up_bias, down_weight, down_bias,
    gain_one, shift_one, gain_two, shift_two, grad_out,
):
    tok, width = datapoints.shape
    count = n_tp * width
    half = tok // 2
    q_scale = DH ** (-0.5)
    t, r = lax.axis_index("tp"), lax.axis_index("rows")
    chain = Chain()
    do, tie = chain.do, chain.tie

    def core_flip(v):
        return lax.ppermute(v, "tp", [(i, i ^ 1) for i in range(n_tp)])

    def x_flip(v):
        return lax.ppermute(v, "tp", [(i, i ^ 2) for i in range(n_tp)])

    def row_flip(v, b):
        return lax.ppermute(v, "rows", [(i, i ^ (1 << b)) for i in range(n_rows)])

    def first_half(v, start):
        return lax.dynamic_slice_in_dim(v, start, half, 0)

    def second_half(v, start):
        turned = jnp.concatenate([v[half:], v[:half]], 0)
        return lax.dynamic_slice_in_dim(turned, start, half, 0)

    def rolled(v, start):
        return lax.dynamic_slice_in_dim(jnp.concatenate([v, v[:half]], 0), start, tok, 0)

    ow = lax.all_gather(out_weight, "tp", axis=0, tiled=True)
    vectors = jnp.concatenate([gain_one, shift_one, gain_two, shift_two, down_bias])
    vec_x = x_flip(vectors)
    vec_c = core_flip(jnp.concatenate([vectors, up_bias]))
    scalars = prepare(lengths, jnp.stack([t, r]).astype(jnp.int32), half)
    start = scalars[3]
    x0 = do(first_half, datapoints, start)
    x0_x, x0_c = x_flip(x0), core_flip(x0)
    x1 = do(second_half, datapoints, start)
    dy = do(rolled, grad_out, start)
    vec_d = core_flip(tie(vec_x))
    d_down_bias = do(lambda v: jnp.sum(v.astype(F32), axis=0), grad_out)
    n_vec = vectors.shape[0] // width

    def vector_orders(*pieces):
        rel = jnp.stack([p[: n_vec * width].reshape(n_vec, width) for p in pieces])
        order = jnp.bitwise_xor(t, jnp.arange(n_tp))
        return rel, jnp.transpose(rel[order], (1, 0, 2)).reshape(n_vec, count)

    gains_rel, gains = do(vector_orders, vectors, vec_c, vec_x, vec_d)
    weight4 = qkv_weight.reshape(3, n_tp, width, width)

    x0_d = core_flip(x0_x)
    x1 = tie(x1, x0_x)
    x1_x, x1_c = x_flip(x1), core_flip(x1)
    xs = [[x0, x0_c, x0_x, x0_d], None]
    qkv, acts, stats, mixed, lse, pieces = [[None] * 2 for _ in range(6)]

    def first(h):
        qkv[h], acts[h], stats[h], mixed[h], lse[h], other, mine = do(
            first_layer, scalars, xs[h], dy, gains_rel, weight4, h
        )
        diag = lax.ppermute(other, "tp", [(i, i ^ 3) for i in range(n_tp)])
        pieces[h] = [mine, core_flip(other), x_flip(mine), diag]

    first(0)
    up_c, down_c = core_flip(tie(up_weight)), core_flip(tie(down_weight))
    x1_d = core_flip(tie(x1_x))
    xs[1] = [x1, x1_c, x1_x, x1_d]
    first(1)

    def both(up_w, down_w, up_b, up_w_c, down_w_c, vec):
        up_b_c = vec[n_vec * width :]
        return (
            jnp.concatenate([up_w, up_w_c], 1),
            jnp.concatenate([down_w, down_w_c], 0),
            jnp.concatenate([up_b, up_b_c]).reshape(1, -1),
        )

    up2, down2, bias2 = do(both, up_weight, down_weight, up_bias, up_c, down_c, vec_c)
    weights = [ow, gains, up2, down2, bias2]
    fed0 = do(feed, scalars, xs[0], pieces[0], *weights)
    db0_x = x_flip(fed0[7])
    fed1 = do(feed, scalars, xs[1], pieces[1], *weights)
    db1_x = x_flip(fed1[7])
    y_cols, b, dyn, g, du = [[fed0[k], fed1[k]] for k in (0, 3, 4, 5, 6)]
    dz0, sums0 = do(norm_back, scalars, fed0[8], db0_x, fed0[1], fed0[2], gains)
    dz0_x, dz0_c = x_flip(dz0), core_flip(dz0)
    down_pair = do(pair_grad, scalars, g, dyn, True)
    up_pair = do(pair_grad, scalars, b, du, False)
    sums = RowSums(
        chain, scalars, r, n_rows, [[0, 1, 2], [1, 0, 2]], [down_pair, up_pair], core_flip
    )
    sums.scatter()
    dz1, sums1 = do(norm_back, scalars, fed1[8], db1_x, fed1[1], fed1[2], gains)
    dz1_x, dz1_c = x_flip(dz1), core_flip(dz1)
    dz0_d = core_flip(tie(dz0_x))
    two_sums = sums0 + sums1
    hidden = up_bias.shape[0]
    bias_grad = do(jnp.add, fed0[9], fed1[9])
    bias_got = core_flip(bias_grad[:, hidden:])

    grads0, dzn0 = do(
        attend_back, scalars, [dz0, dz0_c, dz0_x, dz0_d], out_weight, qkv[0], lse[0], False
    )
    dz1_d = core_flip(tie(dz1_x))
    sums.scatter()
    grads1, dzn1 = do(
        attend_back, scalars, [dz1, dz1_c, dz1_x, dz1_d], out_weight, qkv[1], lse[1], True
    )
    sums.scatter()
    parts = do(attn_grad, scalars, acts, [dzn0, dzn1], [grads0, grads1], mixed, (0, 1))
    attn = RowSums(chain, scalars, r, n_rows, [[0, 1, 2], [1, 0, 2]], [parts[:2], parts[2:]])

    def middle(keep, got):
        return (keep[1].astype(F32) + got[1].astype(F32)).astype(BF16)

    def total_of(keep, got, got_x):
        return keep[0].astype(F32) + got[0].astype(F32) + got_x.astype(F32)

    sums.scatter()
    send, keep_a = do(spread, scalars, [grads0, grads1], qkv_weight, n_tp, (q_scale, 1.0, 1.0))
    got_a = core_flip(send)
    attn.scatter()
    sums.gather()
    da_x = x_flip(do(middle, keep_a, got_a))
    out_send, out_keep = do(out_product, scalars, g, down2)
    attn.scatter()
    sums.gather()
    out_x = x_flip(tie(out_send, da_x))
    gain_row = gain_one.reshape(1, -1)

    def joined(*parts):
        return total_of(*parts).astype(BF16)

    da = do(joined, keep_a, got_a, da_x)
    m0, ones0 = do(norm_sums, scalars, da[:half], x0, stats[0], gain_row)
    m1, ones1 = do(norm_sums, scalars, da[half:], x1, stats[1], gain_row)
    attn.scatter()
    m = do(lambda *a: jnp.concatenate(a, 0), two_sums, m0, m1)
    m_c = core_flip(m)
    c, side = jnp.bitwise_and(t, 1), jnp.right_shift(t, 1)

    def output_rows(keep, got, y0, y1, vecs):
        wide = 2 * width
        extra = lax.dynamic_slice_in_dim(vecs[4], side * wide, wide, 0)
        total = keep.astype(F32) + got.astype(F32) + jnp.concatenate([y0, y1], 0) + extra
        low = total.astype(BF16)
        return (
            lax.dynamic_slice_in_dim(low, (1 - c) * width, width, 1),
            lax.dynamic_slice_in_dim(low, c * width, width, 1),
        )

    rows_send, rows_keep = do(output_rows, out_keep, out_x, *y_cols, gains)
    rows_got = core_flip(rows_send)
    m = do(jnp.add, m, m_c)
    m_x = x_flip(m)
    attn.gather()

    def unroll(first, second):
        thrice = jnp.concatenate([second, first, second], 0)
        return lax.dynamic_slice_in_dim(thrice, half - start, tok, 0)

    def output_of(mine, other):
        part = half // 2
        halves = []
        for h in range(2):
            a, b = mine[h * part : (h + 1) * part], other[h * part : (h + 1) * part]
            halves.append(
                jnp.where(c == 0, jnp.concatenate([a, b], 0), jnp.concatenate([b, a], 0))
            )
        return unroll(*halves)

    output = do(output_of, rows_keep, rows_got)
    m = do(jnp.add, m, m_x)

    def small_of(up_b, down_b, m, ones0, ones1):
        two = lax.dynamic_slice_in_dim(m[:2], t * width, width, 1)
        return jnp.concatenate(
            [up_b.reshape(-1), down_b, (ones0 + ones1).reshape(-1), two.reshape(-1)]
        ).reshape(-1, 128)

    d_up_bias = bias_grad[:, :hidden] + bias_got
    small = do(small_of, d_up_bias, d_down_bias, m, ones0, ones1)
    bits = list(range(n_rows.bit_length() - 1))
    small_got = row_flip(small, bits[0])

    def d_input_of(m, da, *parts):
        halves = []
        for h, (x, stat, dzn) in enumerate((parts[:3], parts[3:])):
            nhat = (x.astype(F32) - stat[:, 0:1]) * stat[:, 1:2]
            first, second = m[2 + 2 * h][:, None] / count, m[3 + 2 * h][:, None] / count
            dz = lax.dynamic_slice_in_dim(dzn, t * width, width, 1).astype(F32)
            n = da[h * half : (h + 1) * half].astype(F32) * gain_one
            halves.append(dz + stat[:, 1:2] * (n - first - nhat * second))
        return unroll(*halves)

    attn.gather()
    d_input = do(d_input_of, m, da, x0, stats[0], dzn0, x1, stats[1], dzn1)
    d_down = sums.finish(0, width)
    for bit in bits[1:]:
        small = do(jnp.add, small, small_got)
        small_got = row_flip(small, bit)
    d_up = sums.finish(1, width)
    small = do(jnp.add, small, small_got).reshape(-1)
    d_qkv, d_out = attn.finish_attn(q_scale)
    d_down_bias, d_gain_one, d_shift_one, d_gain_two, d_shift_two = small[hidden:].reshape(5, width)
    return (
        output, d_input, d_qkv, d_out, d_up, small[:hidden],
        d_down, d_down_bias, d_gain_one, d_shift_one, d_gain_two, d_shift_two,
    )


def solution(mesh):
    grid = P("rows", "tp")
    placed = (
        grid, P("rows", None), P(None, None, "tp"), P("tp", None), P(None, "tp"), P("tp"),
        P("tp", None), P("tp"), P("tp"), P("tp"), P("tp"), P("tp"), grid,
    )
    return jax.shard_map(
        functools.partial(local, mesh.shape["tp"], mesh.shape["rows"]),
        mesh=mesh,
        in_specs=placed,
        out_specs=(
            grid, grid, P(None, None, "tp"), P("tp", None), P(None, "tp"), P("tp"),
            P("tp", None), P("tp"), P("tp"), P("tp"), P("tp"), P("tp"),
        ),
        check_vma=False,
    )
```

time: 482 us -> 428 us (0.89)
  Pallas kernels: 171 us -> 128 us
  local copies, waits for them, and re-layouts: 36.8 us -> 64.4 us
  other arithmetic: 42.2 us -> 22.6 us
  waiting for transfers between devices: 151 us -> 132 us
  between operations: 7.37 us -> 22.4 us
  starting transfers between devices: 64.1 us -> 51.9 us
    pallas_call x22 -> x29, Pallas kernels: 171 us -> 127 us  [call(): pl.pallas_call(body, grid_spec=pltpu.PrefetchScalarGridSpec(num_scalar_pr...]
    ppermute x19 -> x12, waiting for transfers between devices: 62.9 us -> 39.7 us  [x_flip(): return lax.ppermute(v, 'tp', [(i, i ^ 2) for i in range(n_tp)])]
    unnamed x136 -> x163, local copies, waits for them, and re-layouts: 28.8 us -> 51.3 us
    convert_element_type x19 -> x3, other arithmetic: 16.6 us -> 4.07 us  [the longest x1 2 us: joined(): return total_of(*parts).astype(BF16)]
    ppermute x19 -> x12, starting transfers between devices: 24.8 us -> 14.6 us  [x_flip(): return lax.ppermute(v, 'tp', [(i, i ^ 2) for i in range(n_tp)])]
    ppermute x24, waiting for transfers between devices: 87.2 us -> 82.2 us  [flip(): lax.ppermute(value, 'rows', [(i, i ^ 1 << bit) for i in range(self.n_rows)])]
    ppermute x29 -> x20, waiting for transfers between devices: 0.08 us -> 5.02 us  [core_flip(): return lax.ppermute(v, 'tp', [(i, i ^ 1) for i in range(n_tp)])]
  transfers between devices with their start and end apart: 75 -> 62, of which waited for: 22 -> 27; matrix products, arithmetic and copies ran while one was open for 11% -> 9% of each run, Pallas kernels for 29% -> 24%
where the time goes in v2:
time: 428 us; the launch traced here: 421 us
  waiting for transfers between devices  132 us (31%)
  Pallas kernels  128 us (30%)
  local copies, waits for them, and re-layouts  64.4 us (15%)
  starting transfers between devices  51.9 us (12%)
  other arithmetic  22.6 us (5%)
  between operations  22.4 us (5%)
    pallas_call x29, Pallas kernels, call(): pl.pallas_call(body, grid_spec=pltpu.PrefetchScalarGridSpec(num_scalar_pr...  127 us
    ppermute x24, waiting for transfers between devices, flip(): lax.ppermute(value, 'rows', [(i, i ^ 1 << bit) for i in range(self.n_rows)])  82.2 us
    unnamed x163, local copies, waits for them, and re-layouts  51.3 us
    ppermute x12, waiting for transfers between devices, x_flip(): return lax.ppermute(v, 'tp', [(i, i ^ 2) for i in range(n_tp)])  39.7 us
    ppermute x24, starting transfers between devices, flip(): lax.ppermute(value, 'rows', [(i, i ^ 1 << bit) for i in range(self.n_rows)])  29 us
    ppermute x12, starting transfers between devices, x_flip(): return lax.ppermute(v, 'tp', [(i, i ^ 2) for i in range(n_tp)])  14.6 us
  transfers between devices with their start and end apart: 62, of which 27 were waited for; matrix products, arithmetic and copies ran while one was open for 9% of the time, Pallas kernels for 24%

profile of v2, /device:TPU:0, one launch (start us, length us, event | category | flops | bytes accessed | tf_op | source)
XLA Modules:
  0.0 421.2 jit_solution(14208840691580198518)
XLA Ops:
  40.7 10.9 %shard_map.221 = (bf16[3,1024,256]{2,1,0:T(8,128)(2,1)S(1)}, bf16[1024,1024]{1,0:T(8,128)(2,1)S(1)}, f32[1024,2]{1,0:T(8,128)S(1)}, bf16[1024,256]{1,0:T(8,128)(...) custom-call(s32[4]{0:T(128)S(1)} %copy-done.30, ...), custom_call_target="tpu_custom_call" | custom-call | flops 2684354560 | bytes 11046912 | tf_op jit(solution)/shard_map/pallas_call | solution.py:42
  58.5 12.4 %collective-permute-done.12.x2 = bf16[1024,256]{1,0:T(8,128)(2,1)} collective-permute-done((bf16[1024,256]{1,0:T(8,128)(2,1)S(1)}, bf16[1024,256]{1,0:T(8,128)(2,1)}, u32[]{:S(2)}, u32[]{:S(2)}) %collective-permute-start.12) | collective-permute-done | bytes 524320 | tf_op jit(solution)/shard_map/ppermute | solution.py:860
  77.4 13.0 %shard_map.222 = (bf16[3,1024,256]{2,1,0:T(8,128)(2,1)S(1)}, bf16[1024,1024]{1,0:T(8,128)(2,1)S(1)}, f32[1024,2]{1,0:T(8,128)S(1)}, bf16[1024,256]{1,0:T(8,128)(...) custom-call(s32[4]{0:T(128)S(1)} %copy-done.30, ...), custom_call_target="tpu_custom_call" | custom-call | flops 2684354560 | bytes 11046912 | tf_op jit(solution)/shard_map/pallas_call | solution.py:42
  117.3 13.1 %shard_map.223 = (f32[512,512]{1,0:T(8,128)S(1)}, f32[256,1024]{1,0:T(8,128)S(1)}, bf16[256,1024]{1,0:T(8,128)(2,1)S(1)}, bf16[512,1024]{1,0:T(8,128)(2,1)S(1)},...) custom-call(s32[4]{0:T(128)S(1)} %copy-done.30, ...), custom_call_target="tpu_custom_call" | custom-call | flops 7516192768 | bytes 24678400 | tf_op jit(solution)/shard_map/pallas_call | solution.py:42
  135.1 13.9 %shard_map.224 = (f32[512,512]{1,0:T(8,128)S(1)}, f32[256,1024]{1,0:T(8,128)S(1)}, bf16[256,1024]{1,0:T(8,128)(2,1)S(1)}, bf16[512,1024]{1,0:T(8,128)(2,1)S(1)},...) custom-call(s32[4]{0:T(128)S(1)} %copy-done.30, ...), custom_call_target="tpu_custom_call" | custom-call | flops 7516192768 | bytes 24678400 | tf_op jit(solution)/shard_map/pallas_call | solution.py:42
  152.0 6.0 %shard_map.226 = (bf16[1024,1024]{1,0:T(8,128)(2,1)S(1)}, bf16[1024,1024]{1,0:T(8,128)(2,1)S(1)}) custom-call(s32[4]{0:T(128)S(1)} %copy-done.30, bf16[512,2048]{1,0:T(8,128)(2,1)S(1)} %get-tuple-element.562.a0.refs_0_, bf16[512,2048]{1,0:T(8,128)(2,1)S(1)} %get-tuple-element.563.a1.refs_1_, bf16[512,1024]{1,0:T(8,128)(2,1)S(1)} %copy-done.68, ...), custom_call_target="tpu_custom_call" | custom-call | flops 4294967296 | bytes 10485760 | tf_op jit(solution)/shard_map/pallas_call | solution.py:42
  158.0 6.2 %shard_map.227 = (bf16[1024,1024]{1,0:T(8,128)(2,1)S(1)}, bf16[1024,1024]{1,0:T(8,128)(2,1)S(1)}) custom-call(s32[4]{0:T(128)S(1)} %copy-done.30, bf16[512,1024]{1,0:T(8,128)(2,1)S(1)} %get-tuple-element.449.a0, bf16[512,1024]{1,0:T(8,128)(2,1)S(1)} %get-tuple-element.450.a1, bf16[512,2048]{1,0:T(8,128)(2,1)S(1)} %copy-done.64, bf16[512,2048]{1,0:T(8,128)(2,1)S(1)} %copy-done.66), custom_call_target="tpu_custom_call" | custom-call | flops 4294967296 | bytes 10485760 | tf_op jit(solution)/shard_map/pallas_call | solution.py:42
  173.0 6.6 %collective-permute-done.20.p1 = bf16[256,1024]{1,0:T(8,128)(2,1)S(1)} collective-permute-done((bf16[256,1024]{1,0:T(8,128)(2,1)S(1)}, bf16[256,1024]{1,0:T(8,128)(2,1)S(1)}, u32[]{:S(2)}, u32[]{:S(2)}) %collective-permute-start.20) | collective-permute-done | bytes 524320 | tf_op jit(solution)/shard_map/ppermute | solution.py:860
  181.0 9.0 %collective-permute-done.19.z2 = bf16[256,1024]{1,0:T(8,128)(2,1)S(1)} collective-permute-done((bf16[256,1024]{1,0:T(8,128)(2,1)S(1)}, bf16[256,1024]{1,0:T(8,128)(2,1)S(1)}, u32[]{:S(2)}, u32[]{:S(2)}) %collective-permute-start.19) | collective-permute-done | bytes 524320 | tf_op jit(solution)/shard_map/ppermute | solution.py:860
  193.9 10.1 %shard_map.230 = (bf16[1024,768]{1,0:T(8,128)(2,1)S(1)}, bf16[1024,1024]{1,0:T(8,128)(2,1)S(1)}) custom-call(s32[4]{0:T(128)S(1)} %copy-done.30, bf16[256,1024]{1,0:T(8,128)(2,1)S(1)} %get-tuple-element.475.z0, bf16[256,1024]{1,0:T(8,128)(2,1)S(1)} %collective-permute-done.18.z1, bf16[256,1024]{1,0:T(8,128)(2,1)S(1)} %collective-permute-done.19.z2, ...), custom_call_target="tpu_custom_call" | custom-call | flops 3221225472 | bytes 11018240 | tf_op jit(solution)/shard_map/pallas_call | solution.py:42
  206.8 8.8 %collective-permute-done.27.refs_2_ = bf16[512,1024]{1,0:T(8,128)(2,1)S(1)} collective-permute-done((bf16[512,1024]{1,0:T(8,128)(2,1)S(1)}, bf16[512,1024]{1,0:T(8,128)(2,1)S(1)}, u32[]{:S(2)}, u32[]{:S(2)}) %collective-permute-start.27) | collective-permute-done | bytes 1048608 | tf_op jit(solution)/shard_map/ppermute | solution.py:797
  219.9 10.3 %shard_map.232 = (bf16[1024,768]{1,0:T(8,128)(2,1)S(1)}, bf16[1024,1024]{1,0:T(8,128)(2,1)S(1)}) custom-call(s32[4]{0:T(128)S(1)} %copy-done.30, bf16[256,1024]{1,0:T(8,128)(2,1)S(1)} %get-tuple-element.495.z0, bf16[256,1024]{1,0:T(8,128)(2,1)S(1)} %collective-permute-done.24.z1, bf16[256,1024]{1,0:T(8,128)(2,1)S(1)} %collective-permute-done.25.z2, ...), custom_call_target="tpu_custom_call" | custom-call | flops 3221225472 | bytes 11018240 | tf_op jit(solution)/shard_map/pallas_call | solution.py:42
  236.1 6.5 %shard_map.234 = (bf16[512,512]{1,0:T(8,128)(2,1)S(1)}, bf16[512,512]{1,0:T(8,128)(2,1)S(1)}, bf16[512,512]{1,0:T(8,128)(2,1)S(1)}, bf16[512,512]{1,0:T(8,128)(2,1)S(1)}) custom-call(s32[4]{0:T(128)S(1)} %copy-done.30, bf16[1024,1024]{1,0:T(8,128)(2,1)S(1)} %get-tuple-element.522.a0.c0, bf16[1024,1024]{1,0:T(8,128)(2,1)S(1)} %copy-done.1, ...), custom_call_target="tpu_custom_call" | custom-call | flops 4294967296 | bytes 18874368 | tf_op jit(solution)/shard_map/pallas_call | solution.py:42
  242.7 9.2 %collective-permute-done.31.refs_2_ = bf16[128,1024]{1,0:T(8,128)(2,1)S(1)} collective-permute-done((bf16[128,1024]{1,0:T(8,128)(2,1)S(1)}, bf16[128,1024]{1,0:T(8,128)(2,1)S(1)}, u32[]{:S(2)}, u32[]{:S(2)}) %collective-permute-start.31) | collective-permute-done | bytes 262176 | tf_op jit(solution)/shard_map/ppermute | solution.py:797
  251.8 5.5 %collective-permute-done.32.refs_3_ = bf16[128,1024]{1,0:T(8,128)(2,1)S(1)} collective-permute-done((bf16[128,1024]{1,0:T(8,128)(2,1)S(1)}, bf16[128,1024]{1,0:T(8,128)(2,1)S(1)}, u32[]{:S(2)}, u32[]{:S(2)}) %collective-permute-start.32) | collective-permute-done | bytes 262176 | tf_op jit(solution)/shard_map/ppermute | solution.py:797
  258.0 5.7 %shard_map.236 = (bf16[2,2048,256]{2,1,0:T(8,128)(2,1)S(1)}, bf16[2,2048,256]{2,1,0:T(8,128)(2,1)S(1)}) custom-call(s32[4]{0:T(128)S(1)} %copy-done.30, bf16[1024,768]{1,0:T(8,128)(2,1)S(1)} %get-tuple-element.538.d0.refs_0_, bf16[1024,768]{1,0:T(8,128)(2,1)S(1)} %get-tuple-element.539.d1.refs_1_, bf16[3,1024,256]{2,1,0:T(8,128)(2,1)S(1)} %copy-done.40), custom_call_target="tpu_custom_call" | custom-call | flops 3221225472 | bytes 8912896 | tf_op jit(solution)/shard_map/pallas_call | solution.py:42
  267.9 10.3 %collective-permute-done.36.refs_2_ = bf16[512,512]{1,0:T(8,128)(2,1)S(1)} collective-permute-done((bf16[512,512]{1,0:T(8,128)(2,1)S(1)}, bf16[512,512]{1,0:T(8,128)(2,1)S(1)}, u32[]{:S(2)}, u32[]{:S(2)}) %collective-permute-start.36) | collective-permute-done | bytes 524320 | tf_op jit(solution)/shard_map/ppermute | solution.py:797
  278.2 11.5 %collective-permute-done.37.refs_3_ = bf16[512,512]{1,0:T(8,128)(2,1)S(1)} collective-permute-done((bf16[512,512]{1,0:T(8,128)(2,1)S(1)}, bf16[512,512]{1,0:T(8,128)(2,1)S(1)}, u32[]{:S(2)}, u32[]{:S(2)}) %collective-permute-start.37) | collective-permute-done | bytes 524320 | tf_op jit(solution)/shard_map/ppermute | solution.py:797
  296.9 6.7 %shard_map.239 = (bf16[1024,512]{1,0:T(8,128)(2,1)}, bf16[1024,512]{1,0:T(8,128)(2,1)S(1)}) custom-call(s32[4]{0:T(128)S(1)} %copy-done.30, bf16[512,2048]{1,0:T(8,128)(2,1)S(1)} %get-tuple-element.562.a0.refs_0_, bf16[512,2048]{1,0:T(8,128)(2,1)S(1)} %get-tuple-element.563.a1.refs_1_, bf16[2048,1024]{1,0:T(8,128)(2,1)S(1)} %copy-done.22), custom_call_target="tpu_custom_call" | custom-call | flops 4294967296 | bytes 10485760 | tf_op jit(solution)/shard_map/pallas_call | solution.py:42
  303.6 7.1 %collective-permute-done.41.refs_2_ = bf16[256,512]{1,0:T(8,128)(2,1)S(1)} collective-permute-done((bf16[256,512]{1,0:T(8,128)(2,1)S(1)}, bf16[256,512]{1,0:T(8,128)(2,1)S(1)}, u32[]{:S(2)}, u32[]{:S(2)}) %collective-permute-start.41) | collective-permute-done | bytes 262176 | tf_op jit(solution)/shard_map/ppermute | solution.py:797
  331.8 9.0 %collective-permute-done.43 = bf16[1024,512]{1,0:T(8,128)(2,1)} collective-permute-done((bf16[1024,512]{1,0:T(8,128)(2,1)}, bf16[1024,512]{1,0:T(8,128)(2,1)}, u32[]{:S(2)}, u32[]{:S(2)}) %collective-permute-start.43) | collective-permute-done | bytes 1048608 | tf_op jit(solution)/shard_map/ppermute | solution.py:860
  351.4 7.3 %collective-permute-done.47.refs_2_ = bf16[128,512]{1,0:T(8,128)(2,1)S(1)} collective-permute-done((bf16[128,512]{1,0:T(8,128)(2,1)S(1)}, bf16[128,512]{1,0:T(8,128)(2,1)S(1)}, u32[]{:S(2)}, u32[]{:S(2)}) %collective-permute-start.47) | collective-permute-done | bytes 131104 | tf_op jit(solution)/shard_map/ppermute | solution.py:797
  365.7 4.8 %fusion.6 = bf16[2048,256]{1,0:T(8,128)(2,1)} fusion(s32[]{:T(128)S(6)} %select_n.59, bf16[1024,256]{1,0:T(8,128)(2,1)S(1)} %maximum_select_fusion, bf16[1024,256]{1,0:T(8,128)(2,1)S(1)} %maximum_select_fusion.1), kind=kLoop, calls=%fused_computation.19 | loop fusion | flops 3145728 | bytes 2097156 | tf_op jit(solution)/shard_map/concatenate | solution.py:1005
  371.4 13.7 %collective-permute-done.51.refs_2_ = bf16[256,512]{1,0:T(8,128)(2,1)S(1)} collective-permute-done((bf16[256,512]{1,0:T(8,128)(2,1)S(1)}, bf16[256,512]{1,0:T(8,128)(2,1)S(1)}, u32[]{:S(2)}, u32[]{:S(2)}) %collective-permute-start.51) | collective-permute-done | bytes 262176 | tf_op jit(solution)/shard_map/ppermute | solution.py:797
  (353 shorter events, 181.1 us)
Async XLA Ops:
  7.2 99.1 %all-gather.2.cloned.1.call-start = ((), (), s32[]{:S(2)}) async-start(), calls=%async_computation | async-start | bytes 2621440 | tf_op jit(solution)/shard_map/all_gather | solution.py:875
  55.9 35.3 %collective-permute-start.10 = (bf16[1024,1024]{1,0:T(8,128)(2,1)}, bf16[1024,1024]{1,0:T(8,128)(2,1)}, u32[]{:S(2)}, u32[]{:S(2)}) collective-permute-start(bf16[1024,1024]{1,0:T(8,128)(2,1)} %param.19), channel_id=1, source_target_pairs={{0,1},{1,0},{2,3},{3,2},{4,5},{5,4},{6,7},{7,6},{8,9},{9,8},{10,11... | collective-permute-start | bytes 6291464 | tf_op jit(solution)/shard_map/ppermute | solution.py:857
  56.3 35.0 %collective-permute-start.9 = (bf16[1024,1024]{1,0:T(8,128)(2,1)}, bf16[1024,1024]{1,0:T(8,128)(2,1)}, u32[]{:S(2)}, u32[]{:S(2)}) collective-permute-start(bf16[1024,1024]{1,0:T(8,128)(2,1)} %param.17), channel_id=1, source_target_pairs={{0,1},{1,0},{2,3},{3,2},{4,5},{5,4},{6,7},{7,6},{8,9},{9,8},{10,11... | collective-permute-start | bytes 6291464 | tf_op jit(solution)/shard_map/ppermute | solution.py:857
  71.4 31.6 %collective-permute-start.6 = (bf16[1024,256]{1,0:T(8,128)(2,1)}, bf16[1024,256]{1,0:T(8,128)(2,1)S(1)}, u32[]{:S(2)}, u32[]{:S(2)}) collective-permute-start(bf16[1024,256]{1,0:T(8,128)(2,1)} %copy-done.52), channel_id=1, source_target_pairs={{0,1},{1,0},{2,3},{3,2},{4,5},{5,4},{6,7},{7,6},{8,9},{9,8},{10,11... | collective-permute-start | bytes 1572872 | tf_op jit(solution)/shard_map/ppermute | solution.py:857
  72.0 33.4 %collective-permute-start.8 = (bf16[1024,256]{1,0:T(8,128)(2,1)}, bf16[1024,256]{1,0:T(8,128)(2,1)S(1)}, u32[]{:S(2)}, u32[]{:S(2)}) collective-permute-start(bf16[1024,256]{1,0:T(8,128)(2,1)} %copy-done.52), channel_id=1, source_target_pairs={{0,3},{1,2},{2,1},{3,0},{4,7},{5,6},{6,5},{7,4},{8,11},{9,10},{10,... | collective-permute-start | bytes 1572872 | tf_op jit(solution)/shard_map/ppermute | solution.py:907
  73.4 31.2 %collective-permute-start.7 = (bf16[1024,256]{1,0:T(8,128)(2,1)}, bf16[1024,256]{1,0:T(8,128)(2,1)S(1)}, u32[]{:S(2)}, u32[]{:S(2)}) collective-permute-start(bf16[1024,256]{1,0:T(8,128)(2,1)} %copy-done.50), channel_id=1, source_target_pairs={{0,2},{1,3},{2,0},{3,1},{4,6},{5,7},{6,4},{7,5},{8,10},{9,11},{10,... | collective-permute-start | bytes 1572872 | tf_op jit(solution)/shard_map/ppermute | solution.py:860
  91.2 42.6 %collective-permute-start.14 = (bf16[1024,256]{1,0:T(8,128)(2,1)}, bf16[1024,256]{1,0:T(8,128)(2,1)}, u32[]{:S(2)}, u32[]{:S(2)}) collective-permute-start(bf16[1024,256]{1,0:T(8,128)(2,1)} %get-tuple-element.402), channel_id=1, source_target_pairs={{0,1},{1,0},{2,3},{3,2},{4,5},{5,4},{6,7},{7,6},{8,9},{9,8},{10,11... | collective-permute-start | bytes 1572872 | tf_op jit(solution)/shard_map/ppermute | solution.py:857
  91.3 42.5 %collective-permute-start.16 = (bf16[1024,256]{1,0:T(8,128)(2,1)}, bf16[1024,256]{1,0:T(8,128)(2,1)}, u32[]{:S(2)}, u32[]{:S(2)}) collective-permute-start(bf16[1024,256]{1,0:T(8,128)(2,1)} %get-tuple-element.402), channel_id=1, source_target_pairs={{0,3},{1,2},{2,1},{3,0},{4,7},{5,6},{6,5},{7,4},{8,11},{9,10},{10,... | collective-permute-start | bytes 1572872 | tf_op jit(solution)/shard_map/ppermute | solution.py:907
  103.8 30.0 %collective-permute-start.15 = (bf16[1024,256]{1,0:T(8,128)(2,1)}, bf16[1024,256]{1,0:T(8,128)(2,1)}, u32[]{:S(2)}, u32[]{:S(2)}) collective-permute-start(bf16[1024,256]{1,0:T(8,128)(2,1)} %get-tuple-element.409.p0), channel_id=1, source_target_pairs={{0,2},{1,3},{2,0},{3,1},{4,6},{5,7},{6,4},{7,5},{8,10},{9,11},{10,... | collective-permute-start | bytes 1572872 | tf_op jit(solution)/shard_map/ppermute | solution.py:860
  165.6 24.4 %collective-permute-start.19 = (bf16[256,1024]{1,0:T(8,128)(2,1)S(1)}, bf16[256,1024]{1,0:T(8,128)(2,1)S(1)}, u32[]{:S(2)}, u32[]{:S(2)}) collective-permute-start(bf16[256,1024]{1,0:T(8,128)(2,1)S(1)} %get-tuple-element.475.z0), channel_id=1, source_target_pairs={{0,2},{1,3},{2,0},{3,1},{4,6},{5,7},{6,4},{7,5},{8,10},{9,11},{10,... | collective-permute-start | bytes 1572872 | tf_op jit(solution)/shard_map/ppermute | solution.py:860
  166.9 26.9 %collective-permute-start.18 = (bf16[256,1024]{1,0:T(8,128)(2,1)S(1)}, bf16[256,1024]{1,0:T(8,128)(2,1)S(1)}, u32[]{:S(2)}, u32[]{:S(2)}) collective-permute-start(bf16[256,1024]{1,0:T(8,128)(2,1)S(1)} %get-tuple-element.475.z0), channel_id=1, source_target_pairs={{0,1},{1,0},{2,3},{3,2},{4,5},{5,4},{6,7},{7,6},{8,9},{9,8},{10,11... | collective-permute-start | bytes 1572872 | tf_op jit(solution)/shard_map/ppermute | solution.py:857
  190.0 25.6 %collective-permute-start.27 = (bf16[512,1024]{1,0:T(8,128)(2,1)S(1)}, bf16[512,1024]{1,0:T(8,128)(2,1)S(1)}, u32[]{:S(2)}, u32[]{:S(2)}) collective-permute-start(bf16[512,1024]{1,0:T(8,128)(2,1)S(1)} %get-tuple-element.460), channel_id=1, source_target_pairs={{0,4},{4,0},{8,12},{12,8},{16,20},{20,16},{24,28},{28,24},{1,5},{5... | collective-permute-start | bytes 3145736 | tf_op jit(solution)/shard_map/ppermute | solution.py:797
  191.4 25.3 %collective-permute-start.28 = (bf16[512,1024]{1,0:T(8,128)(2,1)S(1)}, bf16[512,1024]{1,0:T(8,128)(2,1)S(1)}, u32[]{:S(2)}, u32[]{:S(2)}) collective-permute-start(bf16[512,1024]{1,0:T(8,128)(2,1)S(1)} %get-tuple-element.487), channel_id=1, source_target_pairs={{0,8},{4,12},{8,0},{12,4},{16,24},{20,28},{24,16},{28,20},{1,9},{5... | collective-permute-start | bytes 3145736 | tf_op jit(solution)/shard_map/ppermute | solution.py:797
  193.8 26.0 %collective-permute-start.24 = (bf16[256,1024]{1,0:T(8,128)(2,1)S(1)}, bf16[256,1024]{1,0:T(8,128)(2,1)S(1)}, u32[]{:S(2)}, u32[]{:S(2)}) collective-permute-start(bf16[256,1024]{1,0:T(8,128)(2,1)S(1)} %get-tuple-element.495.z0), channel_id=1, source_target_pairs={{0,1},{1,0},{2,3},{3,2},{4,5},{5,4},{6,7},{7,6},{8,9},{9,8},{10,11... | collective-permute-start | bytes 1572872 | tf_op jit(solution)/shard_map/ppermute | solution.py:857
  263.8 27.9 %collective-permute-start.33 = (bf16[2,2048,256]{2,1,0:T(8,128)(2,1)S(1)}, bf16[2,2048,256]{2,1,0:T(8,128)(2,1)S(1)}, u32[]{:S(2)}, u32[]{:S(2)}) collective-permute-start(bf16[2,2048,256]{2,1,0:T(8,128)(2,1)S(1)} %get-tuple-element.542), channel_id=1, source_target_pairs={{0,1},{1,0},{2,3},{3,2},{4,5},{5,4},{6,7},{7,6},{8,9},{9,8},{10,11... | collective-permute-start | bytes 6291464 | tf_op jit(solution)/shard_map/ppermute | solution.py:857
  264.7 25.0 %collective-permute-start.37 = (bf16[512,512]{1,0:T(8,128)(2,1)S(1)}, bf16[512,512]{1,0:T(8,128)(2,1)S(1)}, u32[]{:S(2)}, u32[]{:S(2)}) collective-permute-start(bf16[512,512]{1,0:T(8,128)(2,1)S(1)} %get-tuple-element.546), channel_id=1, source_target_pairs={{0,8},{4,12},{8,0},{12,4},{16,24},{20,28},{24,16},{28,20},{1,9},{5... | collective-permute-start | bytes 1572872 | tf_op jit(solution)/shard_map/ppermute | solution.py:797
  264.7 25.8 %collective-permute-start.34 = (bf16[128,1024]{1,0:T(8,128)(2,1)S(1)}, bf16[128,1024]{1,0:T(8,128)(2,1)S(1)}, u32[]{:S(2)}, u32[]{:S(2)}) collective-permute-start(bf16[128,1024]{1,0:T(8,128)(2,1)S(1)} %get-tuple-element.554.refs_0_), channel_id=1, source_target_pairs={{0,16},{4,20},{8,24},{12,28},{16,0},{20,4},{24,8},{28,12},{1,17},{... | collective-permute-start | bytes 786440 | tf_op jit(solution)/shard_map/ppermute | solution.py:797
  292.0 24.3 %collective-permute-start.38 = (bf16[2048,256]{1,0:T(8,128)(2,1)S(1)}, bf16[2048,256]{1,0:T(8,128)(2,1)S(1)}, u32[]{:S(2)}, u32[]{:S(2)}) collective-permute-start(bf16[2048,256]{1,0:T(8,128)(2,1)S(1)} %fusion.8), channel_id=1, source_target_pairs={{0,2},{1,3},{2,0},{3,1},{4,6},{5,7},{6,4},{7,5},{8,10},{9,11},{10,... | collective-permute-start | bytes 3145736 | tf_op jit(solution)/shard_map/ppermute | solution.py:860
  317.3 23.5 %collective-permute-start.43 = (bf16[1024,512]{1,0:T(8,128)(2,1)}, bf16[1024,512]{1,0:T(8,128)(2,1)}, u32[]{:S(2)}, u32[]{:S(2)}) collective-permute-start(bf16[1024,512]{1,0:T(8,128)(2,1)} %get-tuple-element.583), channel_id=1, source_target_pairs={{0,2},{1,3},{2,0},{3,1},{4,6},{5,7},{6,4},{7,5},{8,10},{9,11},{10,... | collective-permute-start | bytes 3145736 | tf_op jit(solution)/shard_map/ppermute | solution.py:860
  348.7 44.4 %collective-permute-start.57 = (bf16[512,1024]{1,0:T(8,128)(2,1)}, bf16[512,1024]{1,0:T(8,128)(2,1)S(1)}, u32[]{:S(2)}, u32[]{:S(2)}) collective-permute-start(bf16[512,1024]{1,0:T(8,128)(2,1)} %copy-done.14), channel_id=1, source_target_pairs={{0,4},{4,0},{8,12},{12,8},{16,20},{20,16},{24,28},{28,24},{1,5},{5... | collective-permute-start | bytes 3145736 | tf_op jit(solution)/shard_map/ppermute | solution.py:797
  350.0 52.1 %collective-permute-start.60 = (bf16[512,1024]{1,0:T(8,128)(2,1)S(1)}, bf16[512,1024]{1,0:T(8,128)(2,1)S(1)}, u32[]{:S(2)}, u32[]{:S(2)}) collective-permute-start(bf16[512,1024]{1,0:T(8,128)(2,1)S(1)} %copy-done.13), channel_id=1, source_target_pairs={{0,8},{4,12},{8,0},{12,4},{16,24},{20,28},{24,16},{28,20},{1,9},{5... | collective-permute-start | bytes 3145736 | tf_op jit(solution)/shard_map/ppermute | solution.py:797
  361.6 23.5 %collective-permute-start.51 = (bf16[256,512]{1,0:T(8,128)(2,1)S(1)}, bf16[256,512]{1,0:T(8,128)(2,1)S(1)}, u32[]{:S(2)}, u32[]{:S(2)}) collective-permute-start(bf16[256,512]{1,0:T(8,128)(2,1)S(1)} %get-tuple-element.642.refs_0_), channel_id=1, source_target_pairs={{0,8},{4,12},{8,0},{12,4},{16,24},{20,28},{24,16},{28,20},{1,9},{5... | collective-permute-start | bytes 786440 | tf_op jit(solution)/shard_map/ppermute | solution.py:797
  361.7 23.4 %collective-permute-start.52 = (bf16[256,512]{1,0:T(8,128)(2,1)S(1)}, bf16[256,512]{1,0:T(8,128)(2,1)S(1)}, u32[]{:S(2)}, u32[]{:S(2)}) collective-permute-start(bf16[256,512]{1,0:T(8,128)(2,1)S(1)} %get-tuple-element.643.refs_1_), channel_id=1, source_target_pairs={{0,4},{4,0},{8,12},{12,8},{16,20},{20,16},{24,28},{28,24},{1,5},{5... | collective-permute-start | bytes 786440 | tf_op jit(solution)/shard_map/ppermute | solution.py:797
  370.6 25.8 %collective-permute-start.56 = (f32[18,128]{1,0:T(8,128)S(1)}, f32[18,128]{1,0:T(8,128)S(1)}, u32[]{:S(2)}, u32[]{:S(2)}) collective-permute-start(f32[18,128]{1,0:T(8,128)S(1)} %maximum_bitcast_fusion), channel_id=1, source_target_pairs={{0,4},{4,0},{8,12},{12,8},{16,20},{20,16},{24,28},{28,24},{1,5},{5... | collective-permute-start | bytes 27656 | tf_op jit(solution)/shard_map/ppermute | solution.py:863
  (114 other events, 873.4 us)
Sparse Core Ops, SparseCore 0:
  21.2 24.0 all-gather.1

commit v3 on v2

--- a/solution.py
+++ b/solution.py
@@ -14,7 +14,7 @@
 F32 = jnp.float32
 BF16 = jnp.bfloat16
 MIB = 1024 * 1024
-COST = 1.0
+COST = 8.0
 GELU_C = 0.7978845608028654
 
 
@@ -30,15 +30,16 @@
     return lax.dot_general(a, b, (((0,), (0,)), ((), ())), preferred_element_type=F32)
 
 
-def call(body, grid, in_specs, out_specs, out_shape, scalars, operands, scratch=(), flops=0, vmem=24, hbm=()):
+def call(body, grid, in_specs, out_specs, out_shape, scalars, operands, scratch=(), flops=0, vmem=24, hbm=False, cost=2e10):
     bytes_moved = sum(o.size * o.dtype.itemsize for o in operands)
     bytes_moved += sum(
         o.size * jnp.dtype(o.dtype).itemsize for o in jax.tree_util.tree_leaves(out_shape)
     )
     operands = [
-        pltpu.with_memory_space_constraint(o, pltpu.HBM) if i in hbm else o
-        for i, o in enumerate(operands)
+        pltpu.with_memory_space_constraint(o, pltpu.HBM) if hbm else o for o in operands
     ]
+    if hbm:
+        out_shape = jax.tree_util.tree_map(lambda o: pltpu.HBM(o.shape, o.dtype), out_shape)
     return pl.pallas_call(
         body,
         grid_spec=pltpu.PrefetchScalarGridSpec(
@@ -54,7 +55,7 @@
             dimension_semantics=("arbitrary",) * len(grid),
         ),
         cost_estimate=pl.CostEstimate(
-            flops=int(flops * COST), bytes_accessed=int(bytes_moved * COST), transcendentals=0
+            flops=int(cost), bytes_accessed=int(bytes_moved), transcendentals=0
         ),
     )(scalars, *operands)
 
@@ -194,6 +195,7 @@
         scalars,
         [*pieces, dy, dy, gains, weight4],
         scratch=[pltpu.VMEM((rows, width), BF16)] * 3,
+        hbm=True,
         flops=2 * rows * n * width * 3 * width + 4 * rows * rows * width,
     )
 
@@ -203,7 +205,7 @@
 
 
 def feed_body(
-    sc, x0, x1, x2, x3, p0, p1, p2, p3, ow, gains, up, down, bias,
+    sc, x0, x1, x2, x3, p0, p1, p2, p3, ow, gains, up, up_c, down, down_c, bias,
     y_cols, y_rows, dy_rows, b_out, dy_out, g_out, du_out, send, keep, bias_grad, y_acc, total,
 ):
     t = sc[0]
@@ -239,16 +241,27 @@
         y_rows[...] = y_acc[mine, :]
         dy_rows[...] = dy_out[mine, :]
 
-    u = dot_nn(b_out[...], up[...]) + bias[...]
-    dh = dot_nt(dy_out[...], down[...])
-    square = u * u
-    half = 0.5 + 0.5 * jnp.tanh(u * (GELU_C + (GELU_C * 0.044715) * square))
-    g_out[...] = (u * half).astype(BF16)
-    inner = u * (2 * GELU_C + (6 * 0.044715 * GELU_C) * square)
-    du = (dh * (half + (half - half * half) * inner)).astype(BF16)
-    du_out[...] = du
-    bias_grad[...] = jnp.sum(du.astype(F32), axis=0, keepdims=True)
-    total[...] += dot_nt(du, up[...])
+    def chunk(up, down):
+        u = dot_nn(b_out[...], up[...]) + bias[...]
+        dh = dot_nt(dy_out[...], down[...])
+        square = u * u
+        half = 0.5 + 0.5 * jnp.tanh(u * (GELU_C + (GELU_C * 0.044715) * square))
+        g_out[...] = (u * half).astype(BF16)
+        inner = u * (2 * GELU_C + (6 * 0.044715 * GELU_C) * square)
+        du = (dh * (half + (half - half * half) * inner)).astype(BF16)
+        du_out[...] = du
+        bias_grad[...] = jnp.sum(du.astype(F32), axis=0, keepdims=True)
+        total[...] += dot_nt(du, up[...])
+
+    steps = pl.num_programs(0)
+
+    @pl.when(i < steps // 2)
+    def _():
+        chunk(up, down)
+
+    @pl.when(i >= steps // 2)
+    def _():
+        chunk(up_c, down_c)
 
     @pl.when(i == pl.num_programs(0) - 1)
     def _():
@@ -257,14 +270,21 @@
             out[...] = total[pl.ds(pl.multiple_of(at * part, part), part), :].astype(BF16)
 
 
-def feed(scalars, xs, pieces, ow, gains, up, down, bias):
+def feed(scalars, xs, pieces, ow, gains, up, up_c, down, down_c, bias):
     rows, width = xs[0].shape
     n = len(xs)
     count = n * width
-    hidden = up.shape[1]
+    step = 512
+    near = up.shape[1] // step
+    hidden = 2 * up.shape[1]
     half = rows // 2
     part = half // 2
-    step = 512
+
+    def own(i):
+        return jnp.minimum(i, near - 1)
+
+    def other(i):
+        return jnp.maximum(i - near, 0)
 
     def mine(i, sc):
         return (jnp.bitwise_and(sc[0], 1), 0)
@@ -282,8 +302,10 @@
         + [full(p.shape) for p in pieces]
         + [full(ow.shape), full(gains.shape)]
         + [
-            pl.BlockSpec((count, step), along),
-            pl.BlockSpec((step, count), lambda i, sc: (i, 0)),
+            pl.BlockSpec((count, step), lambda i, sc: (0, own(i))),
+            pl.BlockSpec((count, step), lambda i, sc: (0, other(i))),
+            pl.BlockSpec((step, count), lambda i, sc: (own(i), 0)),
+            pl.BlockSpec((step, count), lambda i, sc: (other(i), 0)),
             pl.BlockSpec((1, step), along),
         ],
         [
@@ -311,8 +333,9 @@
             shape_of((1, hidden), F32),
         ],
         scalars,
-        [*xs, *pieces, ow, gains, up, down, bias],
+        [*xs, *pieces, ow, gains, up, up_c, down, down_c, bias],
         scratch=[pltpu.VMEM((half, count), F32), pltpu.VMEM((half, count), F32)],
+        hbm=True,
         flops=2 * half * count * (count + 3 * hidden),
         vmem=32,
     )
@@ -422,6 +445,7 @@
         scalars,
         [*dzs, out_w, qkv, qkv, qkv, lse],
         scratch=[pltpu.VMEM((rows, width), F32), pltpu.VMEM((rows, width), F32)],
+        hbm=True,
         flops=2 * rows * count * width + 10 * rows * rows * width,
     )
 
@@ -482,15 +506,19 @@
         [shape_of((2, rows, width), BF16), shape_of((2, rows, width), BF16)],
         scalars,
         [*lefts, right],
+        hbm=True,
         flops=2 * rows * lefts[0].shape[1] * count,
     )
 
 
 def out_body(n_left, sc, *refs):
-    lefts, right, send, keep = refs[:n_left], refs[n_left], refs[-2], refs[-1]
+    lefts, right, right_c, send, keep = refs[:n_left], *refs[n_left:]
     i = pl.program_id(0)
-    rows = lefts[0].shape[0]
-    parts = [dot_nn(left[...], right[...]).astype(BF16) for left in lefts]
+    rows, near = lefts[0].shape[0], right.shape[0]
+    parts = [
+        (dot_nn(left[:, :near], right[...]) + dot_nn(left[:, near:], right_c[...])).astype(BF16)
+        for left in lefts
+    ]
     for step, out in enumerate((send, keep)):
 
         @pl.when(i == step)
@@ -499,7 +527,7 @@
                 out[at * rows : (at + 1) * rows, :] = part
 
 
-def out_product(scalars, lefts, right):
+def out_product(scalars, lefts, right, right_c):
     rows = sum(a.shape[0] for a in lefts)
     hidden, count = right.shape
 
@@ -510,12 +538,14 @@
     return call(
         functools.partial(out_body, len(lefts)),
         (2,),
-        [full(a.shape) for a in lefts] + [pl.BlockSpec((hidden, count // 2), cols)],
+        [full(a.shape) for a in lefts] + [pl.BlockSpec((hidden, count // 2), cols)] * 2,
         [pl.BlockSpec((rows, count // 2), lambda i, sc: (0, 0))] * 2,
         [shape_of((rows, count // 2), BF16)] * 2,
         scalars,
-        [*lefts, right],
-        flops=2 * rows * hidden * count,
+        [*lefts, right, right_c],
+        cost=1e11,
+        hbm=True,
+        flops=4 * rows * hidden * count,
     )
 
 
@@ -544,6 +574,7 @@
         [shape_of((m, count), BF16)] * 2,
         scalars,
         [*lefts, *rights],
+        hbm=True,
         flops=8 * rows * m * count,
         vmem=32,
     )
@@ -575,43 +606,37 @@
     )
 
 
-def attn_grad_body(sc, a0, a1, c0, c1, z0, z1, d0, d1, o0, o1, send1, keep1, send2, keep2):
+def attn_grad_body(sc, a0, a1, z0, z1, d0, d1, o0, o1, send, keep):
     i = pl.program_id(0)
-    width = o0.shape[1]
-    low1 = dot_tn(a0[...], d0[:, : 2 * width]) + dot_tn(a1[...], d1[:, : 2 * width])
-    low2 = dot_tn(c0[...], d0[:, 2 * width :]) + dot_tn(c1[...], d1[:, 2 * width :])
-    low3 = dot_tn(z0[...], o0[...]) + dot_tn(z1[...], o1[...])
-    low1, low2, low3 = low1.astype(BF16), low2.astype(BF16), low3.astype(BF16)
-    for step, (out1, out2) in enumerate(((send1, send2), (keep1, keep2))):
+    wide = d0.shape[1]
+    low1 = (dot_tn(a0[...], d0[...]) + dot_tn(a1[...], d1[...])).astype(BF16)
+    low2 = (dot_tn(z0[...], o0[...]) + dot_tn(z1[...], o1[...])).astype(BF16)
+    for step, out in enumerate((send, keep)):
 
         @pl.when(i == step)
-        def _(out1=out1, out2=out2):
-            out1[...] = low1
-            out2[:, :width] = low2
-            out2[:, width:] = low3
-
-
-def attn_grad(scalars, acts, dzs, grads, mixed, bits):
+        def _(out=out):
+            out[:, :wide] = low1
+            out[:, wide:] = low2
+
+
+def attn_grad(scalars, acts, dzs, grads, mixed, bit):
     rows, m = acts[0].shape
-    width = mixed[0].shape[1]
-
-    def half(bit):
-        def index(i, sc):
-            mine = jnp.bitwise_and(jnp.right_shift(sc[2], bit), 1)
-            return (0, jnp.where(i == 0, 1 - mine, mine))
-
-        return pl.BlockSpec((rows, m // 2), index)
-
-    shape = (m // 2, 2 * width)
+    count = grads[0].shape[1] + mixed[0].shape[1]
+
+    def index(i, sc):
+        mine = jnp.bitwise_and(jnp.right_shift(sc[2], bit), 1)
+        return (0, jnp.where(i == 0, 1 - mine, mine))
+
     return call(
         attn_grad_body,
         (2,),
-        [half(bits[0])] * 2 + [half(bits[1])] * 4 + [full(v.shape) for v in (*grads, *mixed)],
-        [pl.BlockSpec(shape, lambda i, sc: (0, 0))] * 4,
-        [shape_of(shape, BF16)] * 4,
+        [pl.BlockSpec((rows, m // 2), index)] * 4 + [full(v.shape) for v in (*grads, *mixed)],
+        [pl.BlockSpec((m // 2, count), lambda i, sc: (0, 0))] * 2,
+        [shape_of((m // 2, count), BF16)] * 2,
         scalars,
-        [*acts, *acts, *dzs, *grads, *mixed],
-        flops=16 * rows * m * width,
+        [*acts, *dzs, *grads, *mixed],
+        hbm=True,
+        flops=4 * rows * m * count,
         vmem=32,
     )
 
@@ -640,20 +665,18 @@
     )
 
 
-def unpack_body(scale, blocks, sc, f1, s1, f2, s2, d_qkv, d_out):
+def unpack_body(scale, blocks, sc, first, second, d_qkv, d_out):
     i = pl.program_id(0)
-    rows = f1.shape[0] * 2 // blocks
+    n = pl.num_programs(0) - 1
+    rows = first.shape[0] * 2 // blocks
     half = blocks // 2
 
-    def each(first, second, index, put):
+    def each(put):
         for k in range(blocks):
             src = first if k < half else second
             at = (k if k < half else k - half) * rows
-            to = pl.ds(pl.multiple_of(jnp.bitwise_xor(index, k) * rows, rows), rows)
+            to = pl.ds(pl.multiple_of(jnp.bitwise_xor(sc[0], k) * rows, rows), rows)
             put(to, src[at : at + rows, :].astype(F32))
-
-    def plain(to, value):
-        d_qkv[0, to, :] = value
 
     def scaled(to, value):
         d_qkv[0, to, :] = value * jnp.where(i == 0, jnp.float32(scale), jnp.float32(1.0))
@@ -661,88 +684,76 @@
     def turned(to, value):
         d_out[:, to] = jnp.transpose(value)
 
-    @pl.when(i < 2)
-    def _():
-        each(f1, s1, sc[0], scaled)
-
-    @pl.when(i == 2)
-    def _():
-        each(f2, s2, sc[1], plain)
-
-    @pl.when(i == 3)
-    def _():
-        each(f2, s2, sc[1], turned)
-
-
-def unpack(index, first1, second1, first2, second2, blocks, scale):
-    m, count = first1.shape[0] * 2, first1.shape[1]
-    width = count // 2
-    one = pl.BlockSpec((m // 2, width), lambda i, sc: (0, jnp.minimum(i, 1)))
-    two = pl.BlockSpec((m // 2, width), lambda i, sc: (0, jnp.maximum(i - 2, 0)))
+    @pl.when(i < n)
+    def _():
+        each(scaled)
+
+    @pl.when(i == n)
+    def _():
+        each(turned)
+
+
+def unpack(index, first, second, blocks, width, scale):
+    m, count = first.shape[0] * 2, first.shape[1]
+    n = count // width - 1
     return call(
         functools.partial(unpack_body, scale, blocks),
-        (4,),
-        [one, one, two, two],
+        (n + 1,),
+        [pl.BlockSpec((m // 2, width), lambda i, sc: (0, i))] * 2,
         [
-            pl.BlockSpec((1, m, width), lambda i, sc: (jnp.minimum(i, 2), 0, 0)),
+            pl.BlockSpec((1, m, width), lambda i, sc: (jnp.minimum(i, n - 1), 0, 0)),
             pl.BlockSpec((width, m), lambda i, sc: (0, 0)),
         ],
-        [shape_of((3, m, width), F32), shape_of((width, m), F32)],
+        [shape_of((n, m, width), F32), shape_of((width, m), F32)],
         index,
-        [first1, second1, first2, second2],
-    )
-
-
-def halve_body(bits, sc, *refs):
-    n = len(bits)
-    keeps, gots, sends, nexts = refs[:n], refs[n : 2 * n], refs[2 * n : 3 * n], refs[3 * n :]
-    for bit, keep, got, send, nxt in zip(bits, keeps, gots, sends, nexts):
-        half = send.shape[0]
-        mine = jnp.bitwise_and(jnp.right_shift(sc[2], bit), 1)
-        for out, side in ((send, 1 - mine), (nxt, mine)):
-            rows = pl.ds(pl.multiple_of(side * half, half), half)
-            out[...] = (keep[rows, :].astype(F32) + got[rows, :].astype(F32)).astype(BF16)
-
-
-def halve(scalars, keeps, gots, bits):
-    shapes = [shape_of((k.shape[0] // 2, k.shape[1]), BF16) for k in keeps] * 2
-    return call(
-        functools.partial(halve_body, bits),
+        [first, second],
+    )
+
+
+def halve_body(bit, sc, keep, got, send, nxt):
+    half = send.shape[0]
+    mine = jnp.bitwise_and(jnp.right_shift(sc[2], bit), 1)
+    for out, side in ((send, 1 - mine), (nxt, mine)):
+        rows = pl.ds(pl.multiple_of(side * half, half), half)
+        out[...] = (keep[rows, :].astype(F32) + got[rows, :].astype(F32)).astype(BF16)
+
+
+def halve(scalars, keep, got, bit):
+    shape = shape_of((keep.shape[0] // 2, keep.shape[1]), BF16)
+    return call(
+        functools.partial(halve_body, bit),
         (1,),
-        [full(v.shape) for v in (*keeps, *gots)],
-        [pl.BlockSpec(v.shape, lambda i, sc: (0, 0)) for v in shapes],
-        shapes,
+        [full(keep.shape)] * 2,
+        [pl.BlockSpec(shape.shape, lambda i, sc: (0, 0))] * 2,
+        [shape] * 2,
         scalars,
-        [*keeps, *gots],
-    )
-
-
-def join_body(added, sc, *refs):
-    n = len(refs) // 3
-    for a, c, out in zip(refs[:n], refs[n : 2 * n], refs[2 * n :]):
-        rows = a.shape[0]
-        if added:
-            out[...] = (a[...].astype(F32) + c[...].astype(F32)).astype(BF16)
-        else:
-            out[:rows, :] = a[...]
-            out[rows:, :] = c[...]
-
-
-def join(scalars, firsts, seconds, added):
-    times = 1 if added else 2
-    shapes = [shape_of((a.shape[0] * times, a.shape[1]), BF16) for a in firsts]
+        [keep, got],
+    )
+
+
+def join_body(added, sc, a, c, out):
+    rows = a.shape[0]
+    if added:
+        out[...] = (a[...].astype(F32) + c[...].astype(F32)).astype(BF16)
+    else:
+        out[:rows, :] = a[...]
+        out[rows:, :] = c[...]
+
+
+def join(scalars, first, second, added):
+    shape = shape_of((first.shape[0] * (1 if added else 2), first.shape[1]), BF16)
     return call(
         functools.partial(join_body, added),
         (1,),
-        [full(v.shape) for v in (*firsts, *seconds)],
-        [pl.BlockSpec(v.shape, lambda i, sc: (0, 0)) for v in shapes],
-        shapes,
+        [full(first.shape)] * 2,
+        pl.BlockSpec(shape.shape, lambda i, sc: (0, 0)),
+        shape,
         scalars,
-        [*firsts, *seconds],
-    )
-
-
-def prepare_body(half, lens, here, out):
+        [first, second],
+    )
+
+
+def place_of_largest(lens, half):
     count = lens.shape[1]
     start, border, before = jnp.int32(0), jnp.int32(0), jnp.int32(0)
     for i in range(count):
@@ -750,20 +761,40 @@
         start = jnp.where(big, before, start)
         border = jnp.where(big, lens[0, (i + 1) % count], border)
         before = before + lens[0, i]
+    return start, border
+
+
+def turn_body(half, lens, here, x, *outs):
+    start, border = place_of_largest(lens, half)
+    rows = x.shape[0]
+    turned = pltpu.roll(x[...].astype(F32), lax.rem(rows - start, rows), 0).astype(BF16)
+    if len(outs) == 1:
+        outs[0][...] = turned
+        return
+    first, second, out = outs
+    first[...] = turned[:half]
+    second[...] = turned[half:]
     out[0] = here[0]
     out[1] = border
     out[2] = here[1]
     out[3] = start
 
 
-def prepare(lengths, here, half):
+def turn(lengths, here, x, half, split):
     smem = pl.BlockSpec(memory_space=pltpu.SMEM)
+    vmem = pl.BlockSpec(memory_space=pltpu.VMEM)
+    piece = shape_of((half, x.shape[1]), BF16)
+    if split:
+        out_specs, out_shape = [vmem, vmem, smem], [piece, piece, shape_of((4,), jnp.int32)]
+    else:
+        out_specs, out_shape = [vmem], [shape_of(x.shape, BF16)]
     return pl.pallas_call(
-        functools.partial(prepare_body, half),
-        in_specs=[smem, smem],
-        out_specs=smem,
-        out_shape=shape_of((4,), jnp.int32),
-    )(lengths, here)
+        functools.partial(turn_body, half),
+        in_specs=[smem, smem, vmem],
+        out_specs=out_specs,
+        out_shape=out_shape,
+        compiler_params=pltpu.CompilerParams(vmem_limit_bytes=16 * MIB),
+    )(lengths, here, x)
 
 
 class Chain:
@@ -782,62 +813,42 @@
         return out
 
 
-class RowSums:
-    def __init__(self, chain, scalars, r, n_rows, orders, pairs, core_flip=None):
+class RowSum:
+    def __init__(self, chain, scalars, r, n_rows, order, pair, core_flip=None):
         self.chain, self.scalars, self.r, self.n_rows = chain, scalars, r, n_rows
-        self.orders = orders
-        self.depth = len(orders[0])
-        self.rest = [b for b in range(n_rows.bit_length() - 1) if b not in orders[0]]
-        self.keeps = [keep for _, keep in pairs]
-        sends = [send for send, _ in pairs]
+        self.order, self.depth = order, len(order)
+        self.rest = [b for b in range(n_rows.bit_length() - 1) if b not in order]
+        send, self.keep = pair
         self.at = 0 if core_flip is None else -1
-        self.gots = self.flips(sends) if core_flip is None else [core_flip(v) for v in sends]
+        self.got = self.flip(send, order[0]) if core_flip is None else core_flip(send)
 
     def flip(self, value, bit):
         return lax.ppermute(value, "rows", [(i, i ^ (1 << bit)) for i in range(self.n_rows)])
 
-    def flips(self, values):
-        return [self.flip(v, order[self.at]) for v, order in zip(values, self.orders)]
-
-    def scatter(self):
-        self.at += 1
+    def step(self):
+        do = self.chain.do
         if self.at < self.depth:
-            bits = [order[self.at] for order in self.orders]
-            out = self.chain.do(halve, self.scalars, self.keeps, self.gots, bits)
-            n = len(self.orders)
-            self.keeps = out[n:]
-            self.gots = self.flips(out[:n])
-            return
-        total = self.chain.do(join, self.scalars, self.keeps, self.gots, True)
-        for b in self.rest:
-            total = self.chain.do(join, self.scalars, total, [self.flip(v, b) for v in total], True)
-        self.bufs = total
-        self.at = self.depth - 1
-        self.gots = self.flips(self.bufs)
-
-    def gather(self):
-        self.at -= 1
-        self.bufs = self.chain.do(join, self.scalars, self.bufs, self.gots, False)
-        self.gots = self.flips(self.bufs)
-
-    def index(self, which):
+            self.at += 1
+            if self.at < self.depth:
+                bit = self.order[self.at]
+                send, self.keep = do(halve, self.scalars, self.keep, self.got, bit)
+                self.got = self.flip(send, bit)
+                return
+            self.buf = do(join, self.scalars, self.keep, self.got, True)
+            for b in self.rest:
+                self.buf = do(join, self.scalars, self.buf, self.flip(self.buf, b), True)
+            self.left = self.depth - 1
+        else:
+            self.left -= 1
+            self.buf = do(join, self.scalars, self.buf, self.got, False)
+        self.got = self.flip(self.buf, self.order[self.left])
+
+    def finish(self, fn, *args):
         index = 0
-        for b in self.orders[which]:
+        for b in self.order:
             index = index * 2 + jnp.bitwise_and(jnp.right_shift(self.r, b), 1)
-        return index
-
-    def finish(self, which, width):
-        index = jnp.stack([self.index(which)] * 2).astype(jnp.int32)
-        return self.chain.do(
-            place, index, self.bufs[which], self.gots[which], 1 << self.depth, width
-        )
-
-    def finish_attn(self, scale):
-        index = jnp.stack([self.index(0), self.index(1)]).astype(jnp.int32)
-        return self.chain.do(
-            unpack, index, self.bufs[0], self.gots[0], self.bufs[1], self.gots[1],
-            1 << self.depth, scale,
-        )
+        index = jnp.stack([index, index]).astype(jnp.int32)
+        return self.chain.do(fn, index, self.buf, self.got, 1 << self.depth, *args)
 
 
 def local(
@@ -859,44 +870,40 @@
     def x_flip(v):
         return lax.ppermute(v, "tp", [(i, i ^ 2) for i in range(n_tp)])
 
+    def diag_flip(v):
+        return lax.ppermute(v, "tp", [(i, i ^ 3) for i in range(n_tp)])
+
     def row_flip(v, b):
         return lax.ppermute(v, "rows", [(i, i ^ (1 << b)) for i in range(n_rows)])
-
-    def first_half(v, start):
-        return lax.dynamic_slice_in_dim(v, start, half, 0)
-
-    def second_half(v, start):
-        turned = jnp.concatenate([v[half:], v[:half]], 0)
-        return lax.dynamic_slice_in_dim(turned, start, half, 0)
-
-    def rolled(v, start):
-        return lax.dynamic_slice_in_dim(jnp.concatenate([v, v[:half]], 0), start, tok, 0)
 
     ow = lax.all_gather(out_weight, "tp", axis=0, tiled=True)
     vectors = jnp.concatenate([gain_one, shift_one, gain_two, shift_two, down_bias])
     vec_x = x_flip(vectors)
     vec_c = core_flip(jnp.concatenate([vectors, up_bias]))
-    scalars = prepare(lengths, jnp.stack([t, r]).astype(jnp.int32), half)
+    here = jnp.stack([t, r]).astype(jnp.int32)
+    x0, x1, scalars = do(turn, lengths, here, datapoints, half, True)
     start = scalars[3]
-    x0 = do(first_half, datapoints, start)
     x0_x, x0_c = x_flip(x0), core_flip(x0)
-    x1 = do(second_half, datapoints, start)
-    dy = do(rolled, grad_out, start)
+    d_down_bias = do(lambda v: jnp.sum(v.astype(F32), axis=0), grad_out)
     vec_d = core_flip(tie(vec_x))
-    d_down_bias = do(lambda v: jnp.sum(v.astype(F32), axis=0), grad_out)
     n_vec = vectors.shape[0] // width
 
-    def vector_orders(*pieces):
-        rel = jnp.stack([p[: n_vec * width].reshape(n_vec, width) for p in pieces])
+    def relative_vectors(*pieces):
+        return jnp.stack([p[: n_vec * width].reshape(n_vec, width) for p in pieces])
+
+    def vector_orders(rel, vec_c):
         order = jnp.bitwise_xor(t, jnp.arange(n_tp))
-        return rel, jnp.transpose(rel[order], (1, 0, 2)).reshape(n_vec, count)
-
-    gains_rel, gains = do(vector_orders, vectors, vec_c, vec_x, vec_d)
+        bias = jnp.concatenate([up_bias, vec_c[n_vec * width :]]).reshape(1, -1)
+        return jnp.transpose(rel[order], (1, 0, 2)).reshape(n_vec, count), bias
+
     weight4 = qkv_weight.reshape(3, n_tp, width, width)
-
+    gains_rel = do(relative_vectors, vectors, vec_c, vec_x, vec_d)
     x0_d = core_flip(x0_x)
     x1 = tie(x1, x0_x)
     x1_x, x1_c = x_flip(x1), core_flip(x1)
+    (dy,) = do(turn, lengths, here, grad_out, half, False)
+    wide = tie((up_weight, down_weight), x0_x)
+    up_c, down_c = core_flip(wide[0]), core_flip(wide[1])
     xs = [[x0, x0_c, x0_x, x0_d], None]
     qkv, acts, stats, mixed, lse, pieces = [[None] * 2 for _ in range(6)]
 
@@ -904,57 +911,48 @@
         qkv[h], acts[h], stats[h], mixed[h], lse[h], other, mine = do(
             first_layer, scalars, xs[h], dy, gains_rel, weight4, h
         )
-        diag = lax.ppermute(other, "tp", [(i, i ^ 3) for i in range(n_tp)])
-        pieces[h] = [mine, core_flip(other), x_flip(mine), diag]
+        pieces[h] = [mine, core_flip(other), x_flip(mine), diag_flip(other)]
 
     first(0)
-    up_c, down_c = core_flip(tie(up_weight)), core_flip(tie(down_weight))
-    x1_d = core_flip(tie(x1_x))
+    x1_d = core_flip(tie(x1_x, up_c, down_c))
     xs[1] = [x1, x1_c, x1_x, x1_d]
     first(1)
-
-    def both(up_w, down_w, up_b, up_w_c, down_w_c, vec):
-        up_b_c = vec[n_vec * width :]
-        return (
-            jnp.concatenate([up_w, up_w_c], 1),
-            jnp.concatenate([down_w, down_w_c], 0),
-            jnp.concatenate([up_b, up_b_c]).reshape(1, -1),
-        )
-
-    up2, down2, bias2 = do(both, up_weight, down_weight, up_bias, up_c, down_c, vec_c)
-    weights = [ow, gains, up2, down2, bias2]
+    gains, bias2 = do(vector_orders, gains_rel, vec_c)
+
+    weights = [ow, gains, up_weight, up_c, down_weight, down_c, bias2]
     fed0 = do(feed, scalars, xs[0], pieces[0], *weights)
     db0_x = x_flip(fed0[7])
     fed1 = do(feed, scalars, xs[1], pieces[1], *weights)
     db1_x = x_flip(fed1[7])
     y_cols, b, dyn, g, du = [[fed0[k], fed1[k]] for k in (0, 3, 4, 5, 6)]
+    def row_sum(order, pair, *core):
+        return RowSum(chain, scalars, r, n_rows, order, pair, *core)
+
+    def spread_rows(v):
+        return [v, core_flip(v), x_flip(v), diag_flip(v)]
+
     dz0, sums0 = do(norm_back, scalars, fed0[8], db0_x, fed0[1], fed0[2], gains)
-    dz0_x, dz0_c = x_flip(dz0), core_flip(dz0)
-    down_pair = do(pair_grad, scalars, g, dyn, True)
-    up_pair = do(pair_grad, scalars, b, du, False)
-    sums = RowSums(
-        chain, scalars, r, n_rows, [[0, 1, 2], [1, 0, 2]], [down_pair, up_pair], core_flip
-    )
-    sums.scatter()
-    dz1, sums1 = do(norm_back, scalars, fed1[8], db1_x, fed1[1], fed1[2], gains)
-    dz1_x, dz1_c = x_flip(dz1), core_flip(dz1)
-    dz0_d = core_flip(tie(dz0_x))
-    two_sums = sums0 + sums1
+    dzs0 = spread_rows(dz0)
+    up = row_sum([1, 0, 2], do(pair_grad, scalars, b, du, False), core_flip)
+    down = row_sum([0, 1, 2], do(pair_grad, scalars, g, dyn, True), core_flip)
+    dz1, sums1 = do(
+        norm_back, scalars, fed1[8], tie(db1_x, dzs0), fed1[1], fed1[2], gains
+    )
+    dzs1 = spread_rows(dz1)
     hidden = up_bias.shape[0]
-    bias_grad = do(jnp.add, fed0[9], fed1[9])
-    bias_got = core_flip(bias_grad[:, hidden:])
-
-    grads0, dzn0 = do(
-        attend_back, scalars, [dz0, dz0_c, dz0_x, dz0_d], out_weight, qkv[0], lse[0], False
-    )
-    dz1_d = core_flip(tie(dz1_x))
-    sums.scatter()
-    grads1, dzn1 = do(
-        attend_back, scalars, [dz1, dz1_c, dz1_x, dz1_d], out_weight, qkv[1], lse[1], True
-    )
-    sums.scatter()
-    parts = do(attn_grad, scalars, acts, [dzn0, dzn1], [grads0, grads1], mixed, (0, 1))
-    attn = RowSums(chain, scalars, r, n_rows, [[0, 1, 2], [1, 0, 2]], [parts[:2], parts[2:]])
+    up.step()
+    down.step()
+
+    grads0, dzn0 = do(attend_back, scalars, dzs0, out_weight, qkv[0], lse[0], False)
+    grads1, dzn1 = do(attend_back, scalars, dzs1, out_weight, qkv[1], lse[1], True)
+    up.step()
+    down.step()
+    attn = row_sum(
+        [0, 1, 2],
+        do(attn_grad, scalars, acts, [dzn0, dzn1], [grads0, grads1], mixed, 0),
+    )
+    up.step()
+    down.step()
 
     def middle(keep, got):
         return (keep[1].astype(F32) + got[1].astype(F32)).astype(BF16)
@@ -962,27 +960,35 @@
     def total_of(keep, got, got_x):
         return keep[0].astype(F32) + got[0].astype(F32) + got_x.astype(F32)
 
-    sums.scatter()
     send, keep_a = do(spread, scalars, [grads0, grads1], qkv_weight, n_tp, (q_scale, 1.0, 1.0))
     got_a = core_flip(send)
-    attn.scatter()
-    sums.gather()
+    out_send, out_keep = do(out_product, scalars, g, down_weight, down_c)
     da_x = x_flip(do(middle, keep_a, got_a))
-    out_send, out_keep = do(out_product, scalars, g, down2)
-    attn.scatter()
-    sums.gather()
-    out_x = x_flip(tie(out_send, da_x))
+    attn.step()
+    up.step()
+    down.step()
+    bias_grad = do(jnp.add, fed0[9], fed1[9])
+    attn.step()
     gain_row = gain_one.reshape(1, -1)
 
     def joined(*parts):
         return total_of(*parts).astype(BF16)
 
     da = do(joined, keep_a, got_a, da_x)
+    out_x = x_flip(tie(out_send))
+    up.step()
+    down.step()
     m0, ones0 = do(norm_sums, scalars, da[:half], x0, stats[0], gain_row)
     m1, ones1 = do(norm_sums, scalars, da[half:], x1, stats[1], gain_row)
-    attn.scatter()
-    m = do(lambda *a: jnp.concatenate(a, 0), two_sums, m0, m1)
+    attn.step()
+    m = do(lambda a, b, *c: jnp.concatenate([a + b, *c], 0), sums0, sums1, m0, m1)
     m_c = core_flip(m)
+    bias_got = core_flip(bias_grad[:, hidden:])
+    up.step()
+    down.step()
+    m = do(jnp.add, m, m_c)
+    m_x = x_flip(m)
+    attn.step()
     c, side = jnp.bitwise_and(t, 1), jnp.right_shift(t, 1)
 
     def output_rows(keep, got, y0, y1, vecs):
@@ -997,9 +1003,6 @@
 
     rows_send, rows_keep = do(output_rows, out_keep, out_x, *y_cols, gains)
     rows_got = core_flip(rows_send)
-    m = do(jnp.add, m, m_c)
-    m_x = x_flip(m)
-    attn.gather()
 
     def unroll(first, second):
         thrice = jnp.concatenate([second, first, second], 0)
@@ -1015,7 +1018,6 @@
             )
         return unroll(*halves)
 
-    output = do(output_of, rows_keep, rows_got)
     m = do(jnp.add, m, m_x)
 
     def small_of(up_b, down_b, m, ones0, ones1):
@@ -1039,15 +1041,18 @@
             halves.append(dz + stat[:, 1:2] * (n - first - nhat * second))
         return unroll(*halves)
 
-    attn.gather()
+    attn.step()
+    small = do(jnp.add, small, small_got)
+    small_got = row_flip(small, bits[1])
     d_input = do(d_input_of, m, da, x0, stats[0], dzn0, x1, stats[1], dzn1)
-    d_down = sums.finish(0, width)
-    for bit in bits[1:]:
+    output = do(output_of, rows_keep, rows_got)
+    d_down = down.finish(place, width)
+    d_up = up.finish(place, width)
+    for bit in bits[2:]:
         small = do(jnp.add, small, small_got)
         small_got = row_flip(small, bit)
-    d_up = sums.finish(1, width)
     small = do(jnp.add, small, small_got).reshape(-1)
-    d_qkv, d_out = attn.finish_attn(q_scale)
+    d_qkv, d_out = attn.finish(unpack, width, q_scale)
     d_down_bias, d_gain_one, d_shift_one, d_gain_two, d_shift_two = small[hidden:].reshape(5, width)
     return (
         output, d_input, d_qkv, d_out, d_up, small[:hidden],

time: 428 us -> 385 us (0.90)
  Pallas kernels: 128 us -> 180 us
  local copies, waits for them, and re-layouts: 64.4 us -> 18.1 us
  waiting for transfers between devices: 132 us -> 99.3 us
  other arithmetic: 22.6 us -> 16.5 us
  between operations: 22.4 us -> 16.6 us
    pallas_call x29 -> x35, Pallas kernels: 127 us -> 175 us  [call(): pl.pallas_call(body, grid_spec=pltpu.PrefetchScalarGridSpec(num_scalar_pr...]
    unnamed x163 -> x127, local copies, waits for them, and re-layouts: 51.3 us -> 12.6 us
    ppermute x24 -> x18, waiting for transfers between devices: 82.2 us -> 43.5 us  [flip(): lax.ppermute(value, 'rows', [(i, i ^ 1 << bit) for i in range(self.n_rows)])]
    ppermute x12, waiting for transfers between devices: 39.7 us -> 48.2 us  [x_flip(): return lax.ppermute(v, 'tp', [(i, i ^ 2) for i in range(n_tp)])]
    ppermute x24 -> x18, starting transfers between devices: 29 us -> 21.7 us  [flip(): lax.ppermute(value, 'rows', [(i, i ^ 1 << bit) for i in range(self.n_rows)])]
    concatenate x4 -> x2, other arithmetic: 5.77 us -> 0.61 us  [the longest x1 0.6 us: vector_orders(): bias = jnp.concatenate([up_bias, vec_c[n_vec * width:]]).reshape(1, -1)]
    ppermute x2 -> x4, waiting for transfers between devices: 0.01 us -> 5.14 us  [diag_flip(): return lax.ppermute(v, 'tp', [(i, i ^ 3) for i in range(n_tp)])]
    ppermute x20 -> x18, waiting for transfers between devices: 5.02 us -> 0.7 us  [core_flip(): return lax.ppermute(v, 'tp', [(i, i ^ 1) for i in range(n_tp)])]
  transfers between devices with their start and end apart: 62 -> 56, of which waited for: 27 -> 17; matrix products, arithmetic and copies ran while one was open for 9% -> 7% of each run, Pallas kernels for 24% -> 45%
where the time goes in v3:
time: 385 us; the launch traced here: 380 us
  Pallas kernels  180 us (47%)
  waiting for transfers between devices  99.3 us (26%)
  starting transfers between devices  50.2 us (13%)
  local copies, waits for them, and re-layouts  18.1 us (5%)
  between operations  16.6 us (4%)
  other arithmetic  16.5 us (4%)
    pallas_call x35, Pallas kernels, call(): pl.pallas_call(body, grid_spec=pltpu.PrefetchScalarGridSpec(num_scalar_pr...  175 us
    ppermute x12, waiting for transfers between devices, x_flip(): return lax.ppermute(v, 'tp', [(i, i ^ 2) for i in range(n_tp)])  48.2 us
    ppermute x18, waiting for transfers between devices, flip(): lax.ppermute(value, 'rows', [(i, i ^ 1 << bit) for i in range(self.n_rows)])  43.5 us
    ppermute x18, starting transfers between devices, flip(): lax.ppermute(value, 'rows', [(i, i ^ 1 << bit) for i in range(self.n_rows)])  21.7 us
    ppermute x12, starting transfers between devices, x_flip(): return lax.ppermute(v, 'tp', [(i, i ^ 2) for i in range(n_tp)])  16 us
    unnamed x127, local copies, waits for them, and re-layouts  12.6 us
    concatenate x2, other arithmetic, unroll(): thrice = jnp.concatenate([second, first, second], 0)  7.83 us
  transfers between devices with their start and end apart: 56, of which 17 were waited for; matrix products, arithmetic and copies ran while one was open for 7% of the time, Pallas kernels for 45%

profile of v3, /device:TPU:0, one launch (start us, length us, event | category | flops | bytes accessed | tf_op | source)
XLA Modules:
  0.0 380.1 jit_solution(17004828440893558084)
XLA Ops:
  20.7 5.8 %collective-permute-done.4 = f32[1280]{0:T(1024)S(1)} collective-permute-done((f32[1280]{0:T(1024)S(1)}, f32[1280]{0:T(1024)S(1)}, u32[]{:S(2)}, u32[]{:S(2)}) %collective-permute-start.4) | collective-permute-done | bytes 5152 | tf_op jit(solution)/shard_map/ppermute | solution.py:871
  34.3 14.9 %shard_map.222 = (bf16[3,1024,256]{2,1,0:T(8,128)(2,1)}, bf16[1024,1024]{1,0:T(8,128)(2,1)}, f32[1024,2]{1,0:T(8,128)}, bf16[1024,256]{1,0:T(8,128)(2,1)}, f32[2...) custom-call(s32[4]{0:T(128)S(1)} %get-tuple-element.606.sc, bf16[1024,256]{1,0:T(8,128)(2,1)} %copy-done.5, ...), custom_call_target="tpu_custom_call" | custom-call | flops 20000000000 | bytes 11046912 | tf_op jit(solution)/shard_map/pallas_call | solution.py:43
  54.6 14.8 %shard_map.223 = (bf16[3,1024,256]{2,1,0:T(8,128)(2,1)}, bf16[1024,1024]{1,0:T(8,128)(2,1)}, f32[1024,2]{1,0:T(8,128)}, bf16[1024,256]{1,0:T(8,128)(2,1)}, f32[2...) custom-call(s32[4]{0:T(128)S(1)} %get-tuple-element.606.sc, bf16[1024,256]{1,0:T(8,128)(2,1)} %copy-done.7, ...), custom_call_target="tpu_custom_call" | custom-call | flops 20000000000 | bytes 11046912 | tf_op jit(solution)/shard_map/pallas_call | solution.py:43
  73.1 6.8 %collective-permute-done.7.p2 = bf16[1024,256]{1,0:T(8,128)(2,1)} collective-permute-done((bf16[1024,256]{1,0:T(8,128)(2,1)}, bf16[1024,256]{1,0:T(8,128)(2,1)}, u32[]{:S(2)}, u32[]{:S(2)}) %collective-permute-start.7) | collective-permute-done | bytes 524320 | tf_op jit(solution)/shard_map/ppermute | solution.py:871
  81.6 18.0 %shard_map.224 = (f32[512,512]{1,0:T(8,128)}, f32[256,1024]{1,0:T(8,128)}, bf16[256,1024]{1,0:T(8,128)(2,1)}, bf16[512,1024]{1,0:T(8,128)(2,1)}, bf16[512,1024]{...) custom-call(s32[4]{0:T(128)S(1)} %get-tuple-element.606.sc, ...), custom_call_target="tpu_custom_call" | custom-call | flops 20000000000 | bytes 24678400 | tf_op jit(solution)/shard_map/pallas_call | solution.py:43
  103.1 18.3 %shard_map.225 = (f32[512,512]{1,0:T(8,128)}, f32[256,1024]{1,0:T(8,128)}, bf16[256,1024]{1,0:T(8,128)(2,1)}, bf16[512,1024]{1,0:T(8,128)(2,1)}, bf16[512,1024]{...) custom-call(s32[4]{0:T(128)S(1)} %get-tuple-element.606.sc, ...), custom_call_target="tpu_custom_call" | custom-call | flops 20000000000 | bytes 24678400 | tf_op jit(solution)/shard_map/pallas_call | solution.py:43
  124.8 9.9 %shard_map.227 = (bf16[1024,1024]{1,0:T(8,128)(2,1)}, bf16[1024,1024]{1,0:T(8,128)(2,1)}) custom-call(s32[4]{0:T(128)S(1)} %get-tuple-element.606.sc, bf16[512,1024]{1,0:T(8,128)(2,1)} %get-tuple-element.422.a0, bf16[512,1024]{1,0:T(8,128)(2,1)} %get-tuple-element.423.a1, bf16[512,2048]{1,0:T(8,128)(2,1)} %get-tuple-element.424.b0, ...), custom_call_target="tpu_custom_call" | custom-call | flops 20000000000 | bytes 10485760 | tf_op jit(solution)/shard_map/pallas_call | solution.py:43
  136.9 10.1 %shard_map.228 = (bf16[1024,1024]{1,0:T(8,128)(2,1)}, bf16[1024,1024]{1,0:T(8,128)(2,1)}) custom-call(s32[4]{0:T(128)S(1)} %get-tuple-element.606.sc, bf16[512,2048]{1,0:T(8,128)(2,1)} %get-tuple-element.516.a0.refs_0_, bf16[512,2048]{1,0:T(8,128)(2,1)} %get-tuple-element.517.a1.refs_1_, bf16[512,1024]{1,0:T(8,128)(2,1)} %get-tuple-element.430.b0, ...), custom_call_target="tpu_custom_call" | custom-call | flops 20000000000 | bytes 10485760 | tf_op jit(solution)/shard_map/pallas_call | solution.py:43
  148.3 11.5 %collective-permute-done.23.p1 = bf16[256,1024]{1,0:T(8,128)(2,1)S(1)} collective-permute-done((bf16[256,1024]{1,0:T(8,128)(2,1)S(1)}, bf16[256,1024]{1,0:T(8,128)(2,1)S(1)}, u32[]{:S(2)}, u32[]{:S(2)}) %collective-permute-start.23) | collective-permute-done | bytes 524320 | tf_op jit(solution)/shard_map/ppermute | solution.py:871
  168.8 13.6 %shard_map.232 = (bf16[1024,768]{1,0:T(8,128)(2,1)}, bf16[1024,1024]{1,0:T(8,128)(2,1)}) custom-call(s32[4]{0:T(128)S(1)} %get-tuple-element.606.sc, bf16[256,1024]{1,0:T(8,128)(2,1)} %copy-done.13, bf16[256,1024]{1,0:T(8,128)(2,1)} %copy-done.46, bf16[256,1024]{1,0:T(8,128)(2,1)} %copy-done.47, bf16[256,1024]{1,0:T(8,128)(2,1)} %copy-done.48, ...), custom_call_target="tpu_custom_call" | custom-call | flops 20000000000 | bytes 11018240 | tf_op jit(solution)/shard_map/pallas_call | solution.py:43
  182.4 4.1 %collective-permute-done.26.z3 = bf16[256,1024]{1,0:T(8,128)(2,1)S(1)} collective-permute-done((bf16[256,1024]{1,0:T(8,128)(2,1)S(1)}, bf16[256,1024]{1,0:T(8,128)(2,1)S(1)}, u32[]{:S(2)}, u32[]{:S(2)}) %collective-permute-start.26) | collective-permute-done | bytes 524320 | tf_op jit(solution)/shard_map/ppermute | solution.py:874
  187.2 13.8 %shard_map.233 = (bf16[1024,768]{1,0:T(8,128)(2,1)}, bf16[1024,1024]{1,0:T(8,128)(2,1)}) custom-call(s32[4]{0:T(128)S(1)} %get-tuple-element.606.sc, bf16[256,1024]{1,0:T(8,128)(2,1)} %copy-done.14, bf16[256,1024]{1,0:T(8,128)(2,1)} %copy-done.54, bf16[256,1024]{1,0:T(8,128)(2,1)} %copy-done.55, bf16[256,1024]{1,0:T(8,128)(2,1)} %copy-done.56, ...), custom_call_target="tpu_custom_call" | custom-call | flops 20000000000 | bytes 11018240 | tf_op jit(solution)/shard_map/pallas_call | solution.py:43
  206.1 10.7 %shard_map.236 = (bf16[512,1024]{1,0:T(8,128)(2,1)}, bf16[512,1024]{1,0:T(8,128)(2,1)}) custom-call(s32[4]{0:T(128)S(1)} %get-tuple-element.606.sc, bf16[1024,1024]{1,0:T(8,128)(2,1)} %get-tuple-element.493.a0, bf16[1024,1024]{1,0:T(8,128)(2,1)} %get-tuple-element.494.a1, bf16[1024,1024]{1,0:T(8,128)(2,1)} %get-tuple-element.616.z0, ...), custom_call_target="tpu_custom_call" | custom-call | flops 20000000000 | bytes 14680064 | tf_op jit(solution)/shard_map/pallas_call | solution.py:43
  222.9 9.1 %shard_map.239 = (bf16[2,2048,256]{2,1,0:T(8,128)(2,1)}, bf16[2,2048,256]{2,1,0:T(8,128)(2,1)}) custom-call(s32[4]{0:T(128)S(1)} %get-tuple-element.606.sc, bf16[1024,768]{1,0:T(8,128)(2,1)} %get-tuple-element.511.d0.refs_0_, bf16[1024,768]{1,0:T(8,128)(2,1)} %get-tuple-element.512.d1.refs_1_, bf16[3,1024,256]{2,1,0:T(8,128)(2,1)} %refs_2_), custom_call_target="tpu_custom_call" | custom-call | flops 20000000000 | bytes 8912896 | tf_op jit(solution)/shard_map/pallas_call | solution.py:43
  232.1 9.7 %shard_map.240 = (bf16[1024,512]{1,0:T(8,128)(2,1)}, bf16[1024,512]{1,0:T(8,128)(2,1)}) custom-call(s32[4]{0:T(128)S(1)} %get-tuple-element.606.sc, bf16[512,2048]{1,0:T(8,128)(2,1)} %get-tuple-element.516.a0.refs_0_, bf16[512,2048]{1,0:T(8,128)(2,1)} %get-tuple-element.517.a1.refs_1_, bf16[1024,1024]{1,0:T(8,128)(2,1)} %refs_2_.1, ...), custom_call_target="tpu_custom_call" | custom-call | flops 99999997952 | bytes 10485760 | tf_op jit(solution)/shard_map/pallas_call | solution.py:43
  257.7 7.1 %collective-permute-done.34.got = bf16[256,1024]{1,0:T(8,128)(2,1)S(1)} collective-permute-done((bf16[256,1024]{1,0:T(8,128)(2,1)S(1)}, bf16[256,1024]{1,0:T(8,128)(2,1)S(1)}, u32[]{:S(2)}, u32[]{:S(2)}) %collective-permute-start.34) | collective-permute-done | bytes 524320 | tf_op jit(solution)/shard_map/ppermute | solution.py:826
  265.5 12.5 %collective-permute-done.32 = bf16[2048,256]{1,0:T(8,128)(2,1)S(1)} collective-permute-done((bf16[2048,256]{1,0:T(8,128)(2,1)S(1)}, bf16[2048,256]{1,0:T(8,128)(2,1)S(1)}, u32[]{:S(2)}, u32[]{:S(2)}) %collective-permute-start.32) | collective-permute-done | bytes 1048608 | tf_op jit(solution)/shard_map/ppermute | solution.py:871
  283.0 3.8 collective-permute-done.39.c
  296.9 11.4 %collective-permute-done.43.c = bf16[256,1024]{1,0:T(8,128)(2,1)S(1)} collective-permute-done((bf16[256,1024]{1,0:T(8,128)(2,1)S(1)}, bf16[256,1024]{1,0:T(8,128)(2,1)S(1)}, u32[]{:S(2)}, u32[]{:S(2)}) %collective-permute-start.43) | collective-permute-done | bytes 524320 | tf_op jit(solution)/shard_map/ppermute | solution.py:826
  311.4 9.3 %collective-permute-done.37 = bf16[1024,512]{1,0:T(8,128)(2,1)S(1)} collective-permute-done((bf16[1024,512]{1,0:T(8,128)(2,1)S(1)}, bf16[1024,512]{1,0:T(8,128)(2,1)S(1)}, u32[]{:S(2)}, u32[]{:S(2)}) %collective-permute-start.37) | collective-permute-done | bytes 1048608 | tf_op jit(solution)/shard_map/ppermute | solution.py:871
  324.3 17.7 %collective-permute-done.49.c = bf16[256,1024]{1,0:T(8,128)(2,1)S(1)} collective-permute-done((bf16[256,1024]{1,0:T(8,128)(2,1)S(1)}, bf16[256,1024]{1,0:T(8,128)(2,1)S(1)}, u32[]{:S(2)}, u32[]{:S(2)}) %collective-permute-start.49) | collective-permute-done | bytes 524320 | tf_op jit(solution)/shard_map/ppermute | solution.py:826
  351.6 4.8 %fusion.6 = bf16[2048,256]{1,0:T(8,128)(2,1)} fusion(s32[]{:T(128)S(6)} %select_n.46, bf16[1024,256]{1,0:T(8,128)(2,1)S(1)} %maximum_select_fusion, bf16[1024,256]{1,0:T(8,128)(2,1)S(1)} %maximum_select_fusion.1), kind=kLoop, calls=%fused_computation.17 | loop fusion | flops 3145728 | bytes 2097156 | tf_op jit(solution)/shard_map/concatenate | solution.py:1008
  362.9 3.7 collective-permute-start.54
  369.4 3.7 shard_map.256
  (303 shorter events, 118.4 us)
Async XLA Ops:
  7.2 72.8 %all-gather.2.cloned.1.call-start = ((), (), s32[]{:S(2)}) async-start(), calls=%async_computation | async-start | bytes 2621440 | tf_op jit(solution)/shard_map/all_gather | solution.py:879
  50.4 29.5 %collective-permute-start.8 = (bf16[1024,256]{1,0:T(8,128)(2,1)}, bf16[1024,256]{1,0:T(8,128)(2,1)S(1)}, u32[]{:S(2)}, u32[]{:S(2)}) collective-permute-start(bf16[1024,256]{1,0:T(8,128)(2,1)} %get-tuple-element.347), channel_id=1, source_target_pairs={{0,3},{1,2},{2,1},{3,0},{4,7},{5,6},{6,5},{7,4},{8,11},{9,10},{10,... | collective-permute-start | bytes 1572872 | tf_op jit(solution)/shard_map/ppermute | solution.py:874
  52.6 27.3 %collective-permute-start.7 = (bf16[1024,256]{1,0:T(8,128)(2,1)}, bf16[1024,256]{1,0:T(8,128)(2,1)}, u32[]{:S(2)}, u32[]{:S(2)}) collective-permute-start(bf16[1024,256]{1,0:T(8,128)(2,1)} %get-tuple-element.370.p0), channel_id=1, source_target_pairs={{0,2},{1,3},{2,0},{3,1},{4,6},{5,7},{6,4},{7,5},{8,10},{9,11},{10,... | collective-permute-start | bytes 1572872 | tf_op jit(solution)/shard_map/ppermute | solution.py:871
  69.5 31.0 %collective-permute-start.14 = (bf16[1024,256]{1,0:T(8,128)(2,1)}, bf16[1024,256]{1,0:T(8,128)(2,1)S(1)}, u32[]{:S(2)}, u32[]{:S(2)}) collective-permute-start(bf16[1024,256]{1,0:T(8,128)(2,1)} %get-tuple-element.383), channel_id=1, source_target_pairs={{0,1},{1,0},{2,3},{3,2},{4,5},{5,4},{6,7},{7,6},{8,9},{9,8},{10,11... | collective-permute-start | bytes 1572872 | tf_op jit(solution)/shard_map/ppermute | solution.py:868
  69.6 32.5 %collective-permute-start.16 = (bf16[1024,256]{1,0:T(8,128)(2,1)}, bf16[1024,256]{1,0:T(8,128)(2,1)S(1)}, u32[]{:S(2)}, u32[]{:S(2)}) collective-permute-start(bf16[1024,256]{1,0:T(8,128)(2,1)} %get-tuple-element.383), channel_id=1, source_target_pairs={{0,3},{1,2},{2,1},{3,0},{4,7},{5,6},{6,5},{7,4},{8,11},{9,10},{10,... | collective-permute-start | bytes 1572872 | tf_op jit(solution)/shard_map/ppermute | solution.py:874
  122.8 24.2 %collective-permute-start.18 = (bf16[256,1024]{1,0:T(8,128)(2,1)S(1)}, bf16[256,1024]{1,0:T(8,128)(2,1)S(1)}, u32[]{:S(2)}, u32[]{:S(2)}) collective-permute-start(bf16[256,1024]{1,0:T(8,128)(2,1)S(1)} %get-tuple-element.456.z0), channel_id=1, source_target_pairs={{0,1},{1,0},{2,3},{3,2},{4,5},{5,4},{6,7},{7,6},{8,9},{9,8},{10,11... | collective-permute-start | bytes 1572872 | tf_op jit(solution)/shard_map/ppermute | solution.py:868
  122.9 24.3 %collective-permute-start.19 = (bf16[256,1024]{1,0:T(8,128)(2,1)S(1)}, bf16[256,1024]{1,0:T(8,128)(2,1)S(1)}, u32[]{:S(2)}, u32[]{:S(2)}) collective-permute-start(bf16[256,1024]{1,0:T(8,128)(2,1)S(1)} %get-tuple-element.456.z0), channel_id=1, source_target_pairs={{0,2},{1,3},{2,0},{3,1},{4,6},{5,7},{6,4},{7,5},{8,10},{9,11},{10,... | collective-permute-start | bytes 1572872 | tf_op jit(solution)/shard_map/ppermute | solution.py:871
  134.8 28.4 %collective-permute-start.22 = (bf16[1024,1024]{1,0:T(8,128)(2,1)}, bf16[1024,1024]{1,0:T(8,128)(2,1)S(1)}, u32[]{:S(2)}, u32[]{:S(2)}) collective-permute-start(bf16[1024,1024]{1,0:T(8,128)(2,1)} %get-tuple-element.426), channel_id=1, source_target_pairs={{0,1},{1,0},{2,3},{3,2},{4,5},{5,4},{6,7},{7,6},{8,9},{9,8},{10,11... | collective-permute-start | bytes 6291464 | tf_op jit(solution)/shard_map/ppermute | solution.py:868
  135.1 24.7 %collective-permute-start.23 = (bf16[256,1024]{1,0:T(8,128)(2,1)S(1)}, bf16[256,1024]{1,0:T(8,128)(2,1)S(1)}, u32[]{:S(2)}, u32[]{:S(2)}) collective-permute-start(bf16[256,1024]{1,0:T(8,128)(2,1)S(1)} %copy-done.51), channel_id=1, source_target_pairs={{0,2},{1,3},{2,0},{3,1},{4,6},{5,7},{6,4},{7,5},{8,10},{9,11},{10,... | collective-permute-start | bytes 1572872 | tf_op jit(solution)/shard_map/ppermute | solution.py:871
  164.3 36.8 %collective-permute-start.28 = (bf16[512,1024]{1,0:T(8,128)(2,1)S(1)}, bf16[512,1024]{1,0:T(8,128)(2,1)S(1)}, u32[]{:S(2)}, u32[]{:S(2)}) collective-permute-start(bf16[512,1024]{1,0:T(8,128)(2,1)S(1)} %get-tuple-element.450), channel_id=1, source_target_pairs={{0,8},{4,12},{8,0},{12,4},{16,24},{20,28},{24,16},{28,20},{1,9},{5... | collective-permute-start | bytes 3145736 | tf_op jit(solution)/shard_map/ppermute | solution.py:826
  167.2 36.5 %collective-permute-start.27 = (bf16[512,1024]{1,0:T(8,128)(2,1)S(1)}, bf16[512,1024]{1,0:T(8,128)(2,1)S(1)}, u32[]{:S(2)}, u32[]{:S(2)}) collective-permute-start(bf16[512,1024]{1,0:T(8,128)(2,1)S(1)} %get-tuple-element.454), channel_id=1, source_target_pairs={{0,4},{4,0},{8,12},{12,8},{16,20},{20,16},{24,28},{28,24},{1,5},{5... | collective-permute-start | bytes 3145736 | tf_op jit(solution)/shard_map/ppermute | solution.py:826
  216.8 25.4 %collective-permute-start.33 = (bf16[512,1024]{1,0:T(8,128)(2,1)}, bf16[512,1024]{1,0:T(8,128)(2,1)}, u32[]{:S(2)}, u32[]{:S(2)}) collective-permute-start(bf16[512,1024]{1,0:T(8,128)(2,1)} %get-tuple-element.501), channel_id=1, source_target_pairs={{0,4},{4,0},{8,12},{12,8},{16,20},{20,16},{24,28},{28,24},{1,5},{5... | collective-permute-start | bytes 3145736 | tf_op jit(solution)/shard_map/ppermute | solution.py:826
  218.6 28.5 %collective-permute-start.36 = (bf16[128,1024]{1,0:T(8,128)(2,1)}, bf16[128,1024]{1,0:T(8,128)(2,1)}, u32[]{:S(2)}, u32[]{:S(2)}) collective-permute-start(bf16[128,1024]{1,0:T(8,128)(2,1)} %get-tuple-element.505), channel_id=1, source_target_pairs={{0,16},{4,20},{8,24},{12,28},{16,0},{20,4},{24,8},{28,12},{1,17},{... | collective-permute-start | bytes 786440 | tf_op jit(solution)/shard_map/ppermute | solution.py:826
  222.6 26.1 %collective-permute-start.35 = (bf16[128,1024]{1,0:T(8,128)(2,1)}, bf16[128,1024]{1,0:T(8,128)(2,1)}, u32[]{:S(2)}, u32[]{:S(2)}) collective-permute-start(bf16[128,1024]{1,0:T(8,128)(2,1)} %get-tuple-element.509), channel_id=1, source_target_pairs={{0,16},{4,20},{8,24},{12,28},{16,0},{20,4},{24,8},{28,12},{1,17},{... | collective-permute-start | bytes 786440 | tf_op jit(solution)/shard_map/ppermute | solution.py:826
  252.5 25.4 %collective-permute-start.32 = (bf16[2048,256]{1,0:T(8,128)(2,1)S(1)}, bf16[2048,256]{1,0:T(8,128)(2,1)S(1)}, u32[]{:S(2)}, u32[]{:S(2)}) collective-permute-start(bf16[2048,256]{1,0:T(8,128)(2,1)S(1)} %fusion.7), channel_id=1, source_target_pairs={{0,2},{1,3},{2,0},{3,1},{4,6},{5,7},{6,4},{7,5},{8,10},{9,11},{10,... | collective-permute-start | bytes 3145736 | tf_op jit(solution)/shard_map/ppermute | solution.py:871
  254.2 27.0 %collective-permute-start.40 = (bf16[128,1024]{1,0:T(8,128)(2,1)S(1)}, bf16[128,1024]{1,0:T(8,128)(2,1)S(1)}, u32[]{:S(2)}, u32[]{:S(2)}) collective-permute-start(bf16[128,1024]{1,0:T(8,128)(2,1)S(1)} %shard_map.242.a), channel_id=1, source_target_pairs={{0,16},{4,20},{8,24},{12,28},{16,0},{20,4},{24,8},{28,12},{1,17},{... | collective-permute-start | bytes 786440 | tf_op jit(solution)/shard_map/ppermute | solution.py:826
  256.3 30.4 %collective-permute-start.39 = (bf16[128,1024]{1,0:T(8,128)(2,1)S(1)}, bf16[128,1024]{1,0:T(8,128)(2,1)S(1)}, u32[]{:S(2)}, u32[]{:S(2)}) collective-permute-start(bf16[128,1024]{1,0:T(8,128)(2,1)S(1)} %shard_map.243.a), channel_id=1, source_target_pairs={{0,16},{4,20},{8,24},{12,28},{16,0},{20,4},{24,8},{28,12},{1,17},{... | collective-permute-start | bytes 786440 | tf_op jit(solution)/shard_map/ppermute | solution.py:826
  265.4 26.1 %collective-permute-start.38 = (bf16[128,1024]{1,0:T(8,128)(2,1)S(1)}, bf16[128,1024]{1,0:T(8,128)(2,1)S(1)}, u32[]{:S(2)}, u32[]{:S(2)}) collective-permute-start(bf16[128,1024]{1,0:T(8,128)(2,1)S(1)} %get-tuple-element.546), channel_id=1, source_target_pairs={{0,16},{4,20},{8,24},{12,28},{16,0},{20,4},{24,8},{28,12},{1,17},{... | collective-permute-start | bytes 786440 | tf_op jit(solution)/shard_map/ppermute | solution.py:826
  294.8 25.9 %collective-permute-start.37 = (bf16[1024,512]{1,0:T(8,128)(2,1)S(1)}, bf16[1024,512]{1,0:T(8,128)(2,1)S(1)}, u32[]{:S(2)}, u32[]{:S(2)}) collective-permute-start(bf16[1024,512]{1,0:T(8,128)(2,1)S(1)} %copy-done.40), channel_id=1, source_target_pairs={{0,2},{1,3},{2,0},{3,1},{4,6},{5,7},{6,4},{7,5},{8,10},{9,11},{10,... | collective-permute-start | bytes 3145736 | tf_op jit(solution)/shard_map/ppermute | solution.py:871
  296.0 63.6 %collective-permute-start.52 = (bf16[512,1024]{1,0:T(8,128)(2,1)S(1)}, bf16[512,1024]{1,0:T(8,128)(2,1)S(1)}, u32[]{:S(2)}, u32[]{:S(2)}) collective-permute-start(bf16[512,1024]{1,0:T(8,128)(2,1)S(1)} %shard_map.250.first), channel_id=1, source_target_pairs={{0,8},{4,12},{8,0},{12,4},{16,24},{20,28},{24,16},{28,20},{1,9},{5... | collective-permute-start | bytes 3145736 | tf_op jit(solution)/shard_map/ppermute | solution.py:826
  309.0 47.5 %collective-permute-start.53 = (bf16[512,1024]{1,0:T(8,128)(2,1)S(1)}, bf16[512,1024]{1,0:T(8,128)(2,1)S(1)}, u32[]{:S(2)}, u32[]{:S(2)}) collective-permute-start(bf16[512,1024]{1,0:T(8,128)(2,1)S(1)} %shard_map.251.first), channel_id=1, source_target_pairs={{0,4},{4,0},{8,12},{12,8},{16,20},{20,16},{24,28},{28,24},{1,5},{5... | collective-permute-start | bytes 3145736 | tf_op jit(solution)/shard_map/ppermute | solution.py:826
  311.3 30.7 %collective-permute-start.49 = (bf16[256,1024]{1,0:T(8,128)(2,1)S(1)}, bf16[256,1024]{1,0:T(8,128)(2,1)S(1)}, u32[]{:S(2)}, u32[]{:S(2)}) collective-permute-start(bf16[256,1024]{1,0:T(8,128)(2,1)S(1)} %shard_map.252.a), channel_id=1, source_target_pairs={{0,8},{4,12},{8,0},{12,4},{16,24},{20,28},{24,16},{28,20},{1,9},{5... | collective-permute-start | bytes 1572872 | tf_op jit(solution)/shard_map/ppermute | solution.py:826
  322.1 28.9 %collective-permute-start.45 = (bf16[1024,256]{1,0:T(8,128)(2,1)S(1)}, bf16[1024,256]{1,0:T(8,128)(2,1)S(1)}, u32[]{:S(2)}, u32[]{:S(2)}) collective-permute-start(bf16[1024,256]{1,0:T(8,128)(2,1)S(1)} %get-tuple-element.642), channel_id=1, source_target_pairs={{0,1},{1,0},{2,3},{3,2},{4,5},{5,4},{6,7},{7,6},{8,9},{9,8},{10,11... | collective-permute-start | bytes 1572872 | tf_op jit(solution)/shard_map/ppermute | solution.py:868
  342.6 26.8 %collective-permute-start.50 = (bf16[512,1024]{1,0:T(8,128)(2,1)S(1)}, bf16[512,1024]{1,0:T(8,128)(2,1)S(1)}, u32[]{:S(2)}, u32[]{:S(2)}) collective-permute-start(bf16[512,1024]{1,0:T(8,128)(2,1)S(1)} %shard_map.253.first), channel_id=1, source_target_pairs={{0,4},{4,0},{8,12},{12,8},{16,20},{20,16},{24,28},{28,24},{1,5},{5... | collective-permute-start | bytes 3145736 | tf_op jit(solution)/shard_map/ppermute | solution.py:826
  (90 other events, 1001.8 us)
Sparse Core Ops, SparseCore 0:
  31.8 29.7 all-gather.1

commit v4 on v3

--- a/solution.py
+++ b/solution.py
@@ -932,18 +932,21 @@
         return [v, core_flip(v), x_flip(v), diag_flip(v)]
 
     dz0, sums0 = do(norm_back, scalars, fed0[8], db0_x, fed0[1], fed0[2], gains)
-    dzs0 = spread_rows(dz0)
+    dz0_x, dz0_c = x_flip(dz0), core_flip(dz0)
     up = row_sum([1, 0, 2], do(pair_grad, scalars, b, du, False), core_flip)
+    db1_x = tie(db1_x, dz0_c)
     down = row_sum([0, 1, 2], do(pair_grad, scalars, g, dyn, True), core_flip)
-    dz1, sums1 = do(
-        norm_back, scalars, fed1[8], tie(db1_x, dzs0), fed1[1], fed1[2], gains
-    )
+    dz0_x = tie(dz0_x)
+    dzs0 = [dz0, dz0_c, dz0_x, core_flip(dz0_x)]
+    dz1, sums1 = do(norm_back, scalars, fed1[8], db1_x, fed1[1], fed1[2], gains)
     dzs1 = spread_rows(dz1)
     hidden = up_bias.shape[0]
     up.step()
     down.step()
 
     grads0, dzn0 = do(attend_back, scalars, dzs0, out_weight, qkv[0], lse[0], False)
+    up.step()
+    down.step()
     grads1, dzn1 = do(attend_back, scalars, dzs1, out_weight, qkv[1], lse[1], True)
     up.step()
     down.step()
@@ -951,17 +954,17 @@
         [0, 1, 2],
         do(attn_grad, scalars, acts, [dzn0, dzn1], [grads0, grads1], mixed, 0),
     )
+
+    def middle(keep, got):
+        return (keep[1].astype(F32) + got[1].astype(F32)).astype(BF16)
+
+    def total_of(keep, got, got_x):
+        return keep[0].astype(F32) + got[0].astype(F32) + got_x.astype(F32)
+
+    send, keep_a = do(spread, scalars, [grads0, grads1], qkv_weight, n_tp, (q_scale, 1.0, 1.0))
+    got_a = core_flip(send)
     up.step()
     down.step()
-
-    def middle(keep, got):
-        return (keep[1].astype(F32) + got[1].astype(F32)).astype(BF16)
-
-    def total_of(keep, got, got_x):
-        return keep[0].astype(F32) + got[0].astype(F32) + got_x.astype(F32)
-
-    send, keep_a = do(spread, scalars, [grads0, grads1], qkv_weight, n_tp, (q_scale, 1.0, 1.0))
-    got_a = core_flip(send)
     out_send, out_keep = do(out_product, scalars, g, down_weight, down_c)
     da_x = x_flip(do(middle, keep_a, got_a))
     attn.step()
@@ -969,6 +972,9 @@
     down.step()
     bias_grad = do(jnp.add, fed0[9], fed1[9])
     attn.step()
+    up.step()
+    down.step()
+    attn.step()
     gain_row = gain_one.reshape(1, -1)
 
     def joined(*parts):
@@ -976,19 +982,14 @@
 
     da = do(joined, keep_a, got_a, da_x)
     out_x = x_flip(tie(out_send))
-    up.step()
-    down.step()
     m0, ones0 = do(norm_sums, scalars, da[:half], x0, stats[0], gain_row)
     m1, ones1 = do(norm_sums, scalars, da[half:], x1, stats[1], gain_row)
-    attn.step()
     m = do(lambda a, b, *c: jnp.concatenate([a + b, *c], 0), sums0, sums1, m0, m1)
     m_c = core_flip(m)
     bias_got = core_flip(bias_grad[:, hidden:])
-    up.step()
-    down.step()
+    attn.step()
     m = do(jnp.add, m, m_c)
     m_x = x_flip(m)
-    attn.step()
     c, side = jnp.bitwise_and(t, 1), jnp.right_shift(t, 1)
 
     def output_rows(keep, got, y0, y1, vecs):

time: 385 us -> 364 us (0.945)
  waiting for transfers between devices: 99.3 us -> 77.5 us
    ppermute x12, waiting for transfers between devices: 48.2 us -> 27 us  [x_flip(): return lax.ppermute(v, 'tp', [(i, i ^ 2) for i in range(n_tp)])]
    ppermute x4 -> x3, waiting for transfers between devices: 5.14 us -> 0.01 us  [diag_flip(): return lax.ppermute(v, 'tp', [(i, i ^ 3) for i in range(n_tp)])]
    unnamed x127 -> x121, local copies, waits for them, and re-layouts: 12.6 us -> 14 us
  transfers between devices with their start and end apart: 56 -> 56, of which waited for: 17 -> 16; matrix products, arithmetic and copies ran while one was open for 7% -> 7% of each run, Pallas kernels for 45% -> 48%
where the time goes in v4:
time: 364 us; the launch traced here: 359 us
  Pallas kernels  179 us (49%)
  waiting for transfers between devices  77.5 us (21%)
  starting transfers between devices  49.5 us (14%)
  local copies, waits for them, and re-layouts  19.5 us (5%)
  other arithmetic  16.8 us (5%)
  between operations  16.5 us (5%)
    pallas_call x35, Pallas kernels, call(): pl.pallas_call(body, grid_spec=pltpu.PrefetchScalarGridSpec(num_scalar_pr...  175 us
    ppermute x18, waiting for transfers between devices, flip(): lax.ppermute(value, 'rows', [(i, i ^ 1 << bit) for i in range(self.n_rows)])  47.1 us
    ppermute x12, waiting for transfers between devices, x_flip(): return lax.ppermute(v, 'tp', [(i, i ^ 2) for i in range(n_tp)])  27 us
    ppermute x18, starting transfers between devices, flip(): lax.ppermute(value, 'rows', [(i, i ^ 1 << bit) for i in range(self.n_rows)])  24.8 us
    unnamed x121, local copies, waits for them, and re-layouts  14 us
    ppermute x12, starting transfers between devices, x_flip(): return lax.ppermute(v, 'tp', [(i, i ^ 2) for i in range(n_tp)])  12.3 us
    concatenate x2, other arithmetic, unroll(): thrice = jnp.concatenate([second, first, second], 0)  7.8 us
  transfers between devices with their start and end apart: 56, of which 16 were waited for; matrix products, arithmetic and copies ran while one was open for 7% of the time, Pallas kernels for 48%

profile of v4, /device:TPU:0, one launch (start us, length us, event | category | flops | bytes accessed | tf_op | source)
XLA Modules:
  0.0 358.9 jit_solution(15767346935413450352)
XLA Ops:
  20.7 5.8 %collective-permute-done.4 = f32[1280]{0:T(1024)S(1)} collective-permute-done((f32[1280]{0:T(1024)S(1)}, f32[1280]{0:T(1024)S(1)}, u32[]{:S(2)}, u32[]{:S(2)}) %collective-permute-start.4) | collective-permute-done | bytes 5152 | tf_op jit(solution)/shard_map/ppermute | solution.py:871
  34.3 14.9 %shard_map.222 = (bf16[3,1024,256]{2,1,0:T(8,128)(2,1)}, bf16[1024,1024]{1,0:T(8,128)(2,1)}, f32[1024,2]{1,0:T(8,128)}, bf16[1024,256]{1,0:T(8,128)(2,1)}, f32[2...) custom-call(s32[4]{0:T(128)S(1)} %get-tuple-element.608.sc, bf16[1024,256]{1,0:T(8,128)(2,1)} %copy-done.5, ...), custom_call_target="tpu_custom_call" | custom-call | flops 20000000000 | bytes 11046912 | tf_op jit(solution)/shard_map/pallas_call | solution.py:43
  54.6 14.9 %shard_map.223 = (bf16[3,1024,256]{2,1,0:T(8,128)(2,1)}, bf16[1024,1024]{1,0:T(8,128)(2,1)}, f32[1024,2]{1,0:T(8,128)}, bf16[1024,256]{1,0:T(8,128)(2,1)}, f32[2...) custom-call(s32[4]{0:T(128)S(1)} %get-tuple-element.608.sc, bf16[1024,256]{1,0:T(8,128)(2,1)} %copy-done.7, ...), custom_call_target="tpu_custom_call" | custom-call | flops 20000000000 | bytes 11046912 | tf_op jit(solution)/shard_map/pallas_call | solution.py:43
  73.2 6.8 %collective-permute-done.7.p2 = bf16[1024,256]{1,0:T(8,128)(2,1)} collective-permute-done((bf16[1024,256]{1,0:T(8,128)(2,1)}, bf16[1024,256]{1,0:T(8,128)(2,1)}, u32[]{:S(2)}, u32[]{:S(2)}) %collective-permute-start.7) | collective-permute-done | bytes 524320 | tf_op jit(solution)/shard_map/ppermute | solution.py:871
  81.6 18.1 %shard_map.224 = (f32[512,512]{1,0:T(8,128)}, f32[256,1024]{1,0:T(8,128)}, bf16[256,1024]{1,0:T(8,128)(2,1)}, bf16[512,1024]{1,0:T(8,128)(2,1)}, bf16[512,1024]{...) custom-call(s32[4]{0:T(128)S(1)} %get-tuple-element.608.sc, ...), custom_call_target="tpu_custom_call" | custom-call | flops 20000000000 | bytes 24678400 | tf_op jit(solution)/shard_map/pallas_call | solution.py:43
  103.1 18.3 %shard_map.225 = (f32[512,512]{1,0:T(8,128)}, f32[256,1024]{1,0:T(8,128)}, bf16[256,1024]{1,0:T(8,128)(2,1)}, bf16[512,1024]{1,0:T(8,128)(2,1)}, bf16[512,1024]{...) custom-call(s32[4]{0:T(128)S(1)} %get-tuple-element.608.sc, ...), custom_call_target="tpu_custom_call" | custom-call | flops 20000000000 | bytes 24678400 | tf_op jit(solution)/shard_map/pallas_call | solution.py:43
  124.8 9.9 %shard_map.227 = (bf16[1024,1024]{1,0:T(8,128)(2,1)}, bf16[1024,1024]{1,0:T(8,128)(2,1)}) custom-call(s32[4]{0:T(128)S(1)} %get-tuple-element.608.sc, bf16[512,1024]{1,0:T(8,128)(2,1)} %get-tuple-element.422.a0, bf16[512,1024]{1,0:T(8,128)(2,1)} %get-tuple-element.423.a1, bf16[512,2048]{1,0:T(8,128)(2,1)} %get-tuple-element.424.b0, ...), custom_call_target="tpu_custom_call" | custom-call | flops 20000000000 | bytes 10485760 | tf_op jit(solution)/shard_map/pallas_call | solution.py:43
  135.5 10.1 %shard_map.228 = (bf16[1024,1024]{1,0:T(8,128)(2,1)}, bf16[1024,1024]{1,0:T(8,128)(2,1)}) custom-call(s32[4]{0:T(128)S(1)} %get-tuple-element.608.sc, bf16[512,2048]{1,0:T(8,128)(2,1)} %get-tuple-element.526.a0.refs_0_, bf16[512,2048]{1,0:T(8,128)(2,1)} %get-tuple-element.527.a1.refs_1_, bf16[512,1024]{1,0:T(8,128)(2,1)} %get-tuple-element.430.b0, ...), custom_call_target="tpu_custom_call" | custom-call | flops 20000000000 | bytes 10485760 | tf_op jit(solution)/shard_map/pallas_call | solution.py:43
  158.3 13.6 %shard_map.232 = (bf16[1024,768]{1,0:T(8,128)(2,1)}, bf16[1024,1024]{1,0:T(8,128)(2,1)}) custom-call(s32[4]{0:T(128)S(1)} %get-tuple-element.608.sc, bf16[256,1024]{1,0:T(8,128)(2,1)} %copy-done.13, bf16[256,1024]{1,0:T(8,128)(2,1)} %copy-done.45, bf16[256,1024]{1,0:T(8,128)(2,1)} %copy-done.43, bf16[256,1024]{1,0:T(8,128)(2,1)} %copy-done.54, ...), custom_call_target="tpu_custom_call" | custom-call | flops 20000000000 | bytes 11018240 | tf_op jit(solution)/shard_map/pallas_call | solution.py:43
  171.9 7.4 %collective-permute-done.23.got = bf16[512,1024]{1,0:T(8,128)(2,1)S(1)} collective-permute-done((bf16[512,1024]{1,0:T(8,128)(2,1)S(1)}, bf16[512,1024]{1,0:T(8,128)(2,1)S(1)}, u32[]{:S(2)}, u32[]{:S(2)}) %collective-permute-start.23) | collective-permute-done | bytes 1048608 | tf_op jit(solution)/shard_map/ppermute | solution.py:826
  185.2 13.8 %shard_map.235 = (bf16[1024,768]{1,0:T(8,128)(2,1)}, bf16[1024,1024]{1,0:T(8,128)(2,1)}) custom-call(s32[4]{0:T(128)S(1)} %get-tuple-element.608.sc, bf16[256,1024]{1,0:T(8,128)(2,1)} %copy-done.14, bf16[256,1024]{1,0:T(8,128)(2,1)} %copy-done.44, bf16[256,1024]{1,0:T(8,128)(2,1)} %copy-done.46, bf16[256,1024]{1,0:T(8,128)(2,1)} %copy-done.47, ...), custom_call_target="tpu_custom_call" | custom-call | flops 20000000000 | bytes 11018240 | tf_op jit(solution)/shard_map/pallas_call | solution.py:43
  203.5 10.7 %shard_map.238 = (bf16[512,1024]{1,0:T(8,128)(2,1)}, bf16[512,1024]{1,0:T(8,128)(2,1)}) custom-call(s32[4]{0:T(128)S(1)} %get-tuple-element.608.sc, bf16[1024,1024]{1,0:T(8,128)(2,1)} %get-tuple-element.505.a0, bf16[1024,1024]{1,0:T(8,128)(2,1)} %get-tuple-element.506.a1, bf16[1024,1024]{1,0:T(8,128)(2,1)} %get-tuple-element.618.z0, ...), custom_call_target="tpu_custom_call" | custom-call | flops 20000000000 | bytes 14680064 | tf_op jit(solution)/shard_map/pallas_call | solution.py:43
  214.9 9.1 %shard_map.239 = (bf16[2,2048,256]{2,1,0:T(8,128)(2,1)}, bf16[2,2048,256]{2,1,0:T(8,128)(2,1)}) custom-call(s32[4]{0:T(128)S(1)} %get-tuple-element.608.sc, bf16[1024,768]{1,0:T(8,128)(2,1)} %get-tuple-element.515.d0.refs_0_, bf16[1024,768]{1,0:T(8,128)(2,1)} %get-tuple-element.516.d1.refs_1_, bf16[3,1024,256]{2,1,0:T(8,128)(2,1)} %refs_2_), custom_call_target="tpu_custom_call" | custom-call | flops 20000000000 | bytes 8912896 | tf_op jit(solution)/shard_map/pallas_call | solution.py:43
  228.3 9.7 %shard_map.242 = (bf16[1024,512]{1,0:T(8,128)(2,1)}, bf16[1024,512]{1,0:T(8,128)(2,1)}) custom-call(s32[4]{0:T(128)S(1)} %get-tuple-element.608.sc, bf16[512,2048]{1,0:T(8,128)(2,1)} %get-tuple-element.526.a0.refs_0_, bf16[512,2048]{1,0:T(8,128)(2,1)} %get-tuple-element.527.a1.refs_1_, bf16[1024,1024]{1,0:T(8,128)(2,1)} %refs_2_.1, ...), custom_call_target="tpu_custom_call" | custom-call | flops 99999997952 | bytes 10485760 | tf_op jit(solution)/shard_map/pallas_call | solution.py:43
  246.6 4.6 %collective-permute-done.37.c = bf16[128,1024]{1,0:T(8,128)(2,1)S(1)} collective-permute-done((bf16[128,1024]{1,0:T(8,128)(2,1)S(1)}, bf16[128,1024]{1,0:T(8,128)(2,1)S(1)}, u32[]{:S(2)}, u32[]{:S(2)}) %collective-permute-start.37) | collective-permute-done | bytes 262176 | tf_op jit(solution)/shard_map/ppermute | solution.py:826
  255.8 6.7 %collective-permute-done.36.got = bf16[256,1024]{1,0:T(8,128)(2,1)S(1)} collective-permute-done((bf16[256,1024]{1,0:T(8,128)(2,1)S(1)}, bf16[256,1024]{1,0:T(8,128)(2,1)S(1)}, u32[]{:S(2)}, u32[]{:S(2)}) %collective-permute-start.36) | collective-permute-done | bytes 524320 | tf_op jit(solution)/shard_map/ppermute | solution.py:826
  264.6 3.7 %collective-permute-done.41.c = bf16[256,1024]{1,0:T(8,128)(2,1)S(1)} collective-permute-done((bf16[256,1024]{1,0:T(8,128)(2,1)S(1)}, bf16[256,1024]{1,0:T(8,128)(2,1)S(1)}, u32[]{:S(2)}, u32[]{:S(2)}) %collective-permute-start.41) | collective-permute-done | bytes 524320 | tf_op jit(solution)/shard_map/ppermute | solution.py:826
  270.3 9.0 %collective-permute-done.40.c = bf16[256,1024]{1,0:T(8,128)(2,1)S(1)} collective-permute-done((bf16[256,1024]{1,0:T(8,128)(2,1)S(1)}, bf16[256,1024]{1,0:T(8,128)(2,1)S(1)}, u32[]{:S(2)}, u32[]{:S(2)}) %collective-permute-start.40) | collective-permute-done | bytes 524320 | tf_op jit(solution)/shard_map/ppermute | solution.py:826
  289.2 11.6 %collective-permute-done.44.c = bf16[128,1024]{1,0:T(8,128)(2,1)S(1)} collective-permute-done((bf16[128,1024]{1,0:T(8,128)(2,1)S(1)}, bf16[128,1024]{1,0:T(8,128)(2,1)S(1)}, u32[]{:S(2)}, u32[]{:S(2)}) %collective-permute-start.44) | collective-permute-done | bytes 262176 | tf_op jit(solution)/shard_map/ppermute | solution.py:826
  301.3 3.7 %collective-permute-start.49 = (bf16[256,1024]{1,0:T(8,128)(2,1)S(1)}, bf16[256,1024]{1,0:T(8,128)(2,1)S(1)}, u32[]{:S(2)}, u32[]{:S(2)}) collective-permute-start(bf16[256,1024]{1,0:T(8,128)(2,1)S(1)} %shard_map.252.a), channel_id=1, source_target_pairs={{0,8},{4,12},{8,0},{12,4},{16,24},{20,28},{24,16},{28,20},{1,9},{5... | collective-permute-start | bytes 1572872 | tf_op jit(solution)/shard_map/ppermute | solution.py:826
  305.7 8.8 %collective-permute-done.42 = bf16[1024,512]{1,0:T(8,128)(2,1)S(1)} collective-permute-done((bf16[1024,512]{1,0:T(8,128)(2,1)S(1)}, bf16[1024,512]{1,0:T(8,128)(2,1)S(1)}, u32[]{:S(2)}, u32[]{:S(2)}) %collective-permute-start.42) | collective-permute-done | bytes 1048608 | tf_op jit(solution)/shard_map/ppermute | solution.py:871
  329.6 4.8 %fusion.6 = bf16[2048,256]{1,0:T(8,128)(2,1)} fusion(s32[]{:T(128)S(6)} %select_n.46, bf16[1024,256]{1,0:T(8,128)(2,1)S(1)} %maximum_select_fusion, bf16[1024,256]{1,0:T(8,128)(2,1)S(1)} %maximum_select_fusion.1), kind=kLoop, calls=%fused_computation.17 | loop fusion | flops 3145728 | bytes 2097156 | tf_op jit(solution)/shard_map/concatenate | solution.py:1009
  337.6 4.7 %shard_map.255 = f32[1024,1024]{1,0:T(8,128)} custom-call(s32[2]{0:T(128)S(1)} %pad_add_fusion.2.sc, bf16[512,1024]{1,0:T(8,128)(2,1)} %shard_map.247.first, bf16[512,1024]{1,0:T(8,128)(2,1)} %collective-permute-done.52.second), custom_call_target="tpu_custom_call" | custom-call | flops 20000000000 | bytes 6291456 | tf_op jit(solution)/shard_map/pallas_call | solution.py:43
  348.2 3.7 %shard_map.256 = (f32[3,1024,256]{2,1,0:T(8,128)}, f32[256,1024]{1,0:T(8,128)}) custom-call(s32[2]{0:T(128)S(1)} %pad_add_fusion.1.sc, bf16[512,1024]{1,0:T(8,128)(2,1)S(1)} %shard_map.253.first, bf16[512,1024]{1,0:T(8,128)(2,1)S(1)} %collective-permute-done.50.second), custom_call_target="tpu_custom_call" | custom-call | flops 20000000000 | bytes 6291456 | tf_op jit(solution)/shard_map/pallas_call | solution.py:43
  (297 shorter events, 118.0 us)
Async XLA Ops:
  7.2 72.8 %all-gather.2.cloned.1.call-start = ((), (), s32[]{:S(2)}) async-start(), calls=%async_computation | async-start | bytes 2621440 | tf_op jit(solution)/shard_map/all_gather | solution.py:879
  50.0 23.2 %collective-permute-start.6 = (bf16[1024,256]{1,0:T(8,128)(2,1)}, bf16[1024,256]{1,0:T(8,128)(2,1)S(1)}, u32[]{:S(2)}, u32[]{:S(2)}) collective-permute-start(bf16[1024,256]{1,0:T(8,128)(2,1)} %get-tuple-element.348), channel_id=1, source_target_pairs={{0,1},{1,0},{2,3},{3,2},{4,5},{5,4},{6,7},{7,6},{8,9},{9,8},{10,11... | collective-permute-start | bytes 1572872 | tf_op jit(solution)/shard_map/ppermute | solution.py:868
  50.4 29.5 %collective-permute-start.8 = (bf16[1024,256]{1,0:T(8,128)(2,1)}, bf16[1024,256]{1,0:T(8,128)(2,1)S(1)}, u32[]{:S(2)}, u32[]{:S(2)}) collective-permute-start(bf16[1024,256]{1,0:T(8,128)(2,1)} %get-tuple-element.348), channel_id=1, source_target_pairs={{0,3},{1,2},{2,1},{3,0},{4,7},{5,6},{6,5},{7,4},{8,11},{9,10},{10,... | collective-permute-start | bytes 1572872 | tf_op jit(solution)/shard_map/ppermute | solution.py:874
  52.6 27.3 %collective-permute-start.7 = (bf16[1024,256]{1,0:T(8,128)(2,1)}, bf16[1024,256]{1,0:T(8,128)(2,1)}, u32[]{:S(2)}, u32[]{:S(2)}) collective-permute-start(bf16[1024,256]{1,0:T(8,128)(2,1)} %get-tuple-element.371.p0), channel_id=1, source_target_pairs={{0,2},{1,3},{2,0},{3,1},{4,6},{5,7},{6,4},{7,5},{8,10},{9,11},{10,... | collective-permute-start | bytes 1572872 | tf_op jit(solution)/shard_map/ppermute | solution.py:871
  69.5 31.0 %collective-permute-start.14 = (bf16[1024,256]{1,0:T(8,128)(2,1)}, bf16[1024,256]{1,0:T(8,128)(2,1)S(1)}, u32[]{:S(2)}, u32[]{:S(2)}) collective-permute-start(bf16[1024,256]{1,0:T(8,128)(2,1)} %get-tuple-element.384), channel_id=1, source_target_pairs={{0,1},{1,0},{2,3},{3,2},{4,5},{5,4},{6,7},{7,6},{8,9},{9,8},{10,11... | collective-permute-start | bytes 1572872 | tf_op jit(solution)/shard_map/ppermute | solution.py:868
  69.7 32.4 %collective-permute-start.16 = (bf16[1024,256]{1,0:T(8,128)(2,1)}, bf16[1024,256]{1,0:T(8,128)(2,1)S(1)}, u32[]{:S(2)}, u32[]{:S(2)}) collective-permute-start(bf16[1024,256]{1,0:T(8,128)(2,1)} %get-tuple-element.384), channel_id=1, source_target_pairs={{0,3},{1,2},{2,1},{3,0},{4,7},{5,6},{6,5},{7,4},{8,11},{9,10},{10,... | collective-permute-start | bytes 1572872 | tf_op jit(solution)/shard_map/ppermute | solution.py:874
  79.9 22.2 %collective-permute-start.15 = (bf16[1024,256]{1,0:T(8,128)(2,1)}, bf16[1024,256]{1,0:T(8,128)(2,1)S(1)}, u32[]{:S(2)}, u32[]{:S(2)}) collective-permute-start(bf16[1024,256]{1,0:T(8,128)(2,1)} %get-tuple-element.391.p0), channel_id=1, source_target_pairs={{0,2},{1,3},{2,0},{3,1},{4,6},{5,7},{6,4},{7,5},{8,10},{9,11},{10,... | collective-permute-start | bytes 1572872 | tf_op jit(solution)/shard_map/ppermute | solution.py:871
  122.9 28.5 %collective-permute-start.24 = (bf16[256,1024]{1,0:T(8,128)(2,1)S(1)}, bf16[256,1024]{1,0:T(8,128)(2,1)S(1)}, u32[]{:S(2)}, u32[]{:S(2)}) collective-permute-start(bf16[256,1024]{1,0:T(8,128)(2,1)S(1)} %get-tuple-element.460.z0), channel_id=1, source_target_pairs={{0,2},{1,3},{2,0},{3,1},{4,6},{5,7},{6,4},{7,5},{8,10},{9,11},{10,... | collective-permute-start | bytes 1572872 | tf_op jit(solution)/shard_map/ppermute | solution.py:871
  150.6 33.5 %collective-permute-start.28 = (bf16[256,1024]{1,0:T(8,128)(2,1)S(1)}, bf16[256,1024]{1,0:T(8,128)(2,1)S(1)}, u32[]{:S(2)}, u32[]{:S(2)}) collective-permute-start(bf16[256,1024]{1,0:T(8,128)(2,1)S(1)} %get-tuple-element.480.z0), channel_id=1, source_target_pairs={{0,1},{1,0},{2,3},{3,2},{4,5},{5,4},{6,7},{7,6},{8,9},{9,8},{10,11... | collective-permute-start | bytes 1572872 | tf_op jit(solution)/shard_map/ppermute | solution.py:868
  150.7 33.4 %collective-permute-start.29 = (bf16[256,1024]{1,0:T(8,128)(2,1)S(1)}, bf16[256,1024]{1,0:T(8,128)(2,1)S(1)}, u32[]{:S(2)}, u32[]{:S(2)}) collective-permute-start(bf16[256,1024]{1,0:T(8,128)(2,1)S(1)} %get-tuple-element.480.z0), channel_id=1, source_target_pairs={{0,2},{1,3},{2,0},{3,1},{4,6},{5,7},{6,4},{7,5},{8,10},{9,11},{10,... | collective-permute-start | bytes 1572872 | tf_op jit(solution)/shard_map/ppermute | solution.py:871
  151.4 32.7 %collective-permute-start.30 = (bf16[256,1024]{1,0:T(8,128)(2,1)S(1)}, bf16[256,1024]{1,0:T(8,128)(2,1)S(1)}, u32[]{:S(2)}, u32[]{:S(2)}) collective-permute-start(bf16[256,1024]{1,0:T(8,128)(2,1)S(1)} %get-tuple-element.480.z0), channel_id=1, source_target_pairs={{0,3},{1,2},{2,1},{3,0},{4,7},{5,6},{6,5},{7,4},{8,11},{9,10},{10,... | collective-permute-start | bytes 1572872 | tf_op jit(solution)/shard_map/ppermute | solution.py:874
  154.0 25.3 %collective-permute-start.23 = (bf16[512,1024]{1,0:T(8,128)(2,1)S(1)}, bf16[512,1024]{1,0:T(8,128)(2,1)S(1)}, u32[]{:S(2)}, u32[]{:S(2)}) collective-permute-start(bf16[512,1024]{1,0:T(8,128)(2,1)S(1)} %get-tuple-element.450), channel_id=1, source_target_pairs={{0,8},{4,12},{8,0},{12,4},{16,24},{20,28},{24,16},{28,20},{1,9},{5... | collective-permute-start | bytes 3145736 | tf_op jit(solution)/shard_map/ppermute | solution.py:826
  156.7 25.0 %collective-permute-start.22 = (bf16[512,1024]{1,0:T(8,128)(2,1)S(1)}, bf16[512,1024]{1,0:T(8,128)(2,1)S(1)}, u32[]{:S(2)}, u32[]{:S(2)}) collective-permute-start(bf16[512,1024]{1,0:T(8,128)(2,1)S(1)} %get-tuple-element.455), channel_id=1, source_target_pairs={{0,4},{4,0},{8,12},{12,8},{16,20},{20,16},{24,28},{28,24},{1,5},{5... | collective-permute-start | bytes 3145736 | tf_op jit(solution)/shard_map/ppermute | solution.py:826
  199.7 24.3 %collective-permute-start.32 = (bf16[128,1024]{1,0:T(8,128)(2,1)S(1)}, bf16[128,1024]{1,0:T(8,128)(2,1)S(1)}, u32[]{:S(2)}, u32[]{:S(2)}) collective-permute-start(bf16[128,1024]{1,0:T(8,128)(2,1)S(1)} %get-tuple-element.491), channel_id=1, source_target_pairs={{0,16},{4,20},{8,24},{12,28},{16,0},{20,4},{24,8},{28,12},{1,17},{... | collective-permute-start | bytes 786440 | tf_op jit(solution)/shard_map/ppermute | solution.py:826
  203.1 24.2 %collective-permute-start.31 = (bf16[128,1024]{1,0:T(8,128)(2,1)S(1)}, bf16[128,1024]{1,0:T(8,128)(2,1)S(1)}, u32[]{:S(2)}, u32[]{:S(2)}) collective-permute-start(bf16[128,1024]{1,0:T(8,128)(2,1)S(1)} %get-tuple-element.496), channel_id=1, source_target_pairs={{0,16},{4,20},{8,24},{12,28},{16,0},{20,4},{24,8},{28,12},{1,17},{... | collective-permute-start | bytes 786440 | tf_op jit(solution)/shard_map/ppermute | solution.py:826
  214.2 25.2 %collective-permute-start.35 = (bf16[512,1024]{1,0:T(8,128)(2,1)}, bf16[512,1024]{1,0:T(8,128)(2,1)}, u32[]{:S(2)}, u32[]{:S(2)}) collective-permute-start(bf16[512,1024]{1,0:T(8,128)(2,1)} %get-tuple-element.513), channel_id=1, source_target_pairs={{0,4},{4,0},{8,12},{12,8},{16,20},{20,16},{24,28},{28,24},{1,5},{5... | collective-permute-start | bytes 3145736 | tf_op jit(solution)/shard_map/ppermute | solution.py:826
  227.9 23.4 %collective-permute-start.37 = (bf16[128,1024]{1,0:T(8,128)(2,1)S(1)}, bf16[128,1024]{1,0:T(8,128)(2,1)S(1)}, u32[]{:S(2)}, u32[]{:S(2)}) collective-permute-start(bf16[128,1024]{1,0:T(8,128)(2,1)S(1)} %shard_map.241.a), channel_id=1, source_target_pairs={{0,16},{4,20},{8,24},{12,28},{16,0},{20,4},{24,8},{28,12},{1,17},{... | collective-permute-start | bytes 786440 | tf_op jit(solution)/shard_map/ppermute | solution.py:826
  255.2 24.1 %collective-permute-start.40 = (bf16[256,1024]{1,0:T(8,128)(2,1)S(1)}, bf16[256,1024]{1,0:T(8,128)(2,1)S(1)}, u32[]{:S(2)}, u32[]{:S(2)}) collective-permute-start(bf16[256,1024]{1,0:T(8,128)(2,1)S(1)} %shard_map.245.a), channel_id=1, source_target_pairs={{0,8},{4,12},{8,0},{12,4},{16,24},{20,28},{24,16},{28,20},{1,9},{5... | collective-permute-start | bytes 1572872 | tf_op jit(solution)/shard_map/ppermute | solution.py:826
  255.2 27.4 %collective-permute-start.34 = (bf16[2048,256]{1,0:T(8,128)(2,1)}, bf16[2048,256]{1,0:T(8,128)(2,1)S(1)}, u32[]{:S(2)}, u32[]{:S(2)}) collective-permute-start(bf16[2048,256]{1,0:T(8,128)(2,1)} %fusion.7), channel_id=1, source_target_pairs={{0,2},{1,3},{2,0},{3,1},{4,6},{5,7},{6,4},{7,5},{8,10},{9,11},{10,... | collective-permute-start | bytes 3145736 | tf_op jit(solution)/shard_map/ppermute | solution.py:871
  269.9 67.7 %collective-permute-start.52 = (bf16[512,1024]{1,0:T(8,128)(2,1)}, bf16[512,1024]{1,0:T(8,128)(2,1)}, u32[]{:S(2)}, u32[]{:S(2)}) collective-permute-start(bf16[512,1024]{1,0:T(8,128)(2,1)} %shard_map.247.first), channel_id=1, source_target_pairs={{0,8},{4,12},{8,0},{12,4},{16,24},{20,28},{24,16},{28,20},{1,9},{5... | collective-permute-start | bytes 3145736 | tf_op jit(solution)/shard_map/ppermute | solution.py:826
  279.9 54.5 %collective-permute-start.53 = (bf16[512,1024]{1,0:T(8,128)(2,1)S(1)}, bf16[512,1024]{1,0:T(8,128)(2,1)S(1)}, u32[]{:S(2)}, u32[]{:S(2)}) collective-permute-start(bf16[512,1024]{1,0:T(8,128)(2,1)S(1)} %shard_map.248.first), channel_id=1, source_target_pairs={{0,4},{4,0},{8,12},{12,8},{16,20},{20,16},{24,28},{28,24},{1,5},{5... | collective-permute-start | bytes 3145736 | tf_op jit(solution)/shard_map/ppermute | solution.py:826
  288.6 25.9 %collective-permute-start.42 = (bf16[1024,512]{1,0:T(8,128)(2,1)S(1)}, bf16[1024,512]{1,0:T(8,128)(2,1)S(1)}, u32[]{:S(2)}, u32[]{:S(2)}) collective-permute-start(bf16[1024,512]{1,0:T(8,128)(2,1)S(1)} %copy-done.37), channel_id=1, source_target_pairs={{0,2},{1,3},{2,0},{3,1},{4,6},{5,7},{6,4},{7,5},{8,10},{9,11},{10,... | collective-permute-start | bytes 3145736 | tf_op jit(solution)/shard_map/ppermute | solution.py:871
  319.2 29.0 %collective-permute-start.50 = (bf16[512,1024]{1,0:T(8,128)(2,1)S(1)}, bf16[512,1024]{1,0:T(8,128)(2,1)S(1)}, u32[]{:S(2)}, u32[]{:S(2)}) collective-permute-start(bf16[512,1024]{1,0:T(8,128)(2,1)S(1)} %shard_map.253.first), channel_id=1, source_target_pairs={{0,4},{4,0},{8,12},{12,8},{16,20},{20,16},{24,28},{28,24},{1,5},{5... | collective-permute-start | bytes 3145736 | tf_op jit(solution)/shard_map/ppermute | solution.py:826
  320.5 21.9 %collective-permute-start.51 = (f32[18,128]{1,0:T(8,128)S(1)}, f32[18,128]{1,0:T(8,128)S(1)}, u32[]{:S(2)}, u32[]{:S(2)}) collective-permute-start(f32[18,128]{1,0:T(8,128)S(1)} %add.127), channel_id=1, source_target_pairs={{0,8},{4,12},{8,0},{12,4},{16,24},{20,28},{24,16},{28,20},{1,9},{5... | collective-permute-start | bytes 27656 | tf_op jit(solution)/shard_map/ppermute | solution.py:877
  (87 other events, 879.2 us)
Sparse Core Ops, SparseCore 0:
  31.8 29.7 all-gather.1

commit v5 on v4

--- a/solution.py
+++ b/solution.py
@@ -990,6 +990,8 @@
     attn.step()
     m = do(jnp.add, m, m_c)
     m_x = x_flip(m)
+    d_up = up.finish(place, width)
+    d_down = down.finish(place, width)
     c, side = jnp.bitwise_and(t, 1), jnp.right_shift(t, 1)
 
     def output_rows(keep, got, y0, y1, vecs):
@@ -1046,12 +1048,10 @@
     small = do(jnp.add, small, small_got)
     small_got = row_flip(small, bits[1])
     d_input = do(d_input_of, m, da, x0, stats[0], dzn0, x1, stats[1], dzn1)
-    output = do(output_of, rows_keep, rows_got)
-    d_down = down.finish(place, width)
-    d_up = up.finish(place, width)
     for bit in bits[2:]:
         small = do(jnp.add, small, small_got)
         small_got = row_flip(small, bit)
+    output = do(output_of, rows_keep, rows_got)
     small = do(jnp.add, small, small_got).reshape(-1)
     d_qkv, d_out = attn.finish(unpack, width, q_scale)
     d_down_bias, d_gain_one, d_shift_one, d_gain_two, d_shift_two = small[hidden:].reshape(5, width)

time: 364 us -> 360 us (0.989)
    ppermute x18, waiting for transfers between devices: 47.1 us -> 55.6 us  [flip(): lax.ppermute(value, 'rows', [(i, i ^ 1 << bit) for i in range(self.n_rows)])]
    ppermute x12, waiting for transfers between devices: 27 us -> 18.8 us  [x_flip(): return lax.ppermute(v, 'tp', [(i, i ^ 2) for i in range(n_tp)])]
    unnamed x121 -> x123, local copies, waits for them, and re-layouts: 14 us -> 14 us
  transfers between devices with their start and end apart: 56 -> 56, of which waited for: 16 -> 17; matrix products, arithmetic and copies ran while one was open for 7% -> 7% of each run, Pallas kernels for 48% -> 48%
where the time goes in v5:
time: 360 us; the launch traced here: 355 us
  Pallas kernels  176 us (49%)
  waiting for transfers between devices  75.2 us (21%)
  starting transfers between devices  49.9 us (14%)
  local copies, waits for them, and re-layouts  19.5 us (5%)
  other arithmetic  17.5 us (5%)
  between operations  16.5 us (5%)
    pallas_call x35, Pallas kernels, call(): pl.pallas_call(body, grid_spec=pltpu.PrefetchScalarGridSpec(num_scalar_pr...  172 us
    ppermute x18, waiting for transfers between devices, flip(): lax.ppermute(value, 'rows', [(i, i ^ 1 << bit) for i in range(self.n_rows)])  55.6 us
    ppermute x18, starting transfers between devices, flip(): lax.ppermute(value, 'rows', [(i, i ^ 1 << bit) for i in range(self.n_rows)])  24.9 us
    ppermute x12, waiting for transfers between devices, x_flip(): return lax.ppermute(v, 'tp', [(i, i ^ 2) for i in range(n_tp)])  18.8 us
    unnamed x123, local copies, waits for them, and re-layouts  14 us
    ppermute x12, starting transfers between devices, x_flip(): return lax.ppermute(v, 'tp', [(i, i ^ 2) for i in range(n_tp)])  12.7 us
    concatenate x2, other arithmetic, unroll(): thrice = jnp.concatenate([second, first, second], 0)  7.83 us
  transfers between devices with their start and end apart: 56, of which 17 were waited for; matrix products, arithmetic and copies ran while one was open for 7% of the time, Pallas kernels for 48%

profile of v5, /device:TPU:0, one launch (start us, length us, event | category | flops | bytes accessed | tf_op | source)
XLA Modules:
  0.0 354.8 jit_solution(4595450062489095169)
XLA Ops:
  20.7 5.8 %collective-permute-done.4 = f32[1280]{0:T(1024)S(1)} collective-permute-done((f32[1280]{0:T(1024)S(1)}, f32[1280]{0:T(1024)S(1)}, u32[]{:S(2)}, u32[]{:S(2)}) %collective-permute-start.4) | collective-permute-done | bytes 5152 | tf_op jit(solution)/shard_map/ppermute | solution.py:871
  34.3 14.9 %shard_map.222 = (bf16[3,1024,256]{2,1,0:T(8,128)(2,1)}, bf16[1024,1024]{1,0:T(8,128)(2,1)}, f32[1024,2]{1,0:T(8,128)}, bf16[1024,256]{1,0:T(8,128)(2,1)}, f32[2...) custom-call(s32[4]{0:T(128)S(1)} %get-tuple-element.614.sc, bf16[1024,256]{1,0:T(8,128)(2,1)} %copy-done.5, ...), custom_call_target="tpu_custom_call" | custom-call | flops 20000000000 | bytes 11046912 | tf_op jit(solution)/shard_map/pallas_call | solution.py:43
  54.6 14.9 %shard_map.223 = (bf16[3,1024,256]{2,1,0:T(8,128)(2,1)}, bf16[1024,1024]{1,0:T(8,128)(2,1)}, f32[1024,2]{1,0:T(8,128)}, bf16[1024,256]{1,0:T(8,128)(2,1)}, f32[2...) custom-call(s32[4]{0:T(128)S(1)} %get-tuple-element.614.sc, bf16[1024,256]{1,0:T(8,128)(2,1)} %copy-done.7, ...), custom_call_target="tpu_custom_call" | custom-call | flops 20000000000 | bytes 11046912 | tf_op jit(solution)/shard_map/pallas_call | solution.py:43
  73.2 6.8 %collective-permute-done.7.p2 = bf16[1024,256]{1,0:T(8,128)(2,1)} collective-permute-done((bf16[1024,256]{1,0:T(8,128)(2,1)}, bf16[1024,256]{1,0:T(8,128)(2,1)}, u32[]{:S(2)}, u32[]{:S(2)}) %collective-permute-start.7) | collective-permute-done | bytes 524320 | tf_op jit(solution)/shard_map/ppermute | solution.py:871
  81.6 18.1 %shard_map.224 = (f32[512,512]{1,0:T(8,128)}, f32[256,1024]{1,0:T(8,128)}, bf16[256,1024]{1,0:T(8,128)(2,1)}, bf16[512,1024]{1,0:T(8,128)(2,1)}, bf16[512,1024]{...) custom-call(s32[4]{0:T(128)S(1)} %get-tuple-element.614.sc, ...), custom_call_target="tpu_custom_call" | custom-call | flops 20000000000 | bytes 24678400 | tf_op jit(solution)/shard_map/pallas_call | solution.py:43
  103.1 18.3 %shard_map.225 = (f32[512,512]{1,0:T(8,128)}, f32[256,1024]{1,0:T(8,128)}, bf16[256,1024]{1,0:T(8,128)(2,1)}, bf16[512,1024]{1,0:T(8,128)(2,1)}, bf16[512,1024]{...) custom-call(s32[4]{0:T(128)S(1)} %get-tuple-element.614.sc, ...), custom_call_target="tpu_custom_call" | custom-call | flops 20000000000 | bytes 24678400 | tf_op jit(solution)/shard_map/pallas_call | solution.py:43
  124.8 9.9 %shard_map.227 = (bf16[1024,1024]{1,0:T(8,128)(2,1)}, bf16[1024,1024]{1,0:T(8,128)(2,1)}) custom-call(s32[4]{0:T(128)S(1)} %get-tuple-element.614.sc, bf16[512,1024]{1,0:T(8,128)(2,1)} %get-tuple-element.422.a0, bf16[512,1024]{1,0:T(8,128)(2,1)} %get-tuple-element.423.a1, bf16[512,2048]{1,0:T(8,128)(2,1)} %get-tuple-element.424.b0, ...), custom_call_target="tpu_custom_call" | custom-call | flops 20000000000 | bytes 10485760 | tf_op jit(solution)/shard_map/pallas_call | solution.py:43
  135.5 10.1 %shard_map.228 = (bf16[1024,1024]{1,0:T(8,128)(2,1)}, bf16[1024,1024]{1,0:T(8,128)(2,1)}) custom-call(s32[4]{0:T(128)S(1)} %get-tuple-element.614.sc, bf16[512,2048]{1,0:T(8,128)(2,1)} %get-tuple-element.526.a0.refs_0_, bf16[512,2048]{1,0:T(8,128)(2,1)} %get-tuple-element.527.a1.refs_1_, bf16[512,1024]{1,0:T(8,128)(2,1)} %get-tuple-element.430.b0, ...), custom_call_target="tpu_custom_call" | custom-call | flops 20000000000 | bytes 10485760 | tf_op jit(solution)/shard_map/pallas_call | solution.py:43
  145.7 3.4 collective-permute-done.20.p1
  158.3 13.6 %shard_map.232 = (bf16[1024,768]{1,0:T(8,128)(2,1)}, bf16[1024,1024]{1,0:T(8,128)(2,1)}) custom-call(s32[4]{0:T(128)S(1)} %get-tuple-element.614.sc, bf16[256,1024]{1,0:T(8,128)(2,1)} %copy-done.13, bf16[256,1024]{1,0:T(8,128)(2,1)} %copy-done.46, bf16[256,1024]{1,0:T(8,128)(2,1)} %copy-done.44, bf16[256,1024]{1,0:T(8,128)(2,1)} %copy-done.55, ...), custom_call_target="tpu_custom_call" | custom-call | flops 20000000000 | bytes 11018240 | tf_op jit(solution)/shard_map/pallas_call | solution.py:43
  171.9 7.4 %collective-permute-done.23.got = bf16[512,1024]{1,0:T(8,128)(2,1)S(1)} collective-permute-done((bf16[512,1024]{1,0:T(8,128)(2,1)S(1)}, bf16[512,1024]{1,0:T(8,128)(2,1)S(1)}, u32[]{:S(2)}, u32[]{:S(2)}) %collective-permute-start.23) | collective-permute-done | bytes 1048608 | tf_op jit(solution)/shard_map/ppermute | solution.py:826
  185.2 13.8 %shard_map.235 = (bf16[1024,768]{1,0:T(8,128)(2,1)}, bf16[1024,1024]{1,0:T(8,128)(2,1)}) custom-call(s32[4]{0:T(128)S(1)} %get-tuple-element.614.sc, bf16[256,1024]{1,0:T(8,128)(2,1)} %copy-done.14, bf16[256,1024]{1,0:T(8,128)(2,1)} %copy-done.45, bf16[256,1024]{1,0:T(8,128)(2,1)} %copy-done.47, bf16[256,1024]{1,0:T(8,128)(2,1)} %copy-done.48, ...), custom_call_target="tpu_custom_call" | custom-call | flops 20000000000 | bytes 11018240 | tf_op jit(solution)/shard_map/pallas_call | solution.py:43
  203.5 10.5 %shard_map.238 = (bf16[512,1024]{1,0:T(8,128)(2,1)}, bf16[512,1024]{1,0:T(8,128)(2,1)}) custom-call(s32[4]{0:T(128)S(1)} %get-tuple-element.614.sc, bf16[1024,1024]{1,0:T(8,128)(2,1)} %get-tuple-element.505.a0, bf16[1024,1024]{1,0:T(8,128)(2,1)} %get-tuple-element.506.a1, bf16[1024,1024]{1,0:T(8,128)(2,1)} %get-tuple-element.624.z0, ...), custom_call_target="tpu_custom_call" | custom-call | flops 20000000000 | bytes 14680064 | tf_op jit(solution)/shard_map/pallas_call | solution.py:43
  214.7 9.1 %shard_map.239 = (bf16[2,2048,256]{2,1,0:T(8,128)(2,1)}, bf16[2,2048,256]{2,1,0:T(8,128)(2,1)}) custom-call(s32[4]{0:T(128)S(1)} %get-tuple-element.614.sc, bf16[1024,768]{1,0:T(8,128)(2,1)} %get-tuple-element.515.d0.refs_0_, bf16[1024,768]{1,0:T(8,128)(2,1)} %get-tuple-element.516.d1.refs_1_, bf16[3,1024,256]{2,1,0:T(8,128)(2,1)} %refs_2_), custom_call_target="tpu_custom_call" | custom-call | flops 20000000000 | bytes 8912896 | tf_op jit(solution)/shard_map/pallas_call | solution.py:43
  228.1 9.6 %shard_map.242 = (bf16[1024,512]{1,0:T(8,128)(2,1)}, bf16[1024,512]{1,0:T(8,128)(2,1)}) custom-call(s32[4]{0:T(128)S(1)} %get-tuple-element.614.sc, bf16[512,2048]{1,0:T(8,128)(2,1)} %get-tuple-element.526.a0.refs_0_, bf16[512,2048]{1,0:T(8,128)(2,1)} %get-tuple-element.527.a1.refs_1_, bf16[1024,1024]{1,0:T(8,128)(2,1)} %refs_2_.1, ...), custom_call_target="tpu_custom_call" | custom-call | flops 99999997952 | bytes 10485760 | tf_op jit(solution)/shard_map/pallas_call | solution.py:43
  246.4 4.6 %collective-permute-done.37.c = bf16[128,1024]{1,0:T(8,128)(2,1)S(1)} collective-permute-done((bf16[128,1024]{1,0:T(8,128)(2,1)S(1)}, bf16[128,1024]{1,0:T(8,128)(2,1)S(1)}, u32[]{:S(2)}, u32[]{:S(2)}) %collective-permute-start.37) | collective-permute-done | bytes 262176 | tf_op jit(solution)/shard_map/ppermute | solution.py:826
  256.3 6.0 %collective-permute-done.36.got = bf16[256,1024]{1,0:T(8,128)(2,1)S(1)} collective-permute-done((bf16[256,1024]{1,0:T(8,128)(2,1)S(1)}, bf16[256,1024]{1,0:T(8,128)(2,1)S(1)}, u32[]{:S(2)}, u32[]{:S(2)}) %collective-permute-start.36) | collective-permute-done | bytes 524320 | tf_op jit(solution)/shard_map/ppermute | solution.py:826
  264.4 3.7 %collective-permute-done.41.c = bf16[256,1024]{1,0:T(8,128)(2,1)S(1)} collective-permute-done((bf16[256,1024]{1,0:T(8,128)(2,1)S(1)}, bf16[256,1024]{1,0:T(8,128)(2,1)S(1)}, u32[]{:S(2)}, u32[]{:S(2)}) %collective-permute-start.41) | collective-permute-done | bytes 524320 | tf_op jit(solution)/shard_map/ppermute | solution.py:826
  269.2 9.9 %collective-permute-done.40.c = bf16[256,1024]{1,0:T(8,128)(2,1)S(1)} collective-permute-done((bf16[256,1024]{1,0:T(8,128)(2,1)S(1)}, bf16[256,1024]{1,0:T(8,128)(2,1)S(1)}, u32[]{:S(2)}, u32[]{:S(2)}) %collective-permute-start.40) | collective-permute-done | bytes 524320 | tf_op jit(solution)/shard_map/ppermute | solution.py:826
  289.1 11.5 %collective-permute-done.46.c = bf16[128,1024]{1,0:T(8,128)(2,1)S(1)} collective-permute-done((bf16[128,1024]{1,0:T(8,128)(2,1)S(1)}, bf16[128,1024]{1,0:T(8,128)(2,1)S(1)}, u32[]{:S(2)}, u32[]{:S(2)}) %collective-permute-start.46) | collective-permute-done | bytes 262176 | tf_op jit(solution)/shard_map/ppermute | solution.py:826
  301.2 3.7 %collective-permute-start.51 = (bf16[256,1024]{1,0:T(8,128)(2,1)S(1)}, bf16[256,1024]{1,0:T(8,128)(2,1)S(1)}, u32[]{:S(2)}, u32[]{:S(2)}) collective-permute-start(bf16[256,1024]{1,0:T(8,128)(2,1)S(1)} %shard_map.252.a), channel_id=1, source_target_pairs={{0,8},{4,12},{8,0},{12,4},{16,24},{20,28},{24,16},{28,20},{1,9},{5... | collective-permute-start | bytes 1572872 | tf_op jit(solution)/shard_map/ppermute | solution.py:826
  331.3 4.8 %fusion.6 = bf16[2048,256]{1,0:T(8,128)(2,1)} fusion(s32[]{:T(128)S(6)} %select_n.46, bf16[1024,256]{1,0:T(8,128)(2,1)S(1)} %maximum_select_fusion, bf16[1024,256]{1,0:T(8,128)(2,1)S(1)} %maximum_select_fusion.1), kind=kLoop, calls=%fused_computation.17 | loop fusion | flops 3145728 | bytes 2097156 | tf_op jit(solution)/shard_map/concatenate | solution.py:1011
  337.3 6.9 %collective-permute-done.53.second = bf16[512,1024]{1,0:T(8,128)(2,1)S(1)} collective-permute-done((bf16[512,1024]{1,0:T(8,128)(2,1)S(1)}, bf16[512,1024]{1,0:T(8,128)(2,1)S(1)}, u32[]{:S(2)}, u32[]{:S(2)}) %collective-permute-start.53) | collective-permute-done | bytes 1048608 | tf_op jit(solution)/shard_map/ppermute | solution.py:826
  344.1 3.7 %shard_map.256 = (f32[3,1024,256]{2,1,0:T(8,128)}, f32[256,1024]{1,0:T(8,128)}) custom-call(s32[2]{0:T(128)S(1)} %pad_add_fusion.1.sc, bf16[512,1024]{1,0:T(8,128)(2,1)S(1)} %shard_map.255.first, bf16[512,1024]{1,0:T(8,128)(2,1)S(1)} %collective-permute-done.53.second), custom_call_target="tpu_custom_call" | custom-call | flops 20000000000 | bytes 6291456 | tf_op jit(solution)/shard_map/pallas_call | solution.py:43
  (299 shorter events, 117.2 us)
Async XLA Ops:
  7.2 72.8 %all-gather.2.cloned.1.call-start = ((), (), s32[]{:S(2)}) async-start(), calls=%async_computation | async-start | bytes 2621440 | tf_op jit(solution)/shard_map/all_gather | solution.py:879
  50.0 23.2 %collective-permute-start.6 = (bf16[1024,256]{1,0:T(8,128)(2,1)}, bf16[1024,256]{1,0:T(8,128)(2,1)S(1)}, u32[]{:S(2)}, u32[]{:S(2)}) collective-permute-start(bf16[1024,256]{1,0:T(8,128)(2,1)} %get-tuple-element.348), channel_id=1, source_target_pairs={{0,1},{1,0},{2,3},{3,2},{4,5},{5,4},{6,7},{7,6},{8,9},{9,8},{10,11... | collective-permute-start | bytes 1572872 | tf_op jit(solution)/shard_map/ppermute | solution.py:868
  50.4 29.5 %collective-permute-start.8 = (bf16[1024,256]{1,0:T(8,128)(2,1)}, bf16[1024,256]{1,0:T(8,128)(2,1)S(1)}, u32[]{:S(2)}, u32[]{:S(2)}) collective-permute-start(bf16[1024,256]{1,0:T(8,128)(2,1)} %get-tuple-element.348), channel_id=1, source_target_pairs={{0,3},{1,2},{2,1},{3,0},{4,7},{5,6},{6,5},{7,4},{8,11},{9,10},{10,... | collective-permute-start | bytes 1572872 | tf_op jit(solution)/shard_map/ppermute | solution.py:874
  52.6 27.3 %collective-permute-start.7 = (bf16[1024,256]{1,0:T(8,128)(2,1)}, bf16[1024,256]{1,0:T(8,128)(2,1)}, u32[]{:S(2)}, u32[]{:S(2)}) collective-permute-start(bf16[1024,256]{1,0:T(8,128)(2,1)} %get-tuple-element.371.p0), channel_id=1, source_target_pairs={{0,2},{1,3},{2,0},{3,1},{4,6},{5,7},{6,4},{7,5},{8,10},{9,11},{10,... | collective-permute-start | bytes 1572872 | tf_op jit(solution)/shard_map/ppermute | solution.py:871
  69.5 31.0 %collective-permute-start.14 = (bf16[1024,256]{1,0:T(8,128)(2,1)}, bf16[1024,256]{1,0:T(8,128)(2,1)S(1)}, u32[]{:S(2)}, u32[]{:S(2)}) collective-permute-start(bf16[1024,256]{1,0:T(8,128)(2,1)} %get-tuple-element.384), channel_id=1, source_target_pairs={{0,1},{1,0},{2,3},{3,2},{4,5},{5,4},{6,7},{7,6},{8,9},{9,8},{10,11... | collective-permute-start | bytes 1572872 | tf_op jit(solution)/shard_map/ppermute | solution.py:868
  69.7 32.4 %collective-permute-start.16 = (bf16[1024,256]{1,0:T(8,128)(2,1)}, bf16[1024,256]{1,0:T(8,128)(2,1)S(1)}, u32[]{:S(2)}, u32[]{:S(2)}) collective-permute-start(bf16[1024,256]{1,0:T(8,128)(2,1)} %get-tuple-element.384), channel_id=1, source_target_pairs={{0,3},{1,2},{2,1},{3,0},{4,7},{5,6},{6,5},{7,4},{8,11},{9,10},{10,... | collective-permute-start | bytes 1572872 | tf_op jit(solution)/shard_map/ppermute | solution.py:874
  79.9 22.2 %collective-permute-start.15 = (bf16[1024,256]{1,0:T(8,128)(2,1)}, bf16[1024,256]{1,0:T(8,128)(2,1)S(1)}, u32[]{:S(2)}, u32[]{:S(2)}) collective-permute-start(bf16[1024,256]{1,0:T(8,128)(2,1)} %get-tuple-element.391.p0), channel_id=1, source_target_pairs={{0,2},{1,3},{2,0},{3,1},{4,6},{5,7},{6,4},{7,5},{8,10},{9,11},{10,... | collective-permute-start | bytes 1572872 | tf_op jit(solution)/shard_map/ppermute | solution.py:871
  99.7 21.6 %collective-permute-start.17 = (bf16[256,1024]{1,0:T(8,128)(2,1)}, bf16[256,1024]{1,0:T(8,128)(2,1)S(1)}, u32[]{:S(2)}, u32[]{:S(2)}) collective-permute-start(bf16[256,1024]{1,0:T(8,128)(2,1)} %get-tuple-element.410), channel_id=1, source_target_pairs={{0,2},{1,3},{2,0},{3,1},{4,6},{5,7},{6,4},{7,5},{8,10},{9,11},{10,... | collective-permute-start | bytes 1572872 | tf_op jit(solution)/shard_map/ppermute | solution.py:871
  122.9 28.5 %collective-permute-start.24 = (bf16[256,1024]{1,0:T(8,128)(2,1)S(1)}, bf16[256,1024]{1,0:T(8,128)(2,1)S(1)}, u32[]{:S(2)}, u32[]{:S(2)}) collective-permute-start(bf16[256,1024]{1,0:T(8,128)(2,1)S(1)} %get-tuple-element.460.z0), channel_id=1, source_target_pairs={{0,2},{1,3},{2,0},{3,1},{4,6},{5,7},{6,4},{7,5},{8,10},{9,11},{10,... | collective-permute-start | bytes 1572872 | tf_op jit(solution)/shard_map/ppermute | solution.py:871
  150.6 33.5 %collective-permute-start.28 = (bf16[256,1024]{1,0:T(8,128)(2,1)S(1)}, bf16[256,1024]{1,0:T(8,128)(2,1)S(1)}, u32[]{:S(2)}, u32[]{:S(2)}) collective-permute-start(bf16[256,1024]{1,0:T(8,128)(2,1)S(1)} %get-tuple-element.480.z0), channel_id=1, source_target_pairs={{0,1},{1,0},{2,3},{3,2},{4,5},{5,4},{6,7},{7,6},{8,9},{9,8},{10,11... | collective-permute-start | bytes 1572872 | tf_op jit(solution)/shard_map/ppermute | solution.py:868
  150.7 33.4 %collective-permute-start.29 = (bf16[256,1024]{1,0:T(8,128)(2,1)S(1)}, bf16[256,1024]{1,0:T(8,128)(2,1)S(1)}, u32[]{:S(2)}, u32[]{:S(2)}) collective-permute-start(bf16[256,1024]{1,0:T(8,128)(2,1)S(1)} %get-tuple-element.480.z0), channel_id=1, source_target_pairs={{0,2},{1,3},{2,0},{3,1},{4,6},{5,7},{6,4},{7,5},{8,10},{9,11},{10,... | collective-permute-start | bytes 1572872 | tf_op jit(solution)/shard_map/ppermute | solution.py:871
  151.4 32.7 %collective-permute-start.30 = (bf16[256,1024]{1,0:T(8,128)(2,1)S(1)}, bf16[256,1024]{1,0:T(8,128)(2,1)S(1)}, u32[]{:S(2)}, u32[]{:S(2)}) collective-permute-start(bf16[256,1024]{1,0:T(8,128)(2,1)S(1)} %get-tuple-element.480.z0), channel_id=1, source_target_pairs={{0,3},{1,2},{2,1},{3,0},{4,7},{5,6},{6,5},{7,4},{8,11},{9,10},{10,... | collective-permute-start | bytes 1572872 | tf_op jit(solution)/shard_map/ppermute | solution.py:874
  154.0 25.3 %collective-permute-start.23 = (bf16[512,1024]{1,0:T(8,128)(2,1)S(1)}, bf16[512,1024]{1,0:T(8,128)(2,1)S(1)}, u32[]{:S(2)}, u32[]{:S(2)}) collective-permute-start(bf16[512,1024]{1,0:T(8,128)(2,1)S(1)} %get-tuple-element.450), channel_id=1, source_target_pairs={{0,8},{4,12},{8,0},{12,4},{16,24},{20,28},{24,16},{28,20},{1,9},{5... | collective-permute-start | bytes 3145736 | tf_op jit(solution)/shard_map/ppermute | solution.py:826
  156.7 25.0 %collective-permute-start.22 = (bf16[512,1024]{1,0:T(8,128)(2,1)S(1)}, bf16[512,1024]{1,0:T(8,128)(2,1)S(1)}, u32[]{:S(2)}, u32[]{:S(2)}) collective-permute-start(bf16[512,1024]{1,0:T(8,128)(2,1)S(1)} %get-tuple-element.455), channel_id=1, source_target_pairs={{0,4},{4,0},{8,12},{12,8},{16,20},{20,16},{24,28},{28,24},{1,5},{5... | collective-permute-start | bytes 3145736 | tf_op jit(solution)/shard_map/ppermute | solution.py:826
  199.7 24.1 %collective-permute-start.32 = (bf16[128,1024]{1,0:T(8,128)(2,1)S(1)}, bf16[128,1024]{1,0:T(8,128)(2,1)S(1)}, u32[]{:S(2)}, u32[]{:S(2)}) collective-permute-start(bf16[128,1024]{1,0:T(8,128)(2,1)S(1)} %get-tuple-element.491), channel_id=1, source_target_pairs={{0,16},{4,20},{8,24},{12,28},{16,0},{20,4},{24,8},{28,12},{1,17},{... | collective-permute-start | bytes 786440 | tf_op jit(solution)/shard_map/ppermute | solution.py:826
  203.0 24.0 %collective-permute-start.31 = (bf16[128,1024]{1,0:T(8,128)(2,1)S(1)}, bf16[128,1024]{1,0:T(8,128)(2,1)S(1)}, u32[]{:S(2)}, u32[]{:S(2)}) collective-permute-start(bf16[128,1024]{1,0:T(8,128)(2,1)S(1)} %get-tuple-element.496), channel_id=1, source_target_pairs={{0,16},{4,20},{8,24},{12,28},{16,0},{20,4},{24,8},{28,12},{1,17},{... | collective-permute-start | bytes 786440 | tf_op jit(solution)/shard_map/ppermute | solution.py:826
  214.0 25.1 %collective-permute-start.35 = (bf16[512,1024]{1,0:T(8,128)(2,1)}, bf16[512,1024]{1,0:T(8,128)(2,1)}, u32[]{:S(2)}, u32[]{:S(2)}) collective-permute-start(bf16[512,1024]{1,0:T(8,128)(2,1)} %get-tuple-element.513), channel_id=1, source_target_pairs={{0,4},{4,0},{8,12},{12,8},{16,20},{20,16},{24,28},{28,24},{1,5},{5... | collective-permute-start | bytes 3145736 | tf_op jit(solution)/shard_map/ppermute | solution.py:826
  227.7 23.4 %collective-permute-start.37 = (bf16[128,1024]{1,0:T(8,128)(2,1)S(1)}, bf16[128,1024]{1,0:T(8,128)(2,1)S(1)}, u32[]{:S(2)}, u32[]{:S(2)}) collective-permute-start(bf16[128,1024]{1,0:T(8,128)(2,1)S(1)} %shard_map.241.a), channel_id=1, source_target_pairs={{0,16},{4,20},{8,24},{12,28},{16,0},{20,4},{24,8},{28,12},{1,17},{... | collective-permute-start | bytes 786440 | tf_op jit(solution)/shard_map/ppermute | solution.py:826
  255.0 24.1 %collective-permute-start.40 = (bf16[256,1024]{1,0:T(8,128)(2,1)S(1)}, bf16[256,1024]{1,0:T(8,128)(2,1)S(1)}, u32[]{:S(2)}, u32[]{:S(2)}) collective-permute-start(bf16[256,1024]{1,0:T(8,128)(2,1)S(1)} %shard_map.245.a), channel_id=1, source_target_pairs={{0,8},{4,12},{8,0},{12,4},{16,24},{20,28},{24,16},{28,20},{1,9},{5... | collective-permute-start | bytes 1572872 | tf_op jit(solution)/shard_map/ppermute | solution.py:826
  255.0 27.4 %collective-permute-start.34 = (bf16[2048,256]{1,0:T(8,128)(2,1)}, bf16[2048,256]{1,0:T(8,128)(2,1)S(1)}, u32[]{:S(2)}, u32[]{:S(2)}) collective-permute-start(bf16[2048,256]{1,0:T(8,128)(2,1)} %fusion.7), channel_id=1, source_target_pairs={{0,2},{1,3},{2,0},{3,1},{4,6},{5,7},{6,4},{7,5},{8,10},{9,11},{10,... | collective-permute-start | bytes 3145736 | tf_op jit(solution)/shard_map/ppermute | solution.py:871
  268.7 38.5 %collective-permute-start.44 = (bf16[512,1024]{1,0:T(8,128)(2,1)S(1)}, bf16[512,1024]{1,0:T(8,128)(2,1)S(1)}, u32[]{:S(2)}, u32[]{:S(2)}) collective-permute-start(bf16[512,1024]{1,0:T(8,128)(2,1)S(1)} %shard_map.247.first), channel_id=1, source_target_pairs={{0,8},{4,12},{8,0},{12,4},{16,24},{20,28},{24,16},{28,20},{1,9},{5... | collective-permute-start | bytes 3145736 | tf_op jit(solution)/shard_map/ppermute | solution.py:826
  279.8 30.7 %collective-permute-start.43 = (bf16[512,1024]{1,0:T(8,128)(2,1)S(1)}, bf16[512,1024]{1,0:T(8,128)(2,1)S(1)}, u32[]{:S(2)}, u32[]{:S(2)}) collective-permute-start(bf16[512,1024]{1,0:T(8,128)(2,1)S(1)} %shard_map.248.first), channel_id=1, source_target_pairs={{0,4},{4,0},{8,12},{12,8},{16,20},{20,16},{24,28},{28,24},{1,5},{5... | collective-permute-start | bytes 3145736 | tf_op jit(solution)/shard_map/ppermute | solution.py:826
  288.3 25.9 %collective-permute-start.42 = (bf16[1024,512]{1,0:T(8,128)(2,1)S(1)}, bf16[1024,512]{1,0:T(8,128)(2,1)S(1)}, u32[]{:S(2)}, u32[]{:S(2)}) collective-permute-start(bf16[1024,512]{1,0:T(8,128)(2,1)S(1)} %copy-done.38), channel_id=1, source_target_pairs={{0,2},{1,3},{2,0},{3,1},{4,6},{5,7},{6,4},{7,5},{8,10},{9,11},{10,... | collective-permute-start | bytes 3145736 | tf_op jit(solution)/shard_map/ppermute | solution.py:871
  319.0 25.1 %collective-permute-start.53 = (bf16[512,1024]{1,0:T(8,128)(2,1)S(1)}, bf16[512,1024]{1,0:T(8,128)(2,1)S(1)}, u32[]{:S(2)}, u32[]{:S(2)}) collective-permute-start(bf16[512,1024]{1,0:T(8,128)(2,1)S(1)} %shard_map.255.first), channel_id=1, source_target_pairs={{0,4},{4,0},{8,12},{12,8},{16,20},{20,16},{24,28},{28,24},{1,5},{5... | collective-permute-start | bytes 3145736 | tf_op jit(solution)/shard_map/ppermute | solution.py:826
  (88 other events, 804.4 us)
Sparse Core Ops, SparseCore 0:
  31.8 29.7 all-gather.1
